TPU v7x, 32 devices: a whole 2x2x4 slice. The times are simulated.
32 devices in a mesh: fsdp: 8 (over z, core), ctx: 2 (over x), tp: 2 (over y).
Axes of the slice: x: 2, y: 2, z: 4, core: 2. Of those that a mesh axis runs over, the one named last changes fastest.
Arguments:
- image_tokens: bfloat16 [16, 1152, 1536], P('fsdp', 'ctx'), may hold values from -6 to 6
- text_tokens: bfloat16 [16, 176, 1536], P('fsdp', 'ctx'), may hold values from -6 to 6
- cond_vector: bfloat16 [16, 1536], P(None, 'fsdp'), may hold values from -6 to 6
- image_cotangent: bfloat16 [16, 1152, 1536], P('fsdp', 'ctx'), may hold values from -6 to 6
- text_cotangent: bfloat16 [16, 176, 1536], P('fsdp', 'ctx'), may hold values from -6 to 6
- image_counts: int32 [16, 2], P('fsdp'), may hold values from 1 to 576, 1024 in all within a row
- text_counts: int32 [16, 2], P('fsdp'), may hold values from 1 to 88, 154 in all within a row
- seq_live: int32 [16], replicated, may hold values 0 or 1
- ada_weight: bfloat16 [2, 1536, 9216], P(None, 'fsdp', 'tp'), may hold values from -0.15625 to 0.15625
- ada_bias: bfloat16 [2, 9216], P(None, 'tp'), may hold values from -3 to 3
- qkv_weight: bfloat16 [2, 1536, 3, 1536], P(None, 'fsdp', None, 'tp'), may hold values from -0.15625 to 0.15625
- qv_bias: bfloat16 [2, 2, 1536], P(None, None, 'tp'), may hold values from -3 to 3
- attn_out_weight: bfloat16 [2, 1536, 1536], P(None, 'tp', 'fsdp'), may hold values from -2.5 to 2.5
- attn_out_bias: bfloat16 [2, 1536], replicated, may hold values from -3 to 3
- mlp_up_weight: bfloat16 [2, 1536, 6144], P(None, 'fsdp', 'tp'), may hold values from -0.15625 to 0.15625
- mlp_up_bias: bfloat16 [2, 6144], P(None, 'tp'), may hold values from -3 to 3
- mlp_down_weight: bfloat16 [2, 6144, 1536], P(None, 'tp', 'fsdp'), may hold values from -0.078125 to 0.078125
- mlp_down_bias: bfloat16 [2, 1536], replicated, may hold values from -3 to 3
Outputs:
- image_output: bfloat16 [16, 1152, 1536], P('fsdp', 'ctx')
- text_output: bfloat16 [16, 176, 1536], P('fsdp', 'ctx')
- image_grad: bfloat16 [16, 1152, 1536], P('fsdp', 'ctx')
- text_grad: bfloat16 [16, 176, 1536], P('fsdp', 'ctx')
- cond_grad: float32 [16, 1536], P(None, 'fsdp')
- ada_weight_grad: float32 [2, 1536, 9216], P(None, 'fsdp', 'tp')
- ada_bias_grad: float32 [2, 9216], P(None, 'tp')
- qkv_weight_grad: float32 [2, 1536, 3, 1536], P(None, 'fsdp', None, 'tp')
- qv_bias_grad: float32 [2, 2, 1536], P(None, None, 'tp')
- attn_out_weight_grad: float32 [2, 1536, 1536], P(None, 'tp', 'fsdp')
- attn_out_bias_grad: float32 [2, 1536], replicated
- mlp_up_weight_grad: float32 [2, 1536, 6144], P(None, 'fsdp', 'tp')
- mlp_up_bias_grad: float32 [2, 6144], P(None, 'tp')
- mlp_down_weight_grad: float32 [2, 6144, 1536], P(None, 'tp', 'fsdp')
- mlp_down_bias_grad: float32 [2, 1536], replicated
Inputs may be any that keep to these rules, and one draw needn't show every extreme that they name: `image_counts`: each row sums to 1024. `text_counts`: each row sums to 154.
All inputs are finite; a program needn't handle non-finite values.
Results may differ from a plain program's by a relative error of at most 0.01895.
Values may be sent and summed in bfloat16 or wider, within the bound.
No kernel may reach another device: no remote copies, remote signals or barrier semaphores. Data moves between devices by JAX's collectives and lax.ppermute only.
A program may use at most 640 MiB of HBM per device.

v0:
```python
import jax
import jax.numpy as jnp
from jax import lax
from jax.sharding import PartitionSpec as P

D = 1536
HEAD = 64
MB = 2


def shortened(shard):

    def short(part):
        return part.astype(jnp.bfloat16) if part.dtype == jnp.float32 else part

    return jax.tree.map(short, shard)


def layer_norm(values):
    row_mean = jnp.mean(values, axis=-1, keepdims=True)
    centred = values - row_mean
    return centred * lax.rsqrt(jnp.mean(centred * centred, axis=-1, keepdims=True) + 1e-06)


def modulate(values, shift, scale):
    return layer_norm(values) * (1.0 + scale) + shift


def gelu_tanh(values):
    return jax.nn.gelu(values, approximate=True)


def matmul(left, right):
    return jnp.dot(left, right, preferred_element_type=jnp.float32)


def tensor_sum(parts):
    return jax.tree.map(lambda part: part.astype(jnp.float32), lax.psum(shortened(parts), "tp"))


def inner_weights(qkv_weight, mlp_up_weight):
    return (
        lax.all_gather(qkv_weight, "fsdp", axis=1, tiled=True),
        lax.all_gather(mlp_up_weight, "fsdp", axis=1, tiled=True),
    )


def outer_weights(attn_out_weight, mlp_down_weight):
    return (
        lax.all_gather(attn_out_weight, "fsdp", axis=2, tiled=True),
        lax.all_gather(mlp_down_weight, "fsdp", axis=2, tiled=True),
    )


def key_values(key_rows, value_rows, live_flags):
    return (
        lax.all_gather(key_rows, "ctx", axis=0, tiled=True),
        lax.all_gather(value_rows, "ctx", axis=0, tiled=True),
        lax.all_gather(live_flags, "ctx", axis=0, tiled=True),
    )


def on_device(
    image_tokens,
    text_tokens,
    cond_vector,
    image_cotangent,
    text_cotangent,
    image_counts,
    text_counts,
    seq_live,
    ada_weight,
    ada_bias,
    qkv_weight,
    qv_bias,
    attn_out_weight,
    attn_out_bias,
    mlp_up_weight,
    mlp_up_bias,
    mlp_down_weight,
    mlp_down_bias,
):
    slot_count = image_tokens.shape[0]
    per_batch = slot_count // MB
    seq_count = seq_live.shape[0]
    cap_image = image_tokens.shape[1]
    cap_text = text_tokens.shape[1]
    group_index = lax.axis_index("fsdp")
    ctx_index = lax.axis_index("ctx")
    tp_index = lax.axis_index("tp")
    spans = 6 // lax.axis_size("tp")
    width_local = qkv_weight.shape[3]
    heads_local = width_local // HEAD
    score_scale = HEAD ** (-0.5)
    live_all = seq_live.astype(jnp.float32)
    batch_index = jnp.arange(seq_count, dtype=jnp.int32) % slot_count // per_batch
    marked = (batch_index[:, None] == jnp.arange(MB, dtype=jnp.int32)[None, :]).astype(
        jnp.float32
    ) * live_all[:, None]
    members = jnp.sum(marked, axis=0)
    shares = jnp.sum(live_all) / (MB * jnp.maximum(members, 1.0))
    seq_weights = jnp.sum(marked * shares[None, :], axis=1)
    own_weights = lax.dynamic_slice_in_dim(seq_weights, group_index * slot_count, slot_count)
    own_live = lax.dynamic_slice_in_dim(live_all, group_index * slot_count, slot_count)
    cond_float = cond_vector.astype(jnp.float32)
    activated = jax.nn.silu(cond_float).astype(jnp.bfloat16)
    rows_local = ada_weight.shape[1]
    ada_local = ada_weight.reshape(2, rows_local, spans, D)
    ada_partial = jnp.einsum(
        "sd,tdke->stke", activated, ada_local, preferred_element_type=jnp.float32
    )
    mod_half = lax.psum_scatter(
        ada_partial, "fsdp", scatter_dimension=0, tiled=True
    ) + ada_bias.reshape(1, 2, spans, D)
    modulation = lax.all_gather(mod_half, "tp", axis=2, tiled=True)
    image_mask = (
        jnp.arange(cap_image, dtype=jnp.int32)[None, :]
        < lax.dynamic_slice_in_dim(image_counts, ctx_index, 1, 1)
    ).astype(jnp.float32)
    text_mask = (
        jnp.arange(cap_text, dtype=jnp.int32)[None, :]
        < lax.dynamic_slice_in_dim(text_counts, ctx_index, 1, 1)
    ).astype(jnp.float32)
    image_outputs, text_outputs, image_grads, text_grads, mod_grad_list = ([], [], [], [], [])
    bias_totals = None
    grad_totals = None
    for batch in range(MB):
        qkv_full, up_full = inner_weights(qkv_weight, mlp_up_weight)
        out_full, down_full = outer_weights(attn_out_weight, mlp_down_weight)
        run_slot = batch * per_batch
        run_mod_slot = modulation[run_slot]
        run_inputs = (
            image_tokens[run_slot].astype(jnp.float32),
            text_tokens[run_slot].astype(jnp.float32),
        )
        run_live_parts = (image_mask[run_slot], text_mask[run_slot])
        live_flags = jnp.concatenate(run_live_parts, axis=0).astype(jnp.bfloat16)
        hidden_in = []
        query_parts = []
        key_parts = []
        value_parts = []
        for run_stream in range(2):
            normed = modulate(
                run_inputs[run_stream], run_mod_slot[run_stream, 0], run_mod_slot[run_stream, 1]
            ).astype(jnp.bfloat16)
            hidden_in.append(normed)
            projected = jnp.einsum(
                "rd,dke->rke", normed, qkv_full[run_stream], preferred_element_type=jnp.float32
            )
            query_parts.append((projected[:, 0] + qv_bias[run_stream, 0]).astype(jnp.bfloat16))
            key_parts.append(projected[:, 1].astype(jnp.bfloat16))
            value_parts.append((projected[:, 2] + qv_bias[run_stream, 1]).astype(jnp.bfloat16))
        queries = jnp.concatenate(query_parts, axis=0)
        keys_local = jnp.concatenate(key_parts, axis=0)
        values_local = jnp.concatenate(value_parts, axis=0)
        keys_all, values_all, live_keys = key_values(keys_local, values_local, live_flags)
        run_row_count = queries.shape[0]
        run_key_count = keys_all.shape[0]
        run_query_heads = queries.reshape(run_row_count, heads_local, HEAD)
        key_heads = keys_all.reshape(run_key_count, heads_local, HEAD)
        value_heads = values_all.reshape(run_key_count, heads_local, HEAD)
        scores = (
            jnp.einsum(
                "rhe,khe->hrk", run_query_heads, key_heads, preferred_element_type=jnp.float32
            )
            * score_scale
        )
        scores = jnp.where(live_keys[None, None, :] > 0, scores, -1e30)
        row_top = jnp.max(scores, axis=-1, keepdims=True)
        exponent = jnp.exp(scores - row_top)
        sums = jnp.sum(exponent, axis=-1, keepdims=True)
        probs = exponent / sums
        log_total = row_top + jnp.log(sums)
        attended = jnp.einsum(
            "hrk,khe->rhe",
            probs.astype(jnp.bfloat16),
            value_heads,
            preferred_element_type=jnp.float32,
        )
        attended = attended.reshape(run_row_count, width_local).astype(jnp.bfloat16)
        attended_parts = (attended[:cap_image], attended[cap_image:])
        att_sums = tensor_sum(
            (matmul(attended_parts[0], out_full[0]), matmul(attended_parts[1], out_full[1]))
        )
        att_values = []
        middles = []
        hidden_mid = []
        pre_acts = []
        activs = []
        for run_stream in range(2):
            att_value = att_sums[run_stream] + attn_out_bias[run_stream]
            middle = run_inputs[run_stream] + run_mod_slot[run_stream, 2] * att_value
            normed = modulate(
                middle, run_mod_slot[run_stream, 3], run_mod_slot[run_stream, 4]
            ).astype(jnp.bfloat16)
            pre_act = matmul(normed, up_full[run_stream]) + mlp_up_bias[run_stream]
            att_values.append(att_value)
            middles.append(middle)
            hidden_mid.append(normed)
            pre_acts.append(pre_act)
            activs.append(gelu_tanh(pre_act).astype(jnp.bfloat16))
        down_sums = tensor_sum((matmul(activs[0], down_full[0]), matmul(activs[1], down_full[1])))
        mlp_values = []
        finals = []
        for run_stream in range(2):
            mlp_value = down_sums[run_stream] + mlp_down_bias[run_stream]
            mlp_values.append(mlp_value)
            final = (
                (middles[run_stream] + run_mod_slot[run_stream, 5] * mlp_value)
                * run_live_parts[run_stream][:, None]
                * own_live[run_slot]
            )
            finals.append(final.astype(jnp.bfloat16))
        saved_list = {
            "slot": run_slot,
            "mod_slot": run_mod_slot,
            "inputs": run_inputs,
            "live_parts": run_live_parts,
            "live_flags": live_flags,
            "hidden_in": hidden_in,
            "query_heads": run_query_heads,
            "keys_local": keys_local,
            "values_local": values_local,
            "keys_all": keys_all,
            "values_all": values_all,
            "live_keys": live_keys,
            "log_total": log_total,
            "attended_parts": attended_parts,
            "att_values": att_values,
            "middles": middles,
            "hidden_mid": hidden_mid,
            "pre_acts": pre_acts,
            "activs": activs,
            "mlp_values": mlp_values,
            "finals": finals,
        }
        qkv_back, up_back, out_back, down_back = (qkv_full, up_full, out_full, down_full)
        batch_terms = None
        image_outputs.append(saved_list["finals"][0])
        text_outputs.append(saved_list["finals"][1])
        slot = saved_list["slot"]
        mod_slot = saved_list["mod_slot"]
        inputs = saved_list["inputs"]
        live_parts = saved_list["live_parts"]
        cotangents = (image_cotangent[slot], text_cotangent[slot])
        keys_back = saved_list["keys_all"]
        values_back = saved_list["values_all"]
        live_back = saved_list["live_keys"]
        query_heads = saved_list["query_heads"]
        row_count = query_heads.shape[0]
        key_count = keys_back.shape[0]
        grad_finals = []
        gate2_grads = []
        down_bias_grads = []
        down_terms = []
        up_bias_grads = []
        up_terms = []
        hid2_parts = []
        for stream in range(2):
            grad_final = (
                cotangents[stream].astype(jnp.float32)
                * live_parts[stream][:, None]
                * own_weights[slot]
            )
            grad_finals.append(grad_final)
            gate2_grads.append(jnp.sum(grad_final * saved_list["mlp_values"][stream], axis=0))
            grad_mlp = grad_final * mod_slot[stream, 5]
            down_bias_grads.append(jnp.sum(grad_mlp, axis=0))
            grad_mlp_low = grad_mlp.astype(jnp.bfloat16)
            down_terms.append(
                jnp.einsum(
                    "rf,rd->df",
                    saved_list["activs"][stream],
                    grad_mlp_low,
                    preferred_element_type=jnp.float32,
                )
            )
            grad_act = jnp.einsum(
                "rd,fd->rf", grad_mlp_low, down_back[stream], preferred_element_type=jnp.float32
            )
            pre_grad = jax.vjp(gelu_tanh, saved_list["pre_acts"][stream])[1](grad_act)[0]
            up_bias_grads.append(jnp.sum(pre_grad, axis=0))
            pre_low = pre_grad.astype(jnp.bfloat16)
            up_terms.append(
                jnp.einsum(
                    "rd,rf->df",
                    saved_list["hidden_mid"][stream],
                    pre_low,
                    preferred_element_type=jnp.float32,
                )
            )
            hid2_parts.append(
                jnp.einsum(
                    "rf,df->rd", pre_low, up_back[stream], preferred_element_type=jnp.float32
                )
            )
        hid2_sums = tensor_sum((hid2_parts[0], hid2_parts[1]))
        grad_middles = []
        mid_mod_grads = []
        gate1_grads = []
        out_bias_grads = []
        out_terms = []
        grad_attended = []
        for stream in range(2):
            pulled = jax.vjp(
                modulate, saved_list["middles"][stream], mod_slot[stream, 3], mod_slot[stream, 4]
            )[1](hid2_sums[stream])
            grad_middle = grad_finals[stream] + pulled[0]
            grad_middles.append(grad_middle)
            mid_mod_grads.append((pulled[1], pulled[2]))
            gate1_grads.append(jnp.sum(grad_middle * saved_list["att_values"][stream], axis=0))
            grad_att = grad_middle * mod_slot[stream, 2]
            out_bias_grads.append(jnp.sum(grad_att, axis=0))
            grad_att_low = grad_att.astype(jnp.bfloat16)
            out_terms.append(
                jnp.einsum(
                    "rh,rd->dh",
                    saved_list["attended_parts"][stream],
                    grad_att_low,
                    preferred_element_type=jnp.float32,
                )
            )
            grad_attended.append(
                jnp.einsum(
                    "rd,hd->rh", grad_att_low, out_back[stream], preferred_element_type=jnp.float32
                )
            )
        grad_heads = (
            jnp.concatenate(grad_attended, axis=0)
            .astype(jnp.bfloat16)
            .reshape(row_count, heads_local, HEAD)
        )
        key_heads_back = keys_back.reshape(key_count, heads_local, HEAD)
        value_heads_back = values_back.reshape(key_count, heads_local, HEAD)
        scores_back = (
            jnp.einsum(
                "rhe,khe->hrk", query_heads, key_heads_back, preferred_element_type=jnp.float32
            )
            * score_scale
        )
        scores_back = jnp.where(live_back[None, None, :] > 0, scores_back, -1e30)
        probs_back = jnp.exp(scores_back - saved_list["log_total"])
        grad_probs = jnp.einsum(
            "rhe,khe->hrk", grad_heads, value_heads_back, preferred_element_type=jnp.float32
        )
        inner_sum = jnp.sum(probs_back * grad_probs, axis=-1, keepdims=True)
        grad_scores = (probs_back * (grad_probs - inner_sum)).astype(jnp.bfloat16)
        grad_query = (
            jnp.einsum(
                "hrk,khe->rhe", grad_scores, key_heads_back, preferred_element_type=jnp.float32
            )
            * score_scale
        )
        grad_key_all = (
            jnp.einsum("hrk,rhe->khe", grad_scores, query_heads, preferred_element_type=jnp.float32)
            * score_scale
        )
        grad_value_all = jnp.einsum(
            "hrk,rhe->khe",
            probs_back.astype(jnp.bfloat16),
            grad_heads,
            preferred_element_type=jnp.float32,
        )
        key_terms = jnp.concatenate(
            [
                grad_key_all.reshape(key_count, width_local),
                grad_value_all.reshape(key_count, width_local),
            ],
            axis=-1,
        )
        own_pairs = lax.psum_scatter(
            key_terms.astype(jnp.bfloat16), "ctx", scatter_dimension=0, tiled=True
        ).astype(jnp.float32)
        grad_query = grad_query.reshape(row_count, width_local)
        grad_keys = own_pairs[:, :width_local]
        grad_values = own_pairs[:, width_local:]
        qv_grads = []
        qkv_terms = []
        hid_parts = []
        for stream in range(2):
            lower = 0 if stream == 0 else cap_image
            upper = cap_image if stream == 0 else row_count
            query_part = grad_query[lower:upper]
            value_part = grad_values[lower:upper]
            qv_grads.append(
                jnp.stack([jnp.sum(query_part, axis=0), jnp.sum(value_part, axis=0)], axis=0)
            )
            stacked = jnp.stack([query_part, grad_keys[lower:upper], value_part], axis=1).astype(
                jnp.bfloat16
            )
            qkv_terms.append(
                jnp.einsum(
                    "rd,rke->dke",
                    saved_list["hidden_in"][stream],
                    stacked,
                    preferred_element_type=jnp.float32,
                )
            )
            hid_parts.append(
                jnp.einsum(
                    "rke,dke->rd", stacked, qkv_back[stream], preferred_element_type=jnp.float32
                )
            )
        hid_sums = tensor_sum((hid_parts[0], hid_parts[1]))
        mod_rows = []
        input_grads = []
        for stream in range(2):
            pulled = jax.vjp(modulate, inputs[stream], mod_slot[stream, 0], mod_slot[stream, 1])[1](
                hid_sums[stream]
            )
            input_grads.append((grad_middles[stream] + pulled[0]).astype(jnp.bfloat16))
            mod_rows.append(
                jnp.stack(
                    [
                        pulled[1],
                        pulled[2],
                        gate1_grads[stream],
                        mid_mod_grads[stream][0],
                        mid_mod_grads[stream][1],
                        gate2_grads[stream],
                    ],
                    axis=0,
                )
            )
        summed = (
            lax.psum(jnp.stack(mod_rows, axis=0).astype(jnp.bfloat16), "ctx").astype(jnp.float32),
            lax.psum(jnp.stack(qv_grads, axis=0).astype(jnp.bfloat16), "ctx").astype(jnp.float32),
            lax.psum(jnp.stack(up_bias_grads, axis=0).astype(jnp.bfloat16), "ctx").astype(
                jnp.float32
            ),
            lax.psum(jnp.stack(out_bias_grads, axis=0).astype(jnp.bfloat16), "ctx").astype(
                jnp.float32
            ),
            lax.psum(jnp.stack(down_bias_grads, axis=0).astype(jnp.bfloat16), "ctx").astype(
                jnp.float32
            ),
        )
        terms = (
            qkv_terms[0],
            qkv_terms[1],
            up_terms[0],
            up_terms[1],
            out_terms[0],
            out_terms[1],
            down_terms[0],
            down_terms[1],
        )
        input_grads, mod_row, bias_parts, terms = (input_grads, summed[0], summed[1:], terms)
        image_grads.append(input_grads[0])
        text_grads.append(input_grads[1])
        mod_grad_list.append(mod_row)
        if bias_totals is None:
            bias_totals = bias_parts
        else:
            bias_totals = tuple((total + part for total, part in zip(bias_totals, bias_parts)))
        batch_terms = terms
        batch_part = jax.tree.map(
            lambda part: part.astype(jnp.float32),
            lax.psum_scatter(shortened(batch_terms), "fsdp", scatter_dimension=0, tiled=True),
        )
        if grad_totals is None:
            grad_totals = batch_part
        else:
            grad_totals = tuple((total + part for total, part in zip(grad_totals, batch_part)))
    weight_sums = jax.tree.map(
        lambda part: part.astype(jnp.float32), lax.psum(shortened(grad_totals), "ctx")
    )
    mod_grads = jnp.stack(mod_grad_list, axis=0)
    mod_half_grads = lax.dynamic_slice_in_dim(mod_grads, tp_index * spans, spans, 2)
    gathered = (
        lax.all_gather(mod_half_grads.astype(jnp.bfloat16), "fsdp", axis=0, tiled=True).astype(
            mod_half_grads.dtype
        ),
        lax.all_gather(
            bias_totals[0][None].astype(jnp.bfloat16), "fsdp", axis=0, tiled=True
        ).astype(jnp.float32),
        lax.all_gather(
            bias_totals[1][None].astype(jnp.bfloat16), "fsdp", axis=0, tiled=True
        ).astype(jnp.float32),
        lax.all_gather(
            bias_totals[2][None].astype(jnp.bfloat16), "fsdp", axis=0, tiled=True
        ).astype(jnp.float32),
        lax.all_gather(
            bias_totals[3][None].astype(jnp.bfloat16), "fsdp", axis=0, tiled=True
        ).astype(jnp.float32),
    )
    mod_all = gathered[0]
    ada_bias_grad = jnp.sum(mod_all, axis=0).reshape(2, spans * D)
    mod_low = mod_all.astype(jnp.bfloat16)
    ada_weight_grad = jnp.einsum(
        "sd,stke->tdke", activated, mod_low, preferred_element_type=jnp.float32
    ).reshape(2, rows_local, spans * D)
    silu_part = jnp.einsum("stke,tdke->sd", mod_low, ada_local, preferred_element_type=jnp.float32)
    silu_grad = tensor_sum(silu_part)
    cond_grad = jax.vjp(jax.nn.silu, cond_float)[1](silu_grad)[0]
    qkv_grad = jnp.stack([weight_sums[0], weight_sums[1]], axis=0)
    up_grad = jnp.stack([weight_sums[2], weight_sums[3]], axis=0)
    out_grad = jnp.transpose(jnp.stack([weight_sums[4], weight_sums[5]], axis=0), (0, 2, 1))
    down_grad = jnp.transpose(jnp.stack([weight_sums[6], weight_sums[7]], axis=0), (0, 2, 1))
    return (
        jnp.stack(image_outputs, axis=0),
        jnp.stack(text_outputs, axis=0),
        jnp.stack(image_grads, axis=0),
        jnp.stack(text_grads, axis=0),
        cond_grad,
        ada_weight_grad,
        ada_bias_grad,
        qkv_grad,
        jnp.sum(gathered[1], axis=0),
        out_grad,
        jnp.sum(gathered[3], axis=0),
        up_grad,
        jnp.sum(gathered[2], axis=0),
        down_grad,
        jnp.sum(gathered[4], axis=0),
    )


def solution(mesh):
    return jax.shard_map(
        on_device,
        mesh=mesh,
        in_specs=(
            P("fsdp", "ctx", None),
            P("fsdp", "ctx", None),
            P(None, "fsdp"),
            P("fsdp", "ctx", None),
            P("fsdp", "ctx", None),
            P("fsdp", None),
            P("fsdp", None),
            P(),
            P(None, "fsdp", "tp"),
            P(None, "tp"),
            P(None, "fsdp", None, "tp"),
            P(None, None, "tp"),
            P(None, "tp", "fsdp"),
            P(),
            P(None, "fsdp", "tp"),
            P(None, "tp"),
            P(None, "tp", "fsdp"),
            P(),
        ),
        out_specs=(
            P("fsdp", "ctx", None),
            P("fsdp", "ctx", None),
            P("fsdp", "ctx", None),
            P("fsdp", "ctx", None),
            P(None, "fsdp"),
            P(None, "fsdp", "tp"),
            P(None, "tp"),
            P(None, "fsdp", None, "tp"),
            P(None, None, "tp"),
            P(None, "tp", "fsdp"),
            P(),
            P(None, "fsdp", "tp"),
            P(None, "tp"),
            P(None, "tp", "fsdp"),
            P(),
        ),
        check_vma=False,
    )
```

profile of v0, /device:TPU:0, one launch (start us, length us, event | category | flops | bytes accessed | tf_op | source)
XLA Modules:
  0.0 3152.3 jit_solution(1375499902796274341)
XLA Ops:
  22.4 47.9 %all-reduce.18.cloned.1.call-done = f32[16,2,3,1536]{3,0,2,1:T(8,128)} async-done(((f32[16,2,3,1536]{3,0,2,1:T(8,128)}), f32[16,2,3,1536]{3,0,2,1:T(8,128)}) %all-reduce.18.cloned.1.call-update) | async-done | bytes 589840
  78.0 122.6 %all-gather.16.cloned.1.call-done = bf16[2,1536,3,768]{3,1,2,0:T(8,128)(2,1)} async-done(((bf16[2,192,3,768]{3,1,2,0:T(8,128)(2,1)}), bf16[2,1536,3,768]{3,1,2,0:T(8,128)(2,1)}) %all-gather.16.cloned.1.call-update) | async-done | bytes 14155792 | tf_op jit(solution)/shard_map/all_gather | solution.py:43
  253.4 19.5 fusion.474
  273.5 19.2 fusion
  296.9 17.9 fusion.218
  316.6 19.2 all-gather.22.cloned.1.call-done
  346.9 58.1 %all-reduce.26.cloned.1.call-done = (bf16[576,1536]{1,0:T(8,128)(2,1)}, bf16[88,1536]{1,0:T(8,128)(2,1)}) async-done(((bf16[576,1536]{1,0:T(8,128)(2,1)}, bf16[88,1536]{1,0:T(8,128)(2,1)}), (bf16[576,1536]{1,0:T(8,128)(2,1)}, bf16[88,1536]{1,0:T(8,128)(2,1)})) %all-reduce.26.cloned.1.call-update) | async-done | bytes 2039824 | tf_op jit(solution)/shard_map/psum | solution.py:38
  466.3 30.5 all-gather.30.cloned.1.call-done
  501.0 21.9 fusion.475
  522.9 18.8 fusion.1
  542.3 18.1 fusion.219
  569.3 97.5 %all-gather.24.cloned.1.call-done = bf16[2,1536,3072]{2,1,0:T(8,128)(2,1)} async-done(((bf16[2,192,3072]{2,1,0:T(8,128)(2,1)}), bf16[2,1536,3072]{2,1,0:T(8,128)(2,1)}) %all-gather.24.cloned.1.call-update) | async-done | bytes 18874384 | tf_op jit(solution)/shard_map/all_gather | solution.py:44
  673.4 161.4 %all-gather.26.cloned.1.call-done = bf16[2,3072,1536]{1,2,0:T(8,128)(2,1)} async-done(((bf16[2,3072,192]{1,2,0:T(8,128)(2,1)}), bf16[2,3072,1536]{1,2,0:T(8,128)(2,1)}) %all-gather.26.cloned.1.call-update) | async-done | bytes 18874384 | tf_op jit(solution)/shard_map/all_gather | solution.py:51
  859.1 15.3 fusion.479
  900.5 89.6 %all-reduce.24.cloned.1.call-done = (bf16[576,1536]{1,0:T(8,128)(2,1)}, bf16[576,1536]{1,0:T(8,128)(2,1)}, bf16[88,1536]{1,0:T(8,128)(2,1)}, bf16[88,1536]{1,0:T(8,128)(2,1)}) async-done(((bf16[576,1536]{1,0:T(8,128)(2,1)}, bf16[576,1536]{1,0:T(8,128)(2,1)}, bf16[88,1536]{1,0:T(8,128)(2,1)}, bf16[88,1536]{1,0:T(8,128)(2,1)}), (bf16[576,1536]{1,0:T(8,128)(2,1)}, bf16[576,1536]{1,0:T(8,128)(2,1)}, ...) | async-done | bytes 4079632 | tf_op jit(solution)/shard_map/psum | solution.py:38
  1014.0 18.7 fusion.120
  1032.7 29.9 multiply_reduce_fusion.1
  1062.6 36.3 %multiply_convert_fusion.1 = bf16[12,664,1328]{2,1,0:T(8,128)(2,1)} fusion(f32[12,664,1328]{2,1,0:T(8,128)} %get-tuple-element.168, f32[12,664,1328]{2,1,0:T(8,128)} %get-tuple-element.164, f32[12,664]{1,0:T(8,128)} %get-tuple-element.167, f32[12,664]{1,0:T(8,128)} %log_add_fusion.1), kind=kLoop, calls=%fused_computation.3 | loop fusion | flops 42326016 | bytes 105878784 | tf_op jit(solution)/shard_map/convert_element_type | solution.py:347
  1098.9 13.6 multiply_bitcast_fusion.1
  1175.1 15.4 fusion.477
  1223.2 105.6 %all-reduce.22.cloned.1.call-done = (bf16[576,1536]{1,0:T(8,128)(2,1)}, bf16[576,1536]{1,0:T(8,128)(2,1)}, bf16[88,1536]{1,0:T(8,128)(2,1)}, bf16[88,1536]{1,0:T(8,128)(2,1)}) async-done(((bf16[576,1536]{1,0:T(8,128)(2,1)}, bf16[576,1536]{1,0:T(8,128)(2,1)}, bf16[88,1536]{1,0:T(8,128)(2,1)}, bf16[88,1536]{1,0:T(8,128)(2,1)}), (bf16[576,1536]{1,0:T(8,128)(2,1)}, bf16[576,1536]{1,0:T(8,128)(2,1)}, ...) | async-done | bytes 4079632 | tf_op jit(solution)/shard_map/psum | solution.py:38
  1353.9 17.8 fusion.123
  1371.6 29.2 multiply_reduce_fusion
  1403.3 36.1 %multiply_convert_fusion = bf16[12,664,1328]{2,1,0:T(8,128)(2,1)} fusion(f32[12,664,1328]{2,1,0:T(8,128)} %get-tuple-element.170, f32[12,664,1328]{2,1,0:T(8,128)} %get-tuple-element.166, f32[12,664]{1,0:T(8,128)S(1)} %get-tuple-element.169, f32[12,664]{1,0:T(8,128)S(1)} %copy-done.57), kind=kLoop, calls=%fused_computation | loop fusion | flops 42326016 | bytes 105878784 | tf_op jit(solution)/shard_map/convert_element_type | solution.py:347
  1476.6 15.0 convolution_convert_fusion.5
  1491.8 14.7 convolution_convert_fusion.4
  1536.3 13.0 convolution_convert_fusion.7
  1550.0 12.9 convolution_convert_fusion.6
  1571.1 13.7 fusion.126
  1604.2 13.7 multiply_bitcast_fusion
  1764.0 100.1 %reduce-scatter.50.cloned.1.call-done = bf16[192,3072]{1,0:T(8,128)(2,1)} async-done(((bf16[1536,3072]{1,0:T(8,128)(2,1)}), bf16[192,3072]{1,0:T(8,128)(2,1)}) %reduce-scatter.50.cloned.1.call-update) | async-done | bytes 1179664 | tf_op jit(solution)/shard_map/reduce_scatter | solution.py:459
  1867.1 97.2 %reduce-scatter.52.cloned.1.call-done = bf16[192,3072]{1,0:T(8,128)(2,1)} async-done(((bf16[1536,3072]{1,0:T(8,128)(2,1)}), bf16[192,3072]{1,0:T(8,128)(2,1)}) %reduce-scatter.52.cloned.1.call-update) | async-done | bytes 1179664 | tf_op jit(solution)/shard_map/reduce_scatter | solution.py:459
  1964.3 100.2 %reduce-scatter.54.cloned.1.call-done = bf16[192,3072]{1,0:T(8,128)(2,1)} async-done(((bf16[1536,3072]{1,0:T(8,128)(2,1)}), bf16[192,3072]{1,0:T(8,128)(2,1)}) %reduce-scatter.54.cloned.1.call-update) | async-done | bytes 1179664 | tf_op jit(solution)/shard_map/reduce_scatter | solution.py:459
  2067.6 97.1 %reduce-scatter.44.cloned.1.call-done = bf16[192,3072]{1,0:T(8,128)(2,1)} async-done(((bf16[1536,3072]{1,0:T(8,128)(2,1)}), bf16[192,3072]{1,0:T(8,128)(2,1)}) %reduce-scatter.44.cloned.1.call-update) | async-done | bytes 1179664 | tf_op jit(solution)/shard_map/reduce_scatter | solution.py:459
  2164.7 100.1 %reduce-scatter.46.cloned.1.call-done = bf16[192,3072]{1,0:T(8,128)(2,1)} async-done(((bf16[1536,3072]{1,0:T(8,128)(2,1)}), bf16[192,3072]{1,0:T(8,128)(2,1)}) %reduce-scatter.46.cloned.1.call-update) | async-done | bytes 1179664 | tf_op jit(solution)/shard_map/reduce_scatter | solution.py:459
  2267.8 97.2 %reduce-scatter.40.cloned.1.call-done = bf16[192,3072]{1,0:T(8,128)(2,1)} async-done(((bf16[1536,3072]{1,0:T(8,128)(2,1)}), bf16[192,3072]{1,0:T(8,128)(2,1)}) %reduce-scatter.40.cloned.1.call-update) | async-done | bytes 1179664 | tf_op jit(solution)/shard_map/reduce_scatter | solution.py:459
  2365.0 100.1 %reduce-scatter.42.cloned.1.call-done = bf16[192,3072]{1,0:T(8,128)(2,1)} async-done(((bf16[1536,3072]{1,0:T(8,128)(2,1)}), bf16[192,3072]{1,0:T(8,128)(2,1)}) %reduce-scatter.42.cloned.1.call-update) | async-done | bytes 1179664 | tf_op jit(solution)/shard_map/reduce_scatter | solution.py:459
  2471.4 146.0 %all-reduce.20.cloned.1.call-done = (bf16[576,1536]{1,0:T(8,128)(2,1)}, bf16[576,1536]{1,0:T(8,128)(2,1)}, bf16[88,1536]{1,0:T(8,128)(2,1)}, bf16[88,1536]{1,0:T...) async-done(((bf16[576,1536]{1,0:T(8,128)(2,1)}, bf16[576,1536]{1,0:T(8,128)(2,1)}, bf16[88,1536]{1,0:T(8,128)(2,1)}, bf16[88,1536]{1,0:T(8,128)(2,1)}, ...) | async-done | bytes 6119440 | tf_op jit(solution)/shard_map/psum | solution.py:38
  2672.0 25.3 reduce-scatter.24.cloned.1.call-done
  2697.3 78.0 %reduce-scatter.26.cloned.1.call-done = bf16[192,3,768]{2,0,1:T(8,128)(2,1)} async-done(((bf16[1536,3,768]{2,0,1:T(8,128)(2,1)}), bf16[192,3,768]{2,0,1:T(8,128)(2,1)}) %reduce-scatter.26.cloned.1.call-update) | async-done | bytes 884752 | tf_op jit(solution)/shard_map/reduce_scatter | solution.py:459
  2777.9 75.3 %reduce-scatter.28.cloned.1.call-done = bf16[192,3,768]{2,0,1:T(8,128)(2,1)} async-done(((bf16[1536,3,768]{2,0,1:T(8,128)(2,1)}), bf16[192,3,768]{2,0,1:T(8,128)(2,1)}) %reduce-scatter.28.cloned.1.call-update) | async-done | bytes 884752 | tf_op jit(solution)/shard_map/reduce_scatter | solution.py:459
  2853.2 78.6 %reduce-scatter.30.cloned.1.call-done = bf16[192,3,768]{2,0,1:T(8,128)(2,1)} async-done(((bf16[1536,3,768]{2,0,1:T(8,128)(2,1)}), bf16[192,3,768]{2,0,1:T(8,128)(2,1)}) %reduce-scatter.30.cloned.1.call-update) | async-done | bytes 884752 | tf_op jit(solution)/shard_map/reduce_scatter | solution.py:459
  2958.7 14.3 all_gather.63
  2984.6 14.0 all-gather.6
  2998.6 14.0 all-gather.4
  3012.6 14.0 all-gather
  3026.6 14.0 all-gather.5
  3043.8 90.6 %all-reduce.30.cloned.1.call-done = (bf16[1,192,3,768]{3,1,2,0:T(8,128)(2,1)}, bf16[1,192,3,768]{3,1,2,0:T(8,128)(2,1)}, bf16[1,192,768]{2,1,0:T(8,128)(2,1)}, b...) async-done(((bf16[1,192,3,768]{3,1,2,0:T(8,128)(2,1)}, ...) | async-done | bytes 7077904 | tf_op jit(solution)/shard_map/psum | solution.py:466
  (899 shorter events, 734.4 us)
Async XLA Ops:
  7.2 63.2 %all-reduce.18.cloned.1.call-start = ((), (), s32[]{:S(2)}) async-start(), calls=%async_computation.44 | async-start | bytes 1179648
  10.8 189.8 %all-gather.16.cloned.1.call-start = ((), (), s32[]{:S(2)}) async-start(), calls=%async_computation.18 | async-start | bytes 15925248 | tf_op jit(solution)/shard_map/all_gather | solution.py:43
  11.6 237.7 %all-gather.20.cloned.1.call-start = ((), (), s32[]{:S(2)}) async-start(), calls=%async_computation.20 | async-start | bytes 3059712 | tf_op jit(solution)/shard_map/all_gather | solution.py:57
  78.0 127.2 %copy-start.112 = (f32[1536]{0:T(1024)}, f32[1536]{0:T(1024)S(1)}, u32[]{:S(2)}) copy-start(f32[1536]{0:T(1024)S(1)} %get-tuple-element.77) | copy-start | bytes 18436
  78.0 128.1 %copy-start.132 = (f32[1536]{0:T(1024)}, f32[1536]{0:T(1024)S(1)}, u32[]{:S(2)}) copy-start(f32[1536]{0:T(1024)S(1)} %get-tuple-element.79) | copy-start | bytes 18436
  217.2 75.6 %all-gather.18.cloned.1.call-start = ((), (), s32[]{:S(2)}) async-start(), calls=%async_computation.19 | async-start | bytes 3059712 | tf_op jit(solution)/shard_map/all_gather | solution.py:58
  221.5 114.3 %all-gather.22.cloned.1.call-start = ((), (), s32[]{:S(2)}) async-start(), calls=%async_computation.21 | async-start | bytes 5308416 | tf_op jit(solution)/shard_map/all_gather | solution.py:50
  222.1 182.9 %all-reduce.26.cloned.1.call-start = ((), (), s32[]{:S(2)}) async-start(), calls=%async_computation.48 | async-start | bytes 4079616 | tf_op jit(solution)/shard_map/psum | solution.py:38
  344.2 118.0 %all-gather.28.cloned.1.call-start = ((), (), s32[]{:S(2)}) async-start(), calls=%async_computation.24 | async-start | bytes 3059712 | tf_op jit(solution)/shard_map/all_gather | solution.py:58
  345.2 997.4 %copy-start.66 = (f32[1536]{0:T(1024)}, f32[1536]{0:T(1024)S(1)}, u32[]{:S(2)}) copy-start(f32[1536]{0:T(1024)S(1)} %get-tuple-element.95) | copy-start | bytes 18436
  345.2 1000.1 %copy-start.79 = (f32[1536]{0:T(1024)}, f32[1536]{0:T(1024)S(1)}, u32[]{:S(2)}) copy-start(f32[1536]{0:T(1024)S(1)} %get-tuple-element.96) | copy-start | bytes 18436
  429.4 67.4 %all-gather.30.cloned.1.call-start = ((), (), s32[]{:S(2)}) async-start(), calls=%async_computation.25 | async-start | bytes 3059712 | tf_op jit(solution)/shard_map/all_gather | solution.py:57
  433.1 233.7 %all-gather.24.cloned.1.call-start = ((), (), s32[]{:S(2)}) async-start(), calls=%async_computation.22 | async-start | bytes 21233664 | tf_op jit(solution)/shard_map/all_gather | solution.py:44
  433.8 401.0 %all-gather.26.cloned.1.call-start = ((), (), s32[]{:S(2)}) async-start(), calls=%async_computation.23 | async-start | bytes 21233664 | tf_op jit(solution)/shard_map/all_gather | solution.py:51
  434.4 555.8 %all-reduce.24.cloned.1.call-start = ((), (), s32[]{:S(2)}) async-start(), calls=%async_computation.47 | async-start | bytes 8159232 | tf_op jit(solution)/shard_map/psum | solution.py:38
  885.4 316.3 %reduce-scatter.20.cloned.1.call-start = ((), (), s32[]{:S(2)}) async-start(), calls=%async_computation.26 | async-start | bytes 6119424 | tf_op jit(solution)/shard_map/reduce_scatter | solution.py:371
  1136.8 192.0 %all-reduce.22.cloned.1.call-start = ((), (), s32[]{:S(2)}) async-start(), calls=%async_computation.46 | async-start | bytes 8159232 | tf_op jit(solution)/shard_map/psum | solution.py:38
  1221.7 404.7 %reduce-scatter.22.cloned.1.call-start = ((), (), s32[]{:S(2)}) async-start(), calls=%async_computation.27 | async-start | bytes 6119424 | tf_op jit(solution)/shard_map/reduce_scatter | solution.py:371
  1403.3 36.1 %copy-start.40 = (bf16[576,12,64]{0,2,1:T(8,128)(2,1)S(1)}, bf16[576,12,64]{0,2,1:T(8,128)(2,1)}, u32[]{:S(2)}) copy-start(bf16[576,12,64]{0,2,1:T(8,128)(2,1)} %add_convert_fusion.8) | copy-start | bytes 2654212
  1403.3 36.1 %copy-start.61 = (bf16[88,12,64]{0,2,1:T(8,128)(2,1)S(1)}, bf16[88,12,64]{0,2,1:T(8,128)(2,1)}, u32[]{:S(2)}) copy-start(bf16[88,12,64]{0,2,1:T(8,128)(2,1)} %add_convert_fusion.18) | copy-start | bytes 405508
  1457.8 294.4 %reduce-scatter.32.cloned.1.call-start = ((), (), s32[]{:S(2)}) async-start(), calls=%async_computation.32 | async-start | bytes 2654208 | tf_op jit(solution)/shard_map/reduce_scatter | solution.py:459
  1464.5 287.7 %reduce-scatter.34.cloned.1.call-start = ((), (), s32[]{:S(2)}) async-start(), calls=%async_computation.33 | async-start | bytes 2654208 | tf_op jit(solution)/shard_map/reduce_scatter | solution.py:459
  1469.4 284.6 %reduce-scatter.36.cloned.1.call-start = ((), (), s32[]{:S(2)}) async-start(), calls=%async_computation.34 | async-start | bytes 2654208 | tf_op jit(solution)/shard_map/reduce_scatter | solution.py:459
  1472.9 281.2 %reduce-scatter.38.cloned.1.call-start = ((), (), s32[]{:S(2)}) async-start(), calls=%async_computation.35 | async-start | bytes 2654208 | tf_op jit(solution)/shard_map/reduce_scatter | solution.py:459
  1476.5 287.5 %reduce-scatter.48.cloned.1.call-start = ((), (), s32[]{:S(2)}) async-start(), calls=%async_computation.40 | async-start | bytes 10616832 | tf_op jit(solution)/shard_map/reduce_scatter | solution.py:459
  1491.6 372.5 %reduce-scatter.50.cloned.1.call-start = ((), (), s32[]{:S(2)}) async-start(), calls=%async_computation.41 | async-start | bytes 10616832 | tf_op jit(solution)/shard_map/reduce_scatter | solution.py:459
  1506.6 457.7 %reduce-scatter.52.cloned.1.call-start = ((), (), s32[]{:S(2)}) async-start(), calls=%async_computation.42 | async-start | bytes 10616832 | tf_op jit(solution)/shard_map/reduce_scatter | solution.py:459
  1514.0 550.5 %reduce-scatter.54.cloned.1.call-start = ((), (), s32[]{:S(2)}) async-start(), calls=%async_computation.43 | async-start | bytes 10616832 | tf_op jit(solution)/shard_map/reduce_scatter | solution.py:459
  1521.3 643.4 %reduce-scatter.44.cloned.1.call-start = ((), (), s32[]{:S(2)}) async-start(), calls=%async_computation.38 | async-start | bytes 10616832 | tf_op jit(solution)/shard_map/reduce_scatter | solution.py:459
  1527.9 736.9 %reduce-scatter.46.cloned.1.call-start = ((), (), s32[]{:S(2)}) async-start(), calls=%async_computation.39 | async-start | bytes 10616832 | tf_op jit(solution)/shard_map/reduce_scatter | solution.py:459
  1534.3 830.6 %reduce-scatter.40.cloned.1.call-start = ((), (), s32[]{:S(2)}) async-start(), calls=%async_computation.36 | async-start | bytes 10616832 | tf_op jit(solution)/shard_map/reduce_scatter | solution.py:459
  1549.3 915.7 %reduce-scatter.42.cloned.1.call-start = ((), (), s32[]{:S(2)}) async-start(), calls=%async_computation.37 | async-start | bytes 10616832 | tf_op jit(solution)/shard_map/reduce_scatter | solution.py:459
  1562.9 1054.5 %all-reduce.20.cloned.1.call-start = ((), (), s32[]{:S(2)}) async-start(), calls=%async_computation.45 | async-start | bytes 12238848 | tf_op jit(solution)/shard_map/psum | solution.py:38
  1563.1 29.1 slice-start
  1571.1 21.2 slice-start.1
  1646.1 1051.2 %reduce-scatter.24.cloned.1.call-start = ((), (), s32[]{:S(2)}) async-start(), calls=%async_computation.28 | async-start | bytes 7962624 | tf_op jit(solution)/shard_map/reduce_scatter | solution.py:459
  1656.7 1118.6 %reduce-scatter.26.cloned.1.call-start = ((), (), s32[]{:S(2)}) async-start(), calls=%async_computation.29 | async-start | bytes 7962624 | tf_op jit(solution)/shard_map/reduce_scatter | solution.py:459
  1667.3 1185.9 %reduce-scatter.28.cloned.1.call-start = ((), (), s32[]{:S(2)}) async-start(), calls=%async_computation.30 | async-start | bytes 7962624 | tf_op jit(solution)/shard_map/reduce_scatter | solution.py:459
  1674.2 1257.7 %reduce-scatter.30.cloned.1.call-start = ((), (), s32[]{:S(2)}) async-start(), calls=%async_computation.31 | async-start | bytes 7962624 | tf_op jit(solution)/shard_map/reduce_scatter | solution.py:459
  1680.5 1277.4 %all-reduce.28.cloned.1.call-start = ((), (), s32[]{:S(2)}) async-start(), calls=%async_computation.49 | async-start | bytes 270336 | tf_op jit(solution)/shard_map/psum | solution.py:426
  2671.8 462.7 %all-reduce.30.cloned.1.call-start = ((), (), s32[]{:S(2)}) async-start(), calls=%async_computation.50 | async-start | bytes 14155776 | tf_op jit(solution)/shard_map/psum | solution.py:466
  2952.0 21.8 copy-start.161
  2978.5 20.1 copy-start.231
  2978.5 20.1 copy-start.232
  2978.5 34.1 %copy-start.229 = (bf16[2,2,768]{2,1,0:T(2,128)(2,1)S(1)}, bf16[2,2,768]{2,1,0:T(2,128)(2,1)}, u32[]{:S(2)}) copy-start(bf16[2,2,768]{2,1,0:T(2,128)(2,1)} %get-tuple-element.121) | copy-start | bytes 18436
  2978.5 34.1 %copy-start.230 = (bf16[2,2,768]{2,1,0:T(2,128)(2,1)S(1)}, bf16[2,2,768]{2,1,0:T(2,128)(2,1)}, u32[]{:S(2)}) copy-start(bf16[2,2,768]{2,1,0:T(2,128)(2,1)} %get-tuple-element.122) | copy-start | bytes 18436
  2978.5 48.1 %copy-start.219 = (bf16[2,3072]{1,0:T(2,128)(2,1)S(1)}, bf16[2,3072]{1,0:T(2,128)(2,1)}, u32[]{:S(2)}) copy-start(bf16[2,3072]{1,0:T(2,128)(2,1)} %get-tuple-element.125) | copy-start | bytes 36868
  2978.5 48.1 %copy-start.220 = (bf16[2,3072]{1,0:T(2,128)(2,1)S(1)}, bf16[2,3072]{1,0:T(2,128)(2,1)}, u32[]{:S(2)}) copy-start(bf16[2,3072]{1,0:T(2,128)(2,1)} %get-tuple-element.126) | copy-start | bytes 36868
  (236 other events, 1198.5 us)
Sparse Core Ops, SparseCore 0:
  11.0 59.3 all-reduce.17
  72.0 128.6 all-gather.15
  217.3 30.8 all-gather.19
  250.1 32.5 all-gather.17
  284.1 51.6 all-gather.21
  344.3 60.6 all-reduce.25
  429.5 32.6 all-gather.27
  464.3 32.4 all-gather.29
  498.4 168.2 all-gather.23
  668.2 166.4 all-gather.25
  885.5 104.5 all-reduce.23
  1136.9 53.3 reduce-scatter.19
  1221.9 106.8 all-reduce.21
  1457.9 53.3 reduce-scatter.21
  1513.5 36.2 reduce-scatter.31
  1551.9 35.4 reduce-scatter.33
  1589.6 35.7 reduce-scatter.35
  1627.6 35.2 reduce-scatter.37
  1665.2 98.7 reduce-scatter.47
  1766.2 97.8 reduce-scatter.49
  1866.4 97.8 reduce-scatter.51
  1966.6 97.8 reduce-scatter.53
  2066.8 97.8 reduce-scatter.43
  2166.9 97.8 reduce-scatter.45
  2267.1 97.8 reduce-scatter.39
  2367.1 97.8 reduce-scatter.41
  2467.8 149.5 all-reduce.19
  2619.9 77.3 reduce-scatter.23
  2699.7 75.5 reduce-scatter.25
  2777.6 75.5 reduce-scatter.27
  2856.2 75.5 reduce-scatter.29
  2936.1 21.7 all-reduce.27
  2961.7 172.6 all-reduce.29
where the time goes:
time: 3160 us; the launch traced here: 3150 us
  waiting for transfers between devices  1940 us (61%)
  matrix products  585 us (19%)
  other arithmetic  342 us (11%)
  local copies, waits for them, and re-layouts  182 us (6%)
  blocking collectives  86.4 us (3%)
    reduce_scatter x16, waiting for transfers between devices, on_device(): lax.psum_scatter(shortened(batch_terms), 'fsdp', scatter_dimension=0, til...  957 us
    psum x4, waiting for transfers between devices, tensor_sum(): lax.psum(shortened(parts), 'tp')  399 us
    all_gather x1, waiting for transfers between devices, outer_weights(): lax.all_gather(mlp_down_weight, 'fsdp', axis=2, tiled=True)  161 us
    all_gather x1, waiting for transfers between devices, inner_weights(): lax.all_gather(qkv_weight, 'fsdp', axis=1, tiled=True)  123 us
    all_gather x1, waiting for transfers between devices, inner_weights(): lax.all_gather(mlp_up_weight, 'fsdp', axis=1, tiled=True)  97.5 us
    psum x1, waiting for transfers between devices, on_device(): lax.psum(shortened(grad_totals), 'ctx')  90.6 us
    dot_general x12, matrix products, matmul(): return jnp.dot(left, right, preferred_element_type=jnp.float32)  88.4 us
    convert_element_type x2, other arithmetic, on_device(): grad_scores = (probs_back * (grad_probs - inner_sum)).astype(jnp.bfloat16)  72.4 us
  transfers between devices with their start and end apart: 33, of which 25 were waited for; matrix products, arithmetic and copies ran while one was open for 22% of the time, Pallas kernels for 0%

commit v1 on v0

v1 whole, which is shorter than its diff:
```python
import functools

import jax
import jax.numpy as jnp
from jax import lax
from jax.experimental import pallas as pl
from jax.experimental.pallas import tpu as pltpu
from jax.sharding import Mesh
from jax.sharding import PartitionSpec as P

D = 1536
HEAD = 64
LANES = 128
MB = 2
F32 = jnp.float32
BF16 = jnp.bfloat16
FSDP = ("z", "core")
PAIR = ((0, 1), (1, 0))
DEAD = -1e30


def swap(values, axis):
    return lax.ppermute(values, axis, PAIR)


def pair_sum(values, axis):
    mine = values.astype(BF16)
    return mine.astype(F32) + swap(mine, axis).astype(F32)


def ctx_sum(values):
    if lax.axis_size("ctx") == 2:
        return pair_sum(values, "ctx")
    return lax.psum(values.astype(BF16), "ctx").astype(F32)


def dot(left, right):
    return lax.dot_general(left, right, (((1,), (0,)), ((), ())), preferred_element_type=F32)


def dot_nt(left, right):
    return lax.dot_general(left, right, (((1,), (1,)), ((), ())), preferred_element_type=F32)


def dot_tn(left, right):
    return lax.dot_general(left, right, (((0,), (0,)), ((), ())), preferred_element_type=F32)


def gather_rows(shard):
    streams, rows, columns = shard.shape
    if lax.axis_size("ctx") == 2:
        piece = lax.dynamic_index_in_dim(shard, lax.axis_index("ctx"), 0, keepdims=False)
        whole = lax.all_gather(piece, ("ctx",) + FSDP, axis=0, tiled=True)
        return whole.reshape(streams, -1, columns)
    return lax.all_gather(shard, FSDP, axis=1, tiled=True)


def reduce_rows(part):
    own = lax.psum_scatter(part.astype(BF16), FSDP, scatter_dimension=0, tiled=True)
    return ctx_sum(own)


def scatter_groups(parts):
    z_count = lax.axis_size("z")
    z_index, core = lax.axis_index("z"), lax.axis_index("core")
    split = parts.reshape((z_count, 2) + parts.shape[1:])
    keep = lax.dynamic_index_in_dim(split, core, 1, keepdims=False)
    give = lax.dynamic_index_in_dim(split, 1 - core, 1, keepdims=False)
    chip = keep + swap(give, "core")
    total = lax.dynamic_index_in_dim(chip, z_index, 0, keepdims=False)
    for step in range(1, z_count):
        target = lax.rem(z_index + step, z_count)
        sent = lax.dynamic_index_in_dim(chip, target, 0, keepdims=False)
        total = total + lax.ppermute(
            sent, "z", [(index, (index + step) % z_count) for index in range(z_count)]
        )
    return total


def normalise(values):
    row_mean = jnp.mean(values, axis=-1, keepdims=True)
    centred = values - row_mean
    inverse = lax.rsqrt(jnp.mean(centred * centred, axis=-1, keepdims=True) + 1e-06)
    return centred * inverse, inverse


def modulate(values, shift, scale):
    return normalise(values)[0] * (1.0 + scale) + shift


def modulate_back(values, scale, grad):
    unit, inverse = normalise(values)
    unit_grad = grad * (1.0 + scale)
    first = jnp.mean(unit_grad, axis=-1, keepdims=True)
    second = jnp.mean(unit_grad * unit, axis=-1, keepdims=True)
    back = inverse * (unit_grad - first - unit * second)
    return back, jnp.sum(grad, axis=1), jnp.sum(grad * unit, axis=1)


def gelu_tanh(values):
    return jax.nn.gelu(values, approximate=True)


def masked_pair(image, text, stacked, scale):
    first = lax.broadcasted_iota(jnp.int32, (1, LANES), 1) < HEAD
    rows = image.shape[0]
    half = rows + text.shape[0]
    for head in range(2):
        kept = first if head == 0 else jnp.logical_not(first)
        base = head * half
        stacked[base : base + rows] = jnp.where(kept, image * scale, 0.0).astype(BF16)
        stacked[base + rows : base + half] = jnp.where(kept, text * scale, 0.0).astype(BF16)


def unstack(pair):
    first = lax.broadcasted_iota(jnp.int32, (1, LANES), 1) < HEAD
    turned = pair.T
    half = turned.shape[0] // 2
    return jnp.where(first, turned[:half], turned[half:])


def attend_kernel(parts, image_rows, *refs):
    query_image, query_text = refs[0], refs[1]
    key_refs = refs[2 : 2 + parts]
    value_refs = refs[2 + parts : 2 + 2 * parts]
    bias_refs = refs[2 + 2 * parts : 2 + 3 * parts]
    out_image, out_text, log_ref, queries, scores = refs[2 + 3 * parts :]
    masked_pair(
        query_image[...].astype(F32), query_text[...].astype(F32), queries, HEAD ** (-0.5)
    )
    stacked = queries[...]
    top = None
    base = 0
    for part in range(parts):
        rows = key_refs[part].shape[0]
        score = dot_nt(key_refs[part][...], stacked) + bias_refs[part][...]
        scores[base : base + rows] = score
        part_top = jnp.max(score, axis=0, keepdims=True)
        top = part_top if top is None else jnp.maximum(top, part_top)
        base += rows
    total = jnp.zeros_like(top)
    attended = jnp.zeros((LANES, stacked.shape[0]), F32)
    base = 0
    for part in range(parts):
        rows = key_refs[part].shape[0]
        exponent = jnp.exp(scores[base : base + rows] - top)
        total = total + jnp.sum(exponent, axis=0, keepdims=True)
        attended = attended + dot_tn(value_refs[part][...], exponent.astype(BF16))
        base += rows
    result = unstack(attended / total)
    out_image[...] = result[:image_rows].astype(BF16)
    out_text[...] = result[image_rows:].astype(BF16)
    log_ref[...] = top + jnp.log(total)


def attend_back_kernel(streams, image_rows, *refs):
    parts = len(streams)
    query_image, query_text, out_image, out_text, grad_image, grad_text, log_ref = refs[:7]
    key_refs = refs[7 : 7 + parts]
    value_refs = refs[7 + parts : 7 + 2 * parts]
    bias_refs = refs[7 + 2 * parts : 7 + 3 * parts]
    rest = refs[7 + 3 * parts :]
    query_grad_image, query_grad_text, query_sum, value_sum = rest[:4]
    pair_grads = rest[4 : 4 + parts]
    queries, grads, products = rest[4 + parts :]
    masked_pair(
        query_image[...].astype(F32), query_text[...].astype(F32), queries, HEAD ** (-0.5)
    )
    grad_rows_image, grad_rows_text = grad_image[...].astype(F32), grad_text[...].astype(F32)
    masked_pair(grad_rows_image, grad_rows_text, grads, 1.0)
    first = lax.broadcasted_iota(jnp.int32, (1, LANES), 1) < HEAD
    product_image = grad_rows_image * out_image[...].astype(F32)
    product_text = grad_rows_text * out_text[...].astype(F32)
    half = product_image.shape[0] + product_text.shape[0]
    for head in range(2):
        kept = first if head == 0 else jnp.logical_not(first)
        base = head * half
        products[base : base + image_rows] = jnp.where(kept, product_image, 0.0)
        products[base + image_rows : base + half] = jnp.where(kept, product_text, 0.0)
    inner = jnp.sum(products[...].T, axis=0, keepdims=True)
    stacked, grad_stacked = queries[...], grads[...]
    log_total = log_ref[...]
    query_grad = jnp.zeros((LANES, stacked.shape[0]), F32)
    value_totals = [jnp.zeros((1, LANES), F32) for _ in range(2)]
    for part in range(parts):
        keys, values = key_refs[part][...], value_refs[part][...]
        probs = jnp.exp(dot_nt(keys, stacked) + bias_refs[part][...] - log_total)
        grad_probs = dot_nt(values, grad_stacked)
        grad_scores = (probs * (grad_probs - inner)).astype(BF16)
        value_grad = dot(probs.astype(BF16), grad_stacked)
        pair_grads[part][1] = value_grad.astype(BF16)
        stream = streams[part]
        value_totals[stream] = value_totals[stream] + jnp.sum(value_grad, axis=0, keepdims=True)
        pair_grads[part][0] = dot(grad_scores, stacked).astype(BF16)
        query_grad = query_grad + dot_tn(keys, grad_scores)
    result = unstack(query_grad) * HEAD ** (-0.5)
    query_grad_image[...] = result[:image_rows].astype(BF16)
    query_grad_text[...] = result[image_rows:].astype(BF16)
    query_sum[0:1] = jnp.sum(result[:image_rows], axis=0, keepdims=True)
    query_sum[1:2] = jnp.sum(result[image_rows:], axis=0, keepdims=True)
    for stream in range(2):
        value_sum[stream : stream + 1] = value_totals[stream]


def block_of(slot, rows, base=0):
    return pl.BlockSpec((None, rows, LANES), lambda pair: (slot, 0, base + pair))


def flat_block(rows, base=0):
    return pl.BlockSpec((rows, LANES), lambda pair: (0, base + pair))


def column_block(rows):
    return pl.BlockSpec((rows, 1), lambda pair: (0, 0))


def key_specs(slot, key_parts, pairs):
    keys, values, biases = [], [], []
    for rows_array, _, here, _ in key_parts:
        rows = rows_array.shape[-2]
        if here:
            keys.append(block_of(slot, rows))
            values.append(block_of(slot, rows, pairs))
        else:
            keys.append(flat_block(rows))
            values.append(flat_block(rows, pairs))
        biases.append(column_block(rows))
    return keys + values + biases


def key_operands(key_parts):
    arrays = [part[0] for part in key_parts]
    return arrays + arrays + [part[1] for part in key_parts]


def attend(slot, queries, key_parts):
    image, text = queries
    image_rows, text_rows = image.shape[1], text.shape[1]
    width = image.shape[2]
    pairs = width // LANES
    stacked = 2 * (image_rows + text_rows)
    key_rows = sum(part[0].shape[-2] for part in key_parts)
    return pl.pallas_call(
        functools.partial(attend_kernel, len(key_parts), image_rows),
        grid=(pairs,),
        in_specs=[block_of(slot, image_rows), block_of(slot, text_rows)]
        + key_specs(slot, key_parts, pairs),
        out_specs=[
            flat_block(image_rows),
            flat_block(text_rows),
            pl.BlockSpec((None, 1, stacked), lambda pair: (pair, 0, 0)),
        ],
        out_shape=[
            jax.ShapeDtypeStruct((image_rows, width), BF16),
            jax.ShapeDtypeStruct((text_rows, width), BF16),
            jax.ShapeDtypeStruct((pairs, 1, stacked), F32),
        ],
        scratch_shapes=[
            pltpu.VMEM((stacked, LANES), BF16),
            pltpu.VMEM((key_rows, stacked), F32),
        ],
        compiler_params=pltpu.CompilerParams(vmem_limit_bytes=48 * 1024 * 1024),
        cost_estimate=pl.CostEstimate(
            flops=pairs * 4 * key_rows * stacked * 4 * LANES,
            bytes_accessed=2 * width * (2 * image_rows + 2 * key_rows),
            transcendentals=pairs * key_rows * stacked,
        ),
        name="attend",
    )(image, text, *key_operands(key_parts))


def attend_back(slot, queries, outs, grads, log_total, key_parts):
    image, text = queries
    image_rows, text_rows = image.shape[1], text.shape[1]
    width = image.shape[2]
    pairs = width // LANES
    stacked = 2 * (image_rows + text_rows)
    key_rows = sum(part[0].shape[-2] for part in key_parts)
    part_rows = [part[0].shape[-2] for part in key_parts]
    row_blocks = [block_of(slot, image_rows), block_of(slot, text_rows)]
    sum_block = pl.BlockSpec((None, 2, LANES), lambda pair: (pair, 0, 0))
    sum_shape = jax.ShapeDtypeStruct((pairs, 2, LANES), F32)
    return pl.pallas_call(
        functools.partial(
            attend_back_kernel, tuple(part[3] for part in key_parts), image_rows
        ),
        grid=(pairs,),
        in_specs=row_blocks
        + [flat_block(image_rows), flat_block(text_rows)]
        + row_blocks
        + [pl.BlockSpec((None, 1, stacked), lambda pair: (pair, 0, 0))]
        + key_specs(slot, key_parts, pairs),
        out_specs=[flat_block(image_rows), flat_block(text_rows), sum_block, sum_block]
        + [pl.BlockSpec((2, rows, LANES), lambda pair: (0, 0, pair)) for rows in part_rows],
        out_shape=[
            jax.ShapeDtypeStruct((image_rows, width), BF16),
            jax.ShapeDtypeStruct((text_rows, width), BF16),
            sum_shape,
            sum_shape,
        ]
        + [jax.ShapeDtypeStruct((2, rows, width), BF16) for rows in part_rows],
        scratch_shapes=[
            pltpu.VMEM((stacked, LANES), BF16),
            pltpu.VMEM((stacked, LANES), BF16),
            pltpu.VMEM((stacked, LANES), F32),
        ],
        compiler_params=pltpu.CompilerParams(vmem_limit_bytes=48 * 1024 * 1024),
        cost_estimate=pl.CostEstimate(
            flops=pairs * 10 * key_rows * stacked * 4 * LANES,
            bytes_accessed=2 * width * (4 * image_rows + 4 * key_rows),
            transcendentals=pairs * key_rows * stacked,
        ),
        name="attend_back",
    )(image, text, outs[0], outs[1], grads[0], grads[1], log_total, *key_operands(key_parts))


def on_device(
    image_tokens,
    text_tokens,
    cond_vector,
    image_cotangent,
    text_cotangent,
    image_counts,
    text_counts,
    seq_live,
    ada_weight,
    ada_bias,
    qkv_weight,
    qv_bias,
    attn_out_weight,
    attn_out_bias,
    mlp_up_weight,
    mlp_up_bias,
    mlp_down_weight,
    mlp_down_bias,
):
    slot_count = image_tokens.shape[0]
    per_batch = slot_count // MB
    seq_count = seq_live.shape[0]
    cap_image = image_tokens.shape[1]
    cap_text = text_tokens.shape[1]
    text_rows = -(-cap_text // 16) * 16
    extra = ((0, 0), (0, text_rows - cap_text), (0, 0))
    caps = (cap_image, text_rows)
    group_index = lax.axis_index("z") * 2 + lax.axis_index("core")
    ctx_count = lax.axis_size("ctx")
    ctx_index = lax.axis_index("ctx")
    tp_index = lax.axis_index("tp")
    spans = 6 // lax.axis_size("tp")
    rows_local = ada_weight.shape[1]
    width = qkv_weight.shape[3]

    kv_full = gather_rows(qkv_weight[:, :, 1:].reshape(2, rows_local, 2 * width))
    q_full = gather_rows(qkv_weight[:, :, 0])
    out_full = gather_rows(jnp.swapaxes(attn_out_weight, 1, 2))
    up_full = gather_rows(mlp_up_weight)
    down_full = gather_rows(jnp.swapaxes(mlp_down_weight, 1, 2))

    live_all = seq_live.astype(F32)
    batch_index = jnp.arange(seq_count, dtype=jnp.int32) % slot_count // per_batch
    marked = (batch_index[:, None] == jnp.arange(MB, dtype=jnp.int32)[None, :]).astype(
        F32
    ) * live_all[:, None]
    members = jnp.sum(marked, axis=0)
    shares = jnp.sum(live_all) / (MB * jnp.maximum(members, 1.0))
    seq_weights = jnp.sum(marked * shares[None, :], axis=1)
    own_weights = lax.dynamic_slice_in_dim(seq_weights, group_index * slot_count, slot_count)
    own_live = lax.dynamic_slice_in_dim(live_all, group_index * slot_count, slot_count)

    cond_float = cond_vector.astype(F32)
    activated = jax.nn.silu(cond_float).astype(BF16)
    ada_local = ada_weight.reshape(2, rows_local, spans, D)
    ada_partial = jnp.einsum("sd,tdke->stke", activated, ada_local, preferred_element_type=F32)
    mod_half = scatter_groups(
        ada_partial.reshape(seq_count // slot_count, slot_count, 2, spans, D)
    ) + ada_bias.reshape(1, 2, spans, D)
    mod_other = swap(mod_half, "tp")
    modulation = jnp.where(
        tp_index == 0,
        jnp.concatenate([mod_half, mod_other], axis=2),
        jnp.concatenate([mod_other, mod_half], axis=2),
    )

    counts = (image_counts, text_counts)
    live_rows = []
    key_bias = []
    for stream in range(2):
        places = jnp.arange(caps[stream], dtype=jnp.int32)
        own_counts = lax.dynamic_slice_in_dim(counts[stream], ctx_index, 1, 1)
        live_rows.append((places[None, :] < own_counts).astype(F32)[:, :, None])
        key_bias.append(
            jnp.where(
                places[None, None, :, None] < counts[stream][:, :, None, None], 0.0, DEAD
            ).astype(F32)
        )
    tokens = (image_tokens, jnp.pad(text_tokens, extra))
    cotangents = (image_cotangent, jnp.pad(text_cotangent, extra))

    def mod_of(stream, which):
        return modulation[:, stream, which][:, None, :]

    def flat(values):
        return values.reshape(-1, values.shape[-1])

    def tall(stream, values):
        return values.reshape(slot_count, caps[stream], values.shape[-1])

    inputs = [part.astype(F32) for part in tokens]
    hidden_in, queries, key_values = [], [], []
    for stream in range(2):
        normed = flat(
            modulate(inputs[stream], mod_of(stream, 0), mod_of(stream, 1)).astype(BF16)
        )
        hidden_in.append(normed)
        value_bias = jnp.concatenate(
            [jnp.zeros((width,), F32), qv_bias[stream, 1].astype(F32)], axis=0
        )
        key_values.append(
            tall(stream, (dot(normed, kv_full[stream]) + value_bias).astype(BF16))
        )
        queries.append(
            tall(stream, (dot(normed, q_full[stream]) + qv_bias[stream, 0]).astype(BF16))
        )

    key_parts = []
    for slot in range(slot_count):
        parts = []
        for stream in range(2):
            if ctx_count == 2:
                other = swap(key_values[stream][slot], "ctx")
                bias = key_bias[stream][slot]
                parts.append(
                    (
                        key_values[stream],
                        lax.dynamic_index_in_dim(bias, ctx_index, 0, keepdims=False),
                        True,
                        stream,
                    )
                )
                parts.append(
                    (
                        other,
                        lax.dynamic_index_in_dim(bias, 1 - ctx_index, 0, keepdims=False),
                        False,
                        stream,
                    )
                )
            else:
                everyone = lax.all_gather(key_values[stream][slot], "ctx", axis=0, tiled=False)
                parts.append((flat(everyone), flat(key_bias[stream][slot]), False, stream))
        key_parts.append(parts)
    outs, logs = [], []
    for slot in range(slot_count):
        out_image, out_text, log_total = attend(slot, queries, key_parts[slot])
        outs.append((out_image, out_text))
        logs.append(log_total)
    attended = [jnp.concatenate([out[stream] for out in outs], axis=0) for stream in range(2)]

    att_values, middles, hidden_mid, pre_acts, activs = [], [], [], [], []
    for stream in range(2):
        att_value = (
            tall(stream, pair_sum(dot_nt(attended[stream], out_full[stream]), "tp"))
            + attn_out_bias[stream]
        )
        middle = inputs[stream] + mod_of(stream, 2) * att_value
        normed = flat(modulate(middle, mod_of(stream, 3), mod_of(stream, 4)).astype(BF16))
        pre_act = dot(normed, up_full[stream]) + mlp_up_bias[stream]
        att_values.append(att_value)
        middles.append(middle)
        hidden_mid.append(normed)
        pre_acts.append(pre_act)
        activs.append(gelu_tanh(pre_act).astype(BF16))

    grad_finals, grad_mlp_low, down_bias_grads, pre_lows, up_bias_grads = [], [], [], [], []
    for stream in range(2):
        grad_final = (
            cotangents[stream].astype(F32) * live_rows[stream] * own_weights[:, None, None]
        )
        grad_mlp = grad_final * mod_of(stream, 5)
        grad_finals.append(grad_final)
        down_bias_grads.append(jnp.sum(flat(grad_mlp), axis=0))
        grad_mlp_low.append(flat(grad_mlp.astype(BF16)))
        grad_act = dot(grad_mlp_low[stream], down_full[stream])
        pre_grad = jax.vjp(gelu_tanh, pre_acts[stream])[1](grad_act)[0]
        up_bias_grads.append(jnp.sum(pre_grad, axis=0))
        pre_lows.append(pre_grad.astype(BF16))
    hid2_sums = [
        tall(stream, pair_sum(dot_nt(pre_lows[stream], up_full[stream]), "tp"))
        for stream in range(2)
    ]
    down_grads = [
        reduce_rows(dot_tn(grad_mlp_low[stream], activs[stream])) for stream in range(2)
    ]
    up_grads = [reduce_rows(dot_tn(hidden_mid[stream], pre_lows[stream])) for stream in range(2)]

    finals, gate2_grads = [], []
    for stream in range(2):
        mlp_value = (
            tall(stream, pair_sum(dot_nt(activs[stream], down_full[stream]), "tp"))
            + mlp_down_bias[stream]
        )
        gate2_grads.append(jnp.sum(grad_finals[stream] * mlp_value, axis=1))
        final = (
            (middles[stream] + mod_of(stream, 5) * mlp_value)
            * live_rows[stream]
            * own_live[:, None, None]
        )
        finals.append(final.astype(BF16))

    grad_middles, mid_mod_grads, gate1_grads, out_bias_grads = [], [], [], []
    out_grads, grad_attended = [], []
    for stream in range(2):
        back, shift_grad, scale_grad = modulate_back(
            middles[stream], mod_of(stream, 4), hid2_sums[stream]
        )
        grad_middle = grad_finals[stream] + back
        grad_middles.append(grad_middle)
        mid_mod_grads.append((shift_grad, scale_grad))
        gate1_grads.append(jnp.sum(grad_middle * att_values[stream], axis=1))
        grad_att = grad_middle * mod_of(stream, 2)
        out_bias_grads.append(jnp.sum(flat(grad_att), axis=0))
        grad_att_low = flat(grad_att.astype(BF16))
        grad_attended.append(tall(stream, dot(grad_att_low, out_full[stream]).astype(BF16)))
        out_grads.append(reduce_rows(dot_tn(grad_att_low, attended[stream])))

    query_grads, pair_grads = ([], []), ([], [])
    bias_sums = 0.0
    for slot in range(slot_count):
        results = attend_back(
            slot, queries, outs[slot], grad_attended, logs[slot], key_parts[slot]
        )
        bias_sums = bias_sums + jnp.stack(
            [jnp.swapaxes(part, 0, 1).reshape(2, width) for part in results[2:4]], axis=1
        )
        for stream in range(2):
            query_grads[stream].append(results[stream])
            if ctx_count == 2:
                mine, given = results[4 + 2 * stream], results[5 + 2 * stream]
                total = mine.astype(F32) + swap(given, "ctx").astype(F32)
            else:
                total = lax.psum_scatter(
                    results[4 + stream], "ctx", scatter_dimension=1, tiled=True
                ).astype(F32)
            pair_grads[stream].append(
                jnp.concatenate([total[0].astype(BF16), total[1].astype(BF16)], axis=1)
            )

    input_grads, mod_rows, q_weight_grads, kv_weight_grads = [], [], [], []
    for stream in range(2):
        query_grad = jnp.concatenate(query_grads[stream], axis=0)
        pair_grad = jnp.concatenate(pair_grads[stream], axis=0)
        hid_sum = tall(
            stream,
            pair_sum(
                dot_nt(query_grad, q_full[stream]) + dot_nt(pair_grad, kv_full[stream]), "tp"
            ),
        )
        q_weight_grads.append(reduce_rows(dot_tn(hidden_in[stream], query_grad)))
        kv_weight_grads.append(reduce_rows(dot_tn(hidden_in[stream], pair_grad)))
        back, shift_grad, scale_grad = modulate_back(inputs[stream], mod_of(stream, 1), hid_sum)
        input_grads.append((grad_middles[stream] + back).astype(BF16))
        mod_rows.append(
            jnp.stack(
                [
                    shift_grad,
                    scale_grad,
                    gate1_grads[stream],
                    mid_mod_grads[stream][0],
                    mid_mod_grads[stream][1],
                    gate2_grads[stream],
                ],
                axis=1,
            )
        )

    mod_grads = jnp.stack(mod_rows, axis=1)
    mod_half_grads = lax.dynamic_slice_in_dim(mod_grads, tp_index * spans, spans, 2)
    pieces = (
        mod_half_grads,
        bias_sums,
        jnp.stack(up_bias_grads, axis=0),
        jnp.stack(out_bias_grads, axis=0),
        jnp.stack(down_bias_grads, axis=0),
    )
    row = ctx_sum(jnp.concatenate([piece.reshape(-1) for piece in pieces], axis=0))
    everyone = lax.all_gather(row[None].astype(BF16), FSDP, axis=0, tiled=True).astype(F32)
    ends = []
    base = 0
    for piece in pieces:
        ends.append(everyone[:, base : base + piece.size].reshape((-1,) + piece.shape))
        base += piece.size
    mod_all = ends[0].reshape(seq_count, 2, spans, D)
    qv_bias_grad, up_bias_grad, out_bias_grad, down_bias_grad = [
        jnp.sum(part, axis=0) for part in ends[1:]
    ]
    ada_bias_grad = jnp.sum(mod_all, axis=0).reshape(2, spans * D)
    mod_low = mod_all.astype(BF16)
    ada_weight_grad = jnp.einsum(
        "sd,stke->tdke", activated, mod_low, preferred_element_type=F32
    ).reshape(2, rows_local, spans * D)
    silu_part = jnp.einsum("stke,tdke->sd", mod_low, ada_local, preferred_element_type=F32)
    cond_grad = jax.vjp(jax.nn.silu, cond_float)[1](pair_sum(silu_part, "tp"))[0]
    qkv_grad = jnp.stack(
        [
            jnp.concatenate(
                [q_weight_grads[stream][:, None], kv_weight_grads[stream].reshape(-1, 2, width)],
                axis=1,
            )
            for stream in range(2)
        ],
        axis=0,
    )
    return (
        finals[0],
        finals[1][:, :cap_text],
        input_grads[0],
        input_grads[1][:, :cap_text],
        cond_grad,
        ada_weight_grad,
        ada_bias_grad,
        qkv_grad,
        qv_bias_grad,
        jnp.stack([part.T for part in out_grads], axis=0),
        out_bias_grad,
        jnp.stack(up_grads, axis=0),
        up_bias_grad,
        jnp.stack([part.T for part in down_grads], axis=0),
        down_bias_grad,
    )


def solution(mesh):
    fsdp, ctx, tp = (mesh.shape[name] for name in ("fsdp", "ctx", "tp"))
    split = Mesh(mesh.devices.reshape(fsdp // 2, 2, ctx, tp), ("z", "core", "ctx", "tp"))
    rows = P(FSDP, "ctx", None)
    inner = P(None, FSDP, "tp")
    outer = P(None, "tp", FSDP)
    return jax.shard_map(
        on_device,
        mesh=split,
        in_specs=(
            rows,
            rows,
            P(None, FSDP),
            rows,
            rows,
            P(FSDP, None),
            P(FSDP, None),
            P(),
            inner,
            P(None, "tp"),
            P(None, FSDP, None, "tp"),
            P(None, None, "tp"),
            outer,
            P(),
            inner,
            P(None, "tp"),
            outer,
            P(),
        ),
        out_specs=(
            rows,
            rows,
            rows,
            rows,
            P(None, FSDP),
            inner,
            P(None, "tp"),
            P(None, FSDP, None, "tp"),
            P(None, None, "tp"),
            outer,
            P(),
            inner,
            P(None, "tp"),
            outer,
            P(),
        ),
        check_vma=False,
    )
```

time: 3160 us -> 1420 us (0.45)
  waiting for transfers between devices: 1940 us -> 791 us
  matrix products: 585 us -> 253 us
  other arithmetic: 342 us -> 112 us
  Pallas kernels: 0 us -> 109 us
  local copies, waits for them, and re-layouts: 182 us -> 76.5 us
  blocking collectives: 86.4 us -> 18.1 us
  starting transfers between devices: 3.5 us -> 39 us
    reduce_scatter x18 -> x10, waiting for transfers between devices: 957 us -> 190 us  [reduce_rows(): lax.psum_scatter(part.astype(BF16), FSDP, scatter_dimension=0, tiled=True)]
    psum x6 -> x0, waiting for transfers between devices: 494 us -> none  [the longest x4 399 us: tensor_sum(): lax.psum(shortened(parts), 'tp')]
    ppermute x0 -> x33, waiting for transfers between devices: none -> 449 us  [the longest x30 444 us: swap(): return lax.ppermute(values, axis, PAIR)]
    dot_general x62 -> x32, matrix products: 581 us -> 249 us  [the longest x10 86.5 us: dot_tn(): lax.dot_general(left, right, (((0,), (0,)), ((), ())), preferred_element_...]
    all_gather x8 -> x5, waiting for transfers between devices: 433 us -> 151 us  [gather_rows(): whole = lax.all_gather(piece, ('ctx',) + FSDP, axis=0, tiled=True)]
    pallas_call x0 -> x4, Pallas kernels: none -> 109 us  [the longest x2 72.1 us: attend_back(): pl.pallas_call(functools.partial(attend_back_kernel, tuple((part[3] for p...]
    reduce_sum x48 -> x21, other arithmetic: 142 us -> 59.8 us  [the longest x4 17.6 us: modulate_back(): first = jnp.mean(unit_grad, axis=-1, keepdims=True)]
    convert_element_type x18 -> x19, other arithmetic: 91.5 us -> 23.4 us  [the longest x2 10.5 us: on_device(): input_grads.append((grad_middles[stream] + back).astype(BF16))]
  transfers between devices with their start and end apart: 33 -> 48, of which waited for: 25 -> 25; matrix products, arithmetic and copies ran while one was open for 22% -> 28% of each run, Pallas kernels for 0% -> 8%
where the time goes in v1:
time: 1420 us
  waiting for transfers between devices  791 us (56%)
  matrix products  253 us (18%)
  other arithmetic  112 us (8%)
  Pallas kernels  109 us (8%)
  local copies, waits for them, and re-layouts  76.5 us (5%)
  starting transfers between devices  39 us (3%)
  blocking collectives  18.1 us (1%)
  between operations  17.1 us (1%)
    ppermute x30, waiting for transfers between devices, swap(): return lax.ppermute(values, axis, PAIR)  444 us
    reduce_scatter x10, waiting for transfers between devices, reduce_rows(): lax.psum_scatter(part.astype(BF16), FSDP, scatter_dimension=0, tiled=True)  190 us
    all_gather x5, waiting for transfers between devices, gather_rows(): whole = lax.all_gather(piece, ('ctx',) + FSDP, axis=0, tiled=True)  151 us
    dot_general x10, matrix products, dot_tn(): lax.dot_general(left, right, (((0,), (0,)), ((), ())), preferred_element_...  86.5 us
    dot_general x10, matrix products, dot(): lax.dot_general(left, right, (((1,), (0,)), ((), ())), preferred_element_...  83 us
    dot_general x10, matrix products, dot_nt(): lax.dot_general(left, right, (((1,), (1,)), ((), ())), preferred_element_...  72.8 us
    pallas_call x2, Pallas kernels, attend_back(): pl.pallas_call(functools.partial(attend_back_kernel, tuple((part[3] for p...  72.1 us
    pallas_call x2, Pallas kernels, attend(): pl.pallas_call(functools.partial(attend_kernel, len(key_parts), image_row...  36.6 us
  transfers between devices with their start and end apart: 48, of which 25 were waited for; matrix products, arithmetic and copies ran while one was open for 28% of the time, Pallas kernels for 8%

profile of v1, /device:TPU:0, one launch (start us, length us, event | category | flops | bytes accessed | tf_op | source)
XLA Modules:
  0.0 1415.3 jit_solution(8029818910318555993)
XLA Ops:
  17.4 5.9 reshape.511
  58.3 39.0 %all-gather.14.cloned.1.call-done = bf16[1,3072,1536]{2,1,0:T(8,128)(2,1)} async-done(((bf16[1,192,1536]{2,1,0:T(8,128)(2,1)}), bf16[1,3072,1536]{2,1,0:T(8,128)(2,1)}) %all-gather.14.cloned.1.call-update) | async-done | bytes 9437200 | tf_op jit(solution)/shard_map/all_gather | solution.py:53
  97.3 8.6 fusion.20
  109.4 57.2 %all-gather.12.cloned.1.call-done = bf16[1,3072,1,768]{3,1,2,0:T(8,128)(2,1)} async-done(((bf16[1,192,1,768]{3,1,2,0:T(8,128)(2,1)}), bf16[1,3072,1,768]{3,1,2,0:T(8,128)(2,1)}) %all-gather.12.cloned.1.call-update) | async-done | bytes 4718608 | tf_op jit(solution)/shard_map/all_gather | solution.py:53
  166.5 5.7 fusion.48
  179.7 8.8 collective-permute-done.6.refs_5_.refs_9_.refs_10_.refs_14_
  188.5 18.2 %attend.2 = (bf16[576,768]{1,0:T(8,128)(2,1)S(1)}, bf16[96,768]{1,0:T(8,128)(2,1)S(1)}, f32[6,1,1344]{2,1,0:T(1,128)S(1)}) custom-call(bf16[2,576,768]{2,1,0:T(8,128)(2,1)S(1)} %bitcast.321, bf16[2,96,768]{2,1,0:T(8,128)(2,1)S(1)} %bitcast.325, bf16[2,576,1536]{2,1,0:T(8,128)(2,1)} %bitcast.358, ...), custom_call_target="tpu_custom_call" | custom-call | flops 22196256768 | bytes 5898240 | tf_op jit(solution)/shard_map/attend/pallas_call | solution.py:243
  208.1 37.1 %collective-permute-done.7.refs_3_.refs_7_.refs_8_.refs_12_ = bf16[576,1536]{1,0:T(8,128)(2,1)S(1)} collective-permute-done((bf16[576,1536]{1,0:T(8,128)(2,1)S(1)}, bf16[576,1536]{1,0:T(8,128)(2,1)S(1)}, u32[]{:S(2)}, u32[]{:S(2)}) %collective-permute-start.7) | collective-permute-done | bytes 1769504 | tf_op jit(solution)/shard_map/ppermute | solution.py:23
  246.4 18.4 %attend.3 = (bf16[576,768]{1,0:T(8,128)(2,1)S(1)}, bf16[96,768]{1,0:T(8,128)(2,1)S(1)}, f32[6,1,1344]{2,1,0:T(1,128)S(1)}) custom-call(bf16[2,576,768]{2,1,0:T(8,128)(2,1)S(1)} %bitcast.322, bf16[2,96,768]{2,1,0:T(8,128)(2,1)S(1)} %bitcast.326, bf16[2,576,1536]{2,1,0:T(8,128)(2,1)} %bitcast.360, bf16[576,1536]{1,0:T(8,128)(2,1)} %copy-done.176, ...), custom_call_target="tpu_custom_call" | custom-call | flops 22196256768 | bytes 5898240 | tf_op jit(solution)/shard_map/attend/pallas_call | solution.py:243
  266.8 5.3 convolution_convert_fusion.6
  278.2 85.0 %collective-permute-done.11 = bf16[192,1536]{1,0:T(8,128)(2,1)S(1)} collective-permute-done((bf16[192,1536]{1,0:T(8,128)(2,1)S(1)}, bf16[192,1536]{1,0:T(8,128)(2,1)S(1)}, u32[]{:S(2)}, u32[]{:S(2)}) %collective-permute-start.11) | collective-permute-done | bytes 589856 | tf_op jit(solution)/shard_map/ppermute | solution.py:23
  374.4 7.3 fusion.40
  381.7 55.3 %all-gather.20.cloned.1.call-done = bf16[1,3072,3072]{2,1,0:T(8,128)(2,1)} async-done(((bf16[1,192,3072]{2,1,0:T(8,128)(2,1)}), bf16[1,3072,3072]{2,1,0:T(8,128)(2,1)}) %all-gather.20.cloned.1.call-update) | async-done | bytes 18874384 | tf_op jit(solution)/shard_map/all_gather | solution.py:53
  436.9 7.9 fusion.52
  446.4 17.0 %convolution_add_fusion = f32[1152,3072]{1,0:T(8,128)} fusion(bf16[1152,1536]{1,0:T(8,128)(2,1)S(1)} %bitcast.357, bf16[1,3072,3072]{2,1,0:T(8,128)(2,1)} %all-gather.18.cloned.1.call-done, f32[3072]{0:T(1024)S(1)} %bitcast.404), kind=kOutput, calls=%fused_computation.9 | convolution fusion | flops 10875174912 | bytes 27144192 | tf_op jit(solution)/shard_map/dot_general | solution.py:38
  463.4 23.8 %fusion.123 = (bf16[3072]{0:T(1024)(128)(2,1)}, bf16[1152,3072]{1,0:T(8,128)(2,1)S(1)}) fusion(f32[1152,3072]{1,0:T(8,128)} %convolution_add_fusion, bf16[1152,1536]{1,0:T(8,128)(2,1)S(1)} %bitcast.374, bf16[1,3072,3072]{2,1,0:T(8,128)(2,1)} %all-gather.20.cloned.1.call-done), kind=kOutput, calls=%fused_computation.345 | convolution fusion | flops 10945950720 | bytes 34215936 | tf_op jit(solution)/shard_map/dot_general | solution.py:38
  487.2 17.3 %fusion.22 = bf16[1152,1536]{1,0:T(8,128)(2,1)} fusion(bf16[1,3072,3072]{2,1,0:T(8,128)(2,1)} %all-gather.18.cloned.1.call-done, bf16[1152,3072]{1,0:T(8,128)(2,1)S(1)} %get-tuple-element.157), kind=kOutput, calls=%fused_computation.42 | convolution fusion | flops 10873405440 | bytes 20054016 | tf_op jit(solution)/shard_map/dot_general | solution.py:42
  507.3 7.9 fusion.122
  520.8 19.7 %fusion.21 = bf16[1152,1536]{1,0:T(8,128)(2,1)} fusion(bf16[1,3072,3072]{2,1,0:T(8,128)(2,1)} %all-gather.20.cloned.1.call-done, f32[1152,3072]{1,0:T(8,128)} %convolution_add_fusion), kind=kOutput, calls=%fused_computation.41 | convolution fusion | flops 10905255936 | bytes 27131904 | tf_op jit(solution)/shard_map/dot_general | solution.py:42
  541.2 55.6 %collective-permute-done.14 = bf16[192,1536]{1,0:T(8,128)(2,1)S(1)} collective-permute-done((bf16[192,1536]{1,0:T(8,128)(2,1)S(1)}, bf16[192,1536]{1,0:T(8,128)(2,1)S(1)}, u32[]{:S(2)}, u32[]{:S(2)}) %collective-permute-start.14) | collective-permute-done | bytes 589856 | tf_op jit(solution)/shard_map/ppermute | solution.py:23
  609.6 7.4 fusion.33
  617.0 7.1 multiply_reduce_fusion.1
  624.2 47.5 %collective-permute-done.10 = bf16[1152,1536]{1,0:T(8,128)(2,1)} collective-permute-done((bf16[1152,1536]{1,0:T(8,128)(2,1)}, bf16[1152,1536]{1,0:T(8,128)(2,1)}, u32[]{:S(2)}, u32[]{:S(2)}) %collective-permute-start.10) | collective-permute-done | bytes 3538976 | tf_op jit(solution)/shard_map/ppermute | solution.py:23
  675.8 13.7 fusion.35
  692.5 5.8 convolution_convert_fusion.11
  698.4 36.0 %attend_back.2 = (bf16[576,768]{1,0:T(8,128)(2,1)S(1)}, bf16[96,768]{1,0:T(8,128)(2,1)S(1)}, f32[6,2,128]{2,1,0:T(2,128)S(1)}, f32[6,2,128]{2,1,0:T(2,128)S(1)},...) custom-call(bf16[2,576,768]{2,1,0:T(8,128)(2,1)} %bitcast.323, ...), custom_call_target="tpu_custom_call" | custom-call | flops 55490641920 | bytes 11796480 | tf_op jit(solution)/shard_map/attend_back/pallas_call | solution.py:283
  736.2 6.2 convolution_convert_fusion.8
  745.2 36.1 %attend_back.3 = (bf16[576,768]{1,0:T(8,128)(2,1)S(1)}, bf16[96,768]{1,0:T(8,128)(2,1)S(1)}, f32[6,2,128]{2,1,0:T(2,128)S(1)}, f32[6,2,128]{2,1,0:T(2,128)S(1)},...) custom-call(bf16[2,576,768]{2,1,0:T(8,128)(2,1)} %bitcast.324, ...), custom_call_target="tpu_custom_call" | custom-call | flops 55490641920 | bytes 11796480 | tf_op jit(solution)/shard_map/attend_back/pallas_call | solution.py:283
  792.4 7.9 collective-permute-done.19
  811.4 39.7 %collective-permute-done.16 = bf16[2,576,768]{2,1,0:T(8,128)(2,1)S(1)} collective-permute-done((bf16[2,576,768]{2,1,0:T(8,128)(2,1)}, bf16[2,576,768]{2,1,0:T(8,128)(2,1)S(1)}, u32[]{:S(2)}, u32[]{:S(2)}) %collective-permute-start.16) | collective-permute-done | bytes 1769504 | tf_op jit(solution)/shard_map/ppermute | solution.py:23
  851.7 34.6 %collective-permute-done.15 = bf16[2,576,768]{2,1,0:T(8,128)(2,1)S(1)} collective-permute-done((bf16[2,576,768]{2,1,0:T(8,128)(2,1)}, bf16[2,576,768]{2,1,0:T(8,128)(2,1)S(1)}, u32[]{:S(2)}, u32[]{:S(2)}) %collective-permute-start.15) | collective-permute-done | bytes 1769504 | tf_op jit(solution)/shard_map/ppermute | solution.py:23
  889.0 18.7 %convolution_convert_fusion.5 = bf16[1536,1536]{1,0:T(8,128)(2,1)} fusion(bf16[1152,1536]{1,0:T(8,128)(2,1)S(1)} %bitcast.372, bf16[576,768]{1,0:T(8,128)(2,1)S(1)} %get-tuple-element.111, bf16[576,768]{1,0:T(8,128)(2,1)S(1)} %get-tuple-element.110, bf16[576,768]{1,0:T(8,128)(2,1)S(1)} %get-tuple-element.109, bf16[576,768]{1,0:T(8,128)(2,1)S(1)} %get-tuple-element.108), kind=kOutput, calls=%fused_computation.39 | convolution fusion | flops 5452333056 | bytes 11796480 | tf_op jit(solution)/shard_map/dot_general | solution.py:46
  907.8 19.9 %convolution_convert_fusion.1 = bf16[1536,3072]{1,0:T(8,128)(2,1)} fusion(bf16[1152,1536]{1,0:T(8,128)(2,1)} %bitcast.373, f32[1152,3072]{1,0:T(8,128)} %convolution_add_fusion), kind=kOutput, calls=%fused_computation.11 | convolution fusion | flops 10908205056 | bytes 27131904 | tf_op jit(solution)/shard_map/dot_general | solution.py:46
  927.8 18.3 %convolution_convert_fusion.3 = bf16[1536,3072]{1,0:T(8,128)(2,1)} fusion(bf16[1152,1536]{1,0:T(8,128)(2,1)} %bitcast.356, bf16[1152,3072]{1,0:T(8,128)(2,1)} %copy-done.180), kind=kOutput, calls=%fused_computation.13 | convolution fusion | flops 10876354560 | bytes 20054016 | tf_op jit(solution)/shard_map/dot_general | solution.py:46
  948.0 5.2 convolution_convert_fusion
  954.7 5.4 convolution_convert_fusion.2
  967.6 8.3 fusion.37
  976.0 4.7 fusion.19
  989.1 80.7 %collective-permute-done.20 = bf16[192,1536]{1,0:T(8,128)(2,1)S(1)} collective-permute-done((bf16[192,1536]{1,0:T(8,128)(2,1)S(1)}, bf16[192,1536]{1,0:T(8,128)(2,1)S(1)}, u32[]{:S(2)}, u32[]{:S(2)}) %collective-permute-start.20) | collective-permute-done | bytes 589856 | tf_op jit(solution)/shard_map/ppermute | solution.py:23
  1100.8 7.3 fusion.32
  1110.1 5.0 fusion.30
  1126.7 7.8 fusion.29
  1134.6 18.1 %all-gather.5 = bf16[270336]{0:T(1024)(128)(2,1)S(1)} all-gather(bf16[33792]{0:T(1024)(128)(2,1)S(1)} %add_convert_fusion.7), channel_id=7, replica_groups=mesh['z'=4,'core'=2,'ctx'=2,'tp'=2] {'z','core'}, dimensions={0}, use_global_device_ids=true | all-gather | bytes 608256 | tf_op jit(solution)/shard_map/all_gather | solution.py:586
  1165.1 6.6 copy.189
  1180.8 8.0 collective-permute-done.24
  1192.3 87.1 %reduce-scatter.29.cloned.1.call-done = bf16[192,3072]{1,0:T(8,128)(2,1)} async-done(((bf16[1536,3072]{1,0:T(8,128)(2,1)}), bf16[192,3072]{1,0:T(8,128)(2,1)}) %reduce-scatter.29.cloned.1.call-update) | async-done | bytes 1179664 | tf_op jit(solution)/shard_map/reduce_scatter | solution.py:59
  1280.9 98.6 %reduce-scatter.25.cloned.1.call-done = bf16[192,3072]{1,0:T(8,128)(2,1)} async-done(((bf16[1536,3072]{1,0:T(8,128)(2,1)}), bf16[192,3072]{1,0:T(8,128)(2,1)}) %reduce-scatter.25.cloned.1.call-update) | async-done | bytes 1179664 | tf_op jit(solution)/shard_map/reduce_scatter | solution.py:59
  1388.6 16.6 %collective-permute-done.30 = bf16[192,3072]{1,0:T(8,128)(2,1)S(1)} collective-permute-done((bf16[192,3072]{1,0:T(8,128)(2,1)}, bf16[192,3072]{1,0:T(8,128)(2,1)S(1)}, u32[]{:S(2)}, u32[]{:S(2)}) %collective-permute-start.30) | collective-permute-done | bytes 1179680 | tf_op jit(solution)/shard_map/ppermute | solution.py:23
  (681 shorter events, 238.9 us)
Async XLA Ops:
  7.2 90.1 %all-gather.14.cloned.1.call-start = ((), (), s32[]{:S(2)}) async-start(), calls=%async_computation.21 | async-start | bytes 10027008 | tf_op jit(solution)/shard_map/all_gather | solution.py:53
  9.7 156.8 %all-gather.12.cloned.1.call-start = ((), (), s32[]{:S(2)}) async-start(), calls=%async_computation.20 | async-start | bytes 5013504 | tf_op jit(solution)/shard_map/all_gather | solution.py:53
  11.7 255.1 %all-gather.16.cloned.1.call-start = ((), (), s32[]{:S(2)}) async-start(), calls=%async_computation.22 | async-start | bytes 5013504 | tf_op jit(solution)/shard_map/all_gather | solution.py:53
  13.4 361.0 %all-gather.18.cloned.1.call-start = ((), (), s32[]{:S(2)}) async-start(), calls=%async_computation.23 | async-start | bytes 20054016 | tf_op jit(solution)/shard_map/all_gather | solution.py:53
  14.7 422.3 %all-gather.20.cloned.1.call-start = ((), (), s32[]{:S(2)}) async-start(), calls=%async_computation.24 | async-start | bytes 20054016 | tf_op jit(solution)/shard_map/all_gather | solution.py:53
  17.3 1057.7 %reduce-scatter.21.cloned.1.call-start = ((), (), s32[]{:S(2)}) async-start(), calls=%async_computation.15 | async-start | bytes 2654208 | tf_op jit(solution)/shard_map/reduce_scatter | solution.py:59
  26.8 10.1 collective-permute-start
  37.4 9.4 collective-permute-start.1
  40.1 9.6 collective-permute-start.2
  42.7 7.0 collective-permute-start.3
  49.8 4.4 collective-permute-start.4
  108.8 79.7 %collective-permute-start.5 = (bf16[576,1536]{1,0:T(8,128)(2,1)}, bf16[576,1536]{1,0:T(8,128)(2,1)}, u32[]{:S(2)}, u32[]{:S(2)}) collective-permute-start(bf16[576,1536]{1,0:T(8,128)(2,1)} %get-tuple-element.107), channel_id=1, source_target_pairs={{0,2},{2,0},{1,3},{3,1},{4,6},{6,4},{5,7},{7,5},{8,10},{10,8},{9,1... | collective-permute-start | bytes 5308424 | tf_op jit(solution)/shard_map/ppermute | solution.py:23
  176.4 12.1 collective-permute-start.6
  177.6 30.2 %collective-permute-start.8 = (bf16[96,1536]{1,0:T(8,128)(2,1)S(1)}, bf16[96,1536]{1,0:T(8,128)(2,1)S(1)}, u32[]{:S(2)}, u32[]{:S(2)}) collective-permute-start(bf16[96,1536]{1,0:T(8,128)(2,1)S(1)} %get-tuple-element.116), channel_id=1, source_target_pairs={{0,2},{2,0},{1,3},{3,1},{4,6},{6,4},{5,7},{7,5},{8,10},{10,8},{9,1... | collective-permute-start | bytes 884744 | tf_op jit(solution)/shard_map/ppermute | solution.py:23
  179.2 65.9 %collective-permute-start.7 = (bf16[576,1536]{1,0:T(8,128)(2,1)S(1)}, bf16[576,1536]{1,0:T(8,128)(2,1)S(1)}, u32[]{:S(2)}, u32[]{:S(2)}) collective-permute-start(bf16[576,1536]{1,0:T(8,128)(2,1)S(1)} %copy-done.74), channel_id=1, source_target_pairs={{0,2},{2,0},{1,3},{3,1},{4,6},{6,4},{5,7},{7,5},{8,10},{10,8},{9,1... | collective-permute-start | bytes 5308424 | tf_op jit(solution)/shard_map/ppermute | solution.py:23
  272.1 92.3 %collective-permute-start.9 = (bf16[1152,1536]{1,0:T(8,128)(2,1)S(1)}, bf16[1152,1536]{1,0:T(8,128)(2,1)S(1)}, u32[]{:S(2)}, u32[]{:S(2)}) collective-permute-start(bf16[1152,1536]{1,0:T(8,128)(2,1)S(1)} %convolution_convert_fusion.6), channel_id=1, source_target_pairs={{0,1},{1,0},{2,3},{3,2},{4,5},{5,4},{6,7},{7,6},{8,9},{9,8},{10,11... | collective-permute-start | bytes 10616840 | tf_op jit(solution)/shard_map/ppermute | solution.py:23
  274.7 88.6 %collective-permute-start.11 = (bf16[192,1536]{1,0:T(8,128)(2,1)S(1)}, bf16[192,1536]{1,0:T(8,128)(2,1)S(1)}, u32[]{:S(2)}, u32[]{:S(2)}) collective-permute-start(bf16[192,1536]{1,0:T(8,128)(2,1)S(1)} %convolution_convert_fusion.12), channel_id=1, source_target_pairs={{0,1},{1,0},{2,3},{3,2},{4,5},{5,4},{6,7},{7,6},{8,9},{9,8},{10,11... | collective-permute-start | bytes 1769480 | tf_op jit(solution)/shard_map/ppermute | solution.py:23
  444.9 60.2 %collective-permute-start.12 = (bf16[192,1536]{1,0:T(8,128)(2,1)S(1)}, bf16[192,1536]{1,0:T(8,128)(2,1)S(1)}, u32[]{:S(2)}, u32[]{:S(2)}) collective-permute-start(bf16[192,1536]{1,0:T(8,128)(2,1)S(1)} %fusion.52), channel_id=1, source_target_pairs={{0,1},{1,0},{2,3},{3,2},{4,5},{5,4},{6,7},{7,6},{8,9},{9,8},{10,11... | collective-permute-start | bytes 1769480 | tf_op jit(solution)/shard_map/ppermute | solution.py:23
  504.4 105.1 %collective-permute-start.13 = (bf16[1152,1536]{1,0:T(8,128)(2,1)}, bf16[1152,1536]{1,0:T(8,128)(2,1)}, u32[]{:S(2)}, u32[]{:S(2)}) collective-permute-start(bf16[1152,1536]{1,0:T(8,128)(2,1)} %fusion.22), channel_id=1, source_target_pairs={{0,1},{1,0},{2,3},{3,2},{4,5},{5,4},{6,7},{7,6},{8,9},{9,8},{10,11... | collective-permute-start | bytes 10616840 | tf_op jit(solution)/shard_map/ppermute | solution.py:23
  519.2 77.5 %collective-permute-start.14 = (bf16[192,1536]{1,0:T(8,128)(2,1)S(1)}, bf16[192,1536]{1,0:T(8,128)(2,1)S(1)}, u32[]{:S(2)}, u32[]{:S(2)}) collective-permute-start(bf16[192,1536]{1,0:T(8,128)(2,1)S(1)} %fusion.53), channel_id=1, source_target_pairs={{0,1},{1,0},{2,3},{3,2},{4,5},{5,4},{6,7},{7,6},{8,9},{9,8},{10,11... | collective-permute-start | bytes 1769480 | tf_op jit(solution)/shard_map/ppermute | solution.py:23
  540.6 131.1 %collective-permute-start.10 = (bf16[1152,1536]{1,0:T(8,128)(2,1)}, bf16[1152,1536]{1,0:T(8,128)(2,1)}, u32[]{:S(2)}, u32[]{:S(2)}) collective-permute-start(bf16[1152,1536]{1,0:T(8,128)(2,1)} %fusion.21), channel_id=1, source_target_pairs={{0,1},{1,0},{2,3},{3,2},{4,5},{5,4},{6,7},{7,6},{8,9},{9,8},{10,11... | collective-permute-start | bytes 10616840 | tf_op jit(solution)/shard_map/ppermute | solution.py:23
  607.2 469.3 %reduce-scatter.19.cloned.1.call-start = ((), (), s32[]{:S(2)}) async-start(), calls=%async_computation.14 | async-start | bytes 2654208 | tf_op jit(solution)/shard_map/reduce_scatter | solution.py:59
  742.4 342.8 %reduce-scatter.11.cloned.1.call-start = ((), (), s32[]{:S(2)}) async-start(), calls=%async_computation.10 | async-start | bytes 2654208 | tf_op jit(solution)/shard_map/reduce_scatter | solution.py:59
  787.9 298.9 %reduce-scatter.15.cloned.1.call-start = ((), (), s32[]{:S(2)}) async-start(), calls=%async_computation.12 | async-start | bytes 2654208 | tf_op jit(solution)/shard_map/reduce_scatter | solution.py:59
  790.3 366.6 %reduce-scatter.17.cloned.1.call-start = ((), (), s32[]{:S(2)}) async-start(), calls=%async_computation.13 | async-start | bytes 5308416 | tf_op jit(solution)/shard_map/reduce_scatter | solution.py:59
  790.3 10.0 collective-permute-start.19
  791.7 13.1 collective-permute-start.18
  809.2 363.1 %reduce-scatter.13.cloned.1.call-start = ((), (), s32[]{:S(2)}) async-start(), calls=%async_computation.11 | async-start | bytes 5308416 | tf_op jit(solution)/shard_map/reduce_scatter | solution.py:59
  809.3 41.8 %collective-permute-start.16 = (bf16[2,576,768]{2,1,0:T(8,128)(2,1)}, bf16[2,576,768]{2,1,0:T(8,128)(2,1)S(1)}, u32[]{:S(2)}, u32[]{:S(2)}) collective-permute-start(bf16[2,576,768]{2,1,0:T(8,128)(2,1)} %get-tuple-element.48), channel_id=1, source_target_pairs={{0,2},{2,0},{1,3},{3,1},{4,6},{6,4},{5,7},{7,5},{8,10},{10,8},{9,1... | collective-permute-start | bytes 5308424 | tf_op jit(solution)/shard_map/ppermute | solution.py:23
  810.6 75.7 %collective-permute-start.15 = (bf16[2,576,768]{2,1,0:T(8,128)(2,1)}, bf16[2,576,768]{2,1,0:T(8,128)(2,1)S(1)}, u32[]{:S(2)}, u32[]{:S(2)}) collective-permute-start(bf16[2,576,768]{2,1,0:T(8,128)(2,1)} %get-tuple-element.46), channel_id=1, source_target_pairs={{0,2},{2,0},{1,3},{3,1},{4,6},{6,4},{5,7},{7,5},{8,10},{10,8},{9,1... | collective-permute-start | bytes 5308424 | tf_op jit(solution)/shard_map/ppermute | solution.py:23
  907.7 265.8 %reduce-scatter.27.cloned.1.call-start = ((), (), s32[]{:S(2)}) async-start(), calls=%async_computation.18 | async-start | bytes 10616832 | tf_op jit(solution)/shard_map/reduce_scatter | solution.py:59
  927.7 251.6 %reduce-scatter.23.cloned.1.call-start = ((), (), s32[]{:S(2)}) async-start(), calls=%async_computation.16 | async-start | bytes 10616832 | tf_op jit(solution)/shard_map/reduce_scatter | solution.py:59
  946.2 333.3 %reduce-scatter.29.cloned.1.call-start = ((), (), s32[]{:S(2)}) async-start(), calls=%async_computation.19 | async-start | bytes 10616832 | tf_op jit(solution)/shard_map/reduce_scatter | solution.py:59
  953.3 426.2 %reduce-scatter.25.cloned.1.call-start = ((), (), s32[]{:S(2)}) async-start(), calls=%async_computation.17 | async-start | bytes 10616832 | tf_op jit(solution)/shard_map/reduce_scatter | solution.py:59
  980.9 119.9 %collective-permute-start.17 = (bf16[1152,1536]{1,0:T(8,128)(2,1)}, bf16[1152,1536]{1,0:T(8,128)(2,1)}, u32[]{:S(2)}, u32[]{:S(2)}) collective-permute-start(bf16[1152,1536]{1,0:T(8,128)(2,1)} %fusion.19), channel_id=1, source_target_pairs={{0,1},{1,0},{2,3},{3,2},{4,5},{5,4},{6,7},{7,6},{8,9},{9,8},{10,11... | collective-permute-start | bytes 10616840 | tf_op jit(solution)/shard_map/ppermute | solution.py:23
  982.4 87.4 %collective-permute-start.20 = (bf16[192,1536]{1,0:T(8,128)(2,1)S(1)}, bf16[192,1536]{1,0:T(8,128)(2,1)S(1)}, u32[]{:S(2)}, u32[]{:S(2)}) collective-permute-start(bf16[192,1536]{1,0:T(8,128)(2,1)S(1)} %fusion.50), channel_id=1, source_target_pairs={{0,1},{1,0},{2,3},{3,2},{4,5},{5,4},{6,7},{7,6},{8,9},{9,8},{10,11... | collective-permute-start | bytes 1769480 | tf_op jit(solution)/shard_map/ppermute | solution.py:23
  1074.9 10.2 collective-permute-start.28
  1076.5 15.0 %collective-permute-start.27 = (bf16[192,768]{1,0:T(8,128)(2,1)}, bf16[192,768]{1,0:T(8,128)(2,1)S(1)}, u32[]{:S(2)}, u32[]{:S(2)}) collective-permute-start(bf16[192,768]{1,0:T(8,128)(2,1)} %reduce-scatter.19.cloned.1.call-done), channel_id=1, source_target_pairs={{0,2},{2,0},{1,3},{3,1},{4,6},{6,4},{5,7},{7,5},{8,10},{10,8},{9,1... | collective-permute-start | bytes 884744 | tf_op jit(solution)/shard_map/ppermute | solution.py:23
  1085.3 11.5 collective-permute-start.23
  1086.8 13.1 collective-permute-start.25
  1124.4 10.2 collective-permute-start.21
  1156.5 15.2 %collective-permute-start.22 = (bf16[16,192]{1,0:T(8,128)(2,1)S(1)}, bf16[16,192]{1,0:T(8,128)(2,1)S(1)}, u32[]{:S(2)}, u32[]{:S(2)}) collective-permute-start(bf16[16,192]{1,0:T(8,128)(2,1)S(1)} %fusion.74), channel_id=1, source_target_pairs={{0,1},{1,0},{2,3},{3,2},{4,5},{5,4},{6,7},{7,6},{8,9},{9,8},{10,11... | collective-permute-start | bytes 18440 | tf_op jit(solution)/shard_map/ppermute | solution.py:23
  1156.9 17.4 %collective-permute-start.26 = (bf16[192,1536]{1,0:T(8,128)(2,1)}, bf16[192,1536]{1,0:T(8,128)(2,1)S(1)}, u32[]{:S(2)}, u32[]{:S(2)}) collective-permute-start(bf16[192,1536]{1,0:T(8,128)(2,1)} %reduce-scatter.17.cloned.1.call-done), channel_id=1, source_target_pairs={{0,2},{2,0},{1,3},{3,1},{4,6},{6,4},{5,7},{7,5},{8,10},{10,8},{9,1... | collective-permute-start | bytes 1769480 | tf_op jit(solution)/shard_map/ppermute | solution.py:23
  1172.3 16.5 %collective-permute-start.24 = (bf16[192,1536]{1,0:T(8,128)(2,1)}, bf16[192,1536]{1,0:T(8,128)(2,1)}, u32[]{:S(2)}, u32[]{:S(2)}) collective-permute-start(bf16[192,1536]{1,0:T(8,128)(2,1)} %reduce-scatter.13.cloned.1.call-done), channel_id=1, source_target_pairs={{0,2},{2,0},{1,3},{3,1},{4,6},{6,4},{5,7},{7,5},{8,10},{10,8},{9,1... | collective-permute-start | bytes 1769480 | tf_op jit(solution)/shard_map/ppermute | solution.py:23
  1173.6 207.4 %collective-permute-start.31 = (bf16[192,3072]{1,0:T(8,128)(2,1)}, bf16[192,3072]{1,0:T(8,128)(2,1)}, u32[]{:S(2)}, u32[]{:S(2)}) collective-permute-start(bf16[192,3072]{1,0:T(8,128)(2,1)} %reduce-scatter.27.cloned.1.call-done), channel_id=1, source_target_pairs={{0,2},{2,0},{1,3},{3,1},{4,6},{6,4},{5,7},{7,5},{8,10},{10,8},{9,1... | collective-permute-start | bytes 3538952 | tf_op jit(solution)/shard_map/ppermute | solution.py:23
  1179.4 203.2 %collective-permute-start.29 = (bf16[192,3072]{1,0:T(8,128)(2,1)}, bf16[192,3072]{1,0:T(8,128)(2,1)}, u32[]{:S(2)}, u32[]{:S(2)}) collective-permute-start(bf16[192,3072]{1,0:T(8,128)(2,1)} %reduce-scatter.23.cloned.1.call-done), channel_id=1, source_target_pairs={{0,2},{2,0},{1,3},{3,1},{4,6},{6,4},{5,7},{7,5},{8,10},{10,8},{9,1... | collective-permute-start | bytes 3538952 | tf_op jit(solution)/shard_map/ppermute | solution.py:23
  1279.4 104.8 %collective-permute-start.32 = (bf16[192,3072]{1,0:T(8,128)(2,1)}, bf16[192,3072]{1,0:T(8,128)(2,1)}, u32[]{:S(2)}, u32[]{:S(2)}) collective-permute-start(bf16[192,3072]{1,0:T(8,128)(2,1)} %reduce-scatter.29.cloned.1.call-done), channel_id=1, source_target_pairs={{0,2},{2,0},{1,3},{3,1},{4,6},{6,4},{5,7},{7,5},{8,10},{10,8},{9,1... | collective-permute-start | bytes 3538952 | tf_op jit(solution)/shard_map/ppermute | solution.py:23
  1379.5 25.8 %collective-permute-start.30 = (bf16[192,3072]{1,0:T(8,128)(2,1)}, bf16[192,3072]{1,0:T(8,128)(2,1)S(1)}, u32[]{:S(2)}, u32[]{:S(2)}) collective-permute-start(bf16[192,3072]{1,0:T(8,128)(2,1)} %reduce-scatter.25.cloned.1.call-done), channel_id=1, source_target_pairs={{0,2},{2,0},{1,3},{3,1},{4,6},{6,4},{5,7},{7,5},{8,10},{10,8},{9,1... | collective-permute-start | bytes 3538952 | tf_op jit(solution)/shard_map/ppermute | solution.py:23
  (188 other events, 6681.2 us)
Sparse Core Ops, SparseCore 0:
  10.9 86.3 all-gather.13
  100.2 66.2 all-gather.11
  169.4 67.3 all-gather.15
  238.3 97.6 all-gather.17
  338.0 98.9 all-gather.19
  607.3 35.4 reduce-scatter.20
  742.5 35.2 reduce-scatter.18
  788.0 35.3 reduce-scatter.10
  826.3 35.4 reduce-scatter.14
  864.5 53.8 reduce-scatter.16
  921.4 53.3 reduce-scatter.12
  976.9 97.8 reduce-scatter.26
  1077.1 102.2 reduce-scatter.22
  1181.5 97.8 reduce-scatter.28
  1281.6 97.8 reduce-scatter.24

commit v2 on v1

--- a/solution.py
+++ b/solution.py
@@ -17,20 +17,26 @@
 FSDP = ("z", "core")
 PAIR = ((0, 1), (1, 0))
 DEAD = -1e30
+LIGHT = pl.CostEstimate(flops=1, bytes_accessed=1, transcendentals=0)
 
 
 def swap(values, axis):
     return lax.ppermute(values, axis, PAIR)
 
 
-def pair_sum(values, axis):
+def after(value, *others):
+    return lax.optimization_barrier((value,) + others)[0] if others else value
+
+
+def pair_sum(values, axis, *ready):
     mine = values.astype(BF16)
-    return mine.astype(F32) + swap(mine, axis).astype(F32)
-
-
-def ctx_sum(values):
+    other = swap(mine, axis)
+    return after(mine, *ready).astype(F32) + other.astype(F32)
+
+
+def ctx_sum(values, *ready):
     if lax.axis_size("ctx") == 2:
-        return pair_sum(values, "ctx")
+        return pair_sum(values, "ctx", *ready)
     return lax.psum(values.astype(BF16), "ctx").astype(F32)
 
 
@@ -47,33 +53,101 @@
 
 
 def gather_rows(shard):
-    streams, rows, columns = shard.shape
+    streams, rows = shard.shape[:2]
     if lax.axis_size("ctx") == 2:
         piece = lax.dynamic_index_in_dim(shard, lax.axis_index("ctx"), 0, keepdims=False)
+        piece = piece.reshape(rows, -1)
         whole = lax.all_gather(piece, ("ctx",) + FSDP, axis=0, tiled=True)
-        return whole.reshape(streams, -1, columns)
-    return lax.all_gather(shard, FSDP, axis=1, tiled=True)
-
-
-def reduce_rows(part):
-    own = lax.psum_scatter(part.astype(BF16), FSDP, scatter_dimension=0, tiled=True)
-    return ctx_sum(own)
+        return whole.reshape(streams, -1, piece.shape[1])
+    return lax.all_gather(shard.reshape(streams, rows, -1), FSDP, axis=1, tiled=True)
+
+
+def scatter_rows(part):
+    over = FSDP + ("ctx",) if lax.axis_size("ctx") == 2 else FSDP
+    return lax.psum_scatter(part.astype(BF16), over, scatter_dimension=0, tiled=True)
+
+
+def rotate(values, step):
+    count = lax.axis_size("z")
+    return lax.ppermute(values, "z", [(index, (index + step) % count) for index in range(count)])
+
+
+def halves(values, axis_name, dim):
+    index = lax.axis_index(axis_name)
+    keep = lax.dynamic_index_in_dim(values, index, dim, keepdims=False)
+    give = lax.dynamic_index_in_dim(values, 1 - index, dim, keepdims=False)
+    return keep, give
+
+
+def add_low(left, right):
+    return (left.astype(F32) + right.astype(F32)).astype(BF16)
+
+
+def core_step(terms, *ready):
+    if lax.axis_size("ctx") != 2:
+        return jnp.concatenate([scatter_rows(term) for term in terms], axis=-1)
+    count = lax.axis_size("z")
+    sums = []
+    for term in terms:
+        keep, give = halves(term.reshape(count, 2, -1, term.shape[1]), "core", 1)
+        sums.append(add_low(after(keep, *ready), swap(give, "core")))
+    return jnp.concatenate(sums, axis=-1)
+
+
+def ctx_step(chip, *ready):
+    if lax.axis_size("ctx") != 2:
+        return chip
+    count, rows, columns = chip.shape
+    keep, give = halves(chip.reshape(count, 2, rows // 2, columns), "ctx", 1)
+    return add_low(after(keep, *ready), swap(give, "ctx"))
+
+
+def z_step(both, *ready):
+    if lax.axis_size("ctx") != 2:
+        return both
+    count, z_index = lax.axis_size("z"), lax.axis_index("z")
+    keep = lax.dynamic_index_in_dim(both, z_index, 0, keepdims=False)
+    total = after(keep, *ready).astype(F32)
+    for step in range(1, count):
+        target = lax.rem(z_index + step, count)
+        given = lax.dynamic_index_in_dim(both, target, 0, keepdims=False)
+        total = total + rotate(given, step).astype(F32)
+    return total.astype(BF16)
+
+
+def end_step(mine, *ready):
+    if lax.axis_size("ctx") != 2:
+        return ctx_sum(mine)
+    other = swap(mine, "ctx")
+    mine = after(mine, *ready)
+    first = lax.axis_index("ctx") == 0
+    return jnp.concatenate(
+        [jnp.where(first, mine, other), jnp.where(first, other, mine)], axis=0
+    ).astype(F32)
+
+
+def gather_groups(row):
+    count = lax.axis_size("z")
+    other = swap(row, "core")
+    first = lax.axis_index("core") == 0
+    chip = jnp.stack([jnp.where(first, row, other), jnp.where(first, other, row)], axis=0)
+    rows = [chip] + [rotate(chip, step) for step in range(1, count)]
+    ring = jnp.stack([rows[-place % count] for place in range(2 * count)], axis=0)
+    start = lax.rem(count - lax.axis_index("z"), count)
+    return lax.dynamic_slice_in_dim(ring, start, count, 0).reshape(2 * count, -1)
 
 
 def scatter_groups(parts):
     z_count = lax.axis_size("z")
-    z_index, core = lax.axis_index("z"), lax.axis_index("core")
+    z_index = lax.axis_index("z")
     split = parts.reshape((z_count, 2) + parts.shape[1:])
-    keep = lax.dynamic_index_in_dim(split, core, 1, keepdims=False)
-    give = lax.dynamic_index_in_dim(split, 1 - core, 1, keepdims=False)
+    keep, give = halves(split, "core", 1)
     chip = keep + swap(give, "core")
     total = lax.dynamic_index_in_dim(chip, z_index, 0, keepdims=False)
     for step in range(1, z_count):
         target = lax.rem(z_index + step, z_count)
         sent = lax.dynamic_index_in_dim(chip, target, 0, keepdims=False)
-        total = total + lax.ppermute(
-            sent, "z", [(index, (index + step) % z_count) for index in range(z_count)]
-        )
+        total = total + rotate(sent, step)
     return total
 
 
@@ -202,6 +276,120 @@
         value_sum[stream : stream + 1] = value_totals[stream]
 
 
+def weight_kernel(groups, *refs):
+    result = refs[-1]
+
+    def body(step, carry):
+        columns = pl.ds(pl.multiple_of(step * 256, 256), 256)
+        base = 0
+        place = 0
+        for count, width in groups:
+            total = None
+            for _ in range(count):
+                term = dot_tn(refs[place][:, columns], refs[place + 1][...])
+                total = term if total is None else total + term
+                place += 2
+            result[columns, base : base + width] = total.astype(BF16)
+            base += width
+        return carry
+
+    lax.fori_loop(0, result.shape[0] // 256, body, 0)
+
+
+def weight_terms(groups):
+    flat_operands = [part for group in groups for pair in group for part in pair]
+    shape = tuple((len(group), group[0][1].shape[1]) for group in groups)
+    rows = flat_operands[0].shape[1]
+    return pl.pallas_call(
+        functools.partial(weight_kernel, shape),
+        in_specs=[pl.BlockSpec(memory_space=pltpu.VMEM)] * len(flat_operands),
+        out_specs=pl.BlockSpec(memory_space=pltpu.VMEM),
+        out_shape=jax.ShapeDtypeStruct((rows, sum(part[1] for part in shape)), BF16),
+        compiler_params=pltpu.CompilerParams(vmem_limit_bytes=52 * 1024 * 1024),
+        cost_estimate=LIGHT,
+        name="weight_terms",
+    )(*flat_operands)
+
+
+def unit_parts(values):
+    row_mean = jnp.mean(values, axis=-1, keepdims=True)
+    centred = values - row_mean
+    inverse = lax.rsqrt(jnp.mean(centred * centred, axis=-1, keepdims=True) + 1e-06)
+    return centred * inverse, inverse
+
+
+def middle_kernel(mine, other, tokens, mods, bias, att_ref, middle_ref, hidden_ref):
+    att = mine[...].astype(F32) + other[...].astype(F32) + bias[...]
+    middle = tokens[...].astype(F32) + mods[2:3] * att
+    att_ref[...] = att
+    middle_ref[...] = middle
+    unit, _ = unit_parts(middle)
+    hidden_ref[...] = (unit * (1.0 + mods[4:5]) + mods[3:4]).astype(BF16)
+
+
+def add_rows(sums, values):
+    @pl.when(pl.program_id(1) == 0)
+    def _():
+        sums[...] = jnp.zeros_like(sums)
+
+    for place, value in enumerate(values):
+        sums[place : place + 1] += jnp.sum(value, axis=0, keepdims=True)
+
+
+def norm_back(values, scale, grad):
+    unit, inverse = unit_parts(values)
+    unit_grad = grad * (1.0 + scale)
+    first = jnp.mean(unit_grad, axis=-1, keepdims=True)
+    second = jnp.mean(unit_grad * unit, axis=-1, keepdims=True)
+    return inverse * (unit_grad - first - unit * second), grad * unit
+
+
+def middle_back_kernel(
+    mine, other, middle, att, final_grad, mods, middle_grad, att_grad, sums
+):
+    grad = mine[...].astype(F32) + other[...].astype(F32)
+    back, scaled = norm_back(middle[...], mods[4:5], grad)
+    total = final_grad[...] + back
+    middle_grad[...] = total
+    low = total * mods[2:3]
+    att_grad[...] = low.astype(BF16)
+    add_rows(sums, (grad, scaled, total * att[...], low))
+
+
+def edge_back_kernel(mine, other, tokens, middle_grad, mods, input_grad, sums):
+    grad = mine[...].astype(F32) + other[...].astype(F32)
+    back, scaled = norm_back(tokens[...].astype(F32), mods[1:2], grad)
+    input_grad[...] = (middle_grad[...] + back).astype(BF16)
+    add_rows(sums, (grad, scaled))
+
+
+def by_rows(kernel, name, rows_arrays, slot_arrays, shared, outputs, with_sums):
+    slots, rows = rows_arrays[0].shape[:2]
+    step = next(size for size in (96, 72, 48, 32, 16) if rows % size == 0)
+    row_spec = pl.BlockSpec((None, step, D), lambda slot, block: (slot, block, 0))
+    sums_spec = pl.BlockSpec((None, 8, D), lambda slot, block: (slot, 0, 0))
+    out_specs = [row_spec] * len(outputs)
+    out_shape = [jax.ShapeDtypeStruct((slots, rows, D), dtype) for dtype in outputs]
+    if with_sums:
+        out_specs.append(sums_spec)
+        out_shape.append(jax.ShapeDtypeStruct((slots, 8, D), F32))
+    return pl.pallas_call(
+        kernel,
+        grid=(slots, rows // step),
+        in_specs=[row_spec] * len(rows_arrays)
+        + [
+            pl.BlockSpec((None, part.shape[1], D), lambda slot, block: (slot, 0, 0))
+            for part in slot_arrays
+        ]
+        + [pl.BlockSpec((1, D), lambda slot, block: (0, 0)) for _ in shared],
+        out_specs=out_specs,
+        out_shape=out_shape,
+        compiler_params=pltpu.CompilerParams(vmem_limit_bytes=40 * 1024 * 1024),
+        cost_estimate=LIGHT,
+        name=name,
+    )(*rows_arrays, *slot_arrays, *shared)
+
+
 def block_of(slot, rows, base=0):
     return pl.BlockSpec((None, rows, LANES), lambda pair: (slot, 0, base + pair))
 
@@ -219,8 +407,8 @@
     for rows_array, _, here, _ in key_parts:
         rows = rows_array.shape[-2]
         if here:
-            keys.append(block_of(slot, rows))
-            values.append(block_of(slot, rows, pairs))
+            keys.append(block_of(slot, rows, pairs))
+            values.append(block_of(slot, rows, 2 * pairs))
         else:
             keys.append(flat_block(rows))
             values.append(flat_block(rows, pairs))
@@ -233,10 +421,9 @@
     return arrays + arrays + [part[1] for part in key_parts]
 
 
-def attend(slot, queries, key_parts):
+def attend(slot, width, queries, key_parts):
     image, text = queries
     image_rows, text_rows = image.shape[1], text.shape[1]
-    width = image.shape[2]
     pairs = width // LANES
     stacked = 2 * (image_rows + text_rows)
     key_rows = sum(part[0].shape[-2] for part in key_parts)
@@ -260,19 +447,14 @@
             pltpu.VMEM((key_rows, stacked), F32),
         ],
         compiler_params=pltpu.CompilerParams(vmem_limit_bytes=48 * 1024 * 1024),
-        cost_estimate=pl.CostEstimate(
-            flops=pairs * 4 * key_rows * stacked * 4 * LANES,
-            bytes_accessed=2 * width * (2 * image_rows + 2 * key_rows),
-            transcendentals=pairs * key_rows * stacked,
-        ),
+        cost_estimate=LIGHT,
         name="attend",
     )(image, text, *key_operands(key_parts))
 
 
-def attend_back(slot, queries, outs, grads, log_total, key_parts):
+def attend_back(slot, width, queries, outs, grads, log_total, key_parts):
     image, text = queries
     image_rows, text_rows = image.shape[1], text.shape[1]
-    width = image.shape[2]
     pairs = width // LANES
     stacked = 2 * (image_rows + text_rows)
     key_rows = sum(part[0].shape[-2] for part in key_parts)
@@ -287,7 +469,7 @@
         grid=(pairs,),
         in_specs=row_blocks
         + [flat_block(image_rows), flat_block(text_rows)]
-        + row_blocks
+        + [flat_block(image_rows), block_of(slot, text_rows)]
         + [pl.BlockSpec((None, 1, stacked), lambda pair: (pair, 0, 0))]
         + key_specs(slot, key_parts, pairs),
         out_specs=[flat_block(image_rows), flat_block(text_rows), sum_block, sum_block]
@@ -305,11 +487,7 @@
             pltpu.VMEM((stacked, LANES), F32),
         ],
         compiler_params=pltpu.CompilerParams(vmem_limit_bytes=48 * 1024 * 1024),
-        cost_estimate=pl.CostEstimate(
-            flops=pairs * 10 * key_rows * stacked * 4 * LANES,
-            bytes_accessed=2 * width * (4 * image_rows + 4 * key_rows),
-            transcendentals=pairs * key_rows * stacked,
-        ),
+        cost_estimate=LIGHT,
         name="attend_back",
     )(image, text, outs[0], outs[1], grads[0], grads[1], log_total, *key_operands(key_parts))
 
@@ -350,8 +528,7 @@
     rows_local = ada_weight.shape[1]
     width = qkv_weight.shape[3]
 
-    kv_full = gather_rows(qkv_weight[:, :, 1:].reshape(2, rows_local, 2 * width))
-    q_full = gather_rows(qkv_weight[:, :, 0])
+    qkv_full = gather_rows(qkv_weight)
     out_full = gather_rows(jnp.swapaxes(attn_out_weight, 1, 2))
     up_full = gather_rows(mlp_up_weight)
     down_full = gather_rows(jnp.swapaxes(mlp_down_weight, 1, 2))
@@ -369,17 +546,16 @@
 
     cond_float = cond_vector.astype(F32)
     activated = jax.nn.silu(cond_float).astype(BF16)
-    ada_local = ada_weight.reshape(2, rows_local, spans, D)
-    ada_partial = jnp.einsum("sd,tdke->stke", activated, ada_local, preferred_element_type=F32)
+    ada_partial = jnp.einsum("sd,tdk->stk", activated, ada_weight, preferred_element_type=F32)
     mod_half = scatter_groups(
-        ada_partial.reshape(seq_count // slot_count, slot_count, 2, spans, D)
-    ) + ada_bias.reshape(1, 2, spans, D)
+        ada_partial.reshape(seq_count // slot_count, slot_count, 2, spans * D)
+    ) + ada_bias
     mod_other = swap(mod_half, "tp")
     modulation = jnp.where(
         tp_index == 0,
         jnp.concatenate([mod_half, mod_other], axis=2),
         jnp.concatenate([mod_other, mod_half], axis=2),
-    )
+    ).reshape(slot_count, 2, 6, D)
 
     counts = (image_counts, text_counts)
     live_rows = []
@@ -406,32 +582,26 @@
         return values.reshape(slot_count, caps[stream], values.shape[-1])
 
     inputs = [part.astype(F32) for part in tokens]
-    hidden_in, queries, key_values = [], [], []
+    hidden_in, projected = [], []
     for stream in range(2):
         normed = flat(
             modulate(inputs[stream], mod_of(stream, 0), mod_of(stream, 1)).astype(BF16)
         )
         hidden_in.append(normed)
-        value_bias = jnp.concatenate(
-            [jnp.zeros((width,), F32), qv_bias[stream, 1].astype(F32)], axis=0
-        )
-        key_values.append(
-            tall(stream, (dot(normed, kv_full[stream]) + value_bias).astype(BF16))
-        )
-        queries.append(
-            tall(stream, (dot(normed, q_full[stream]) + qv_bias[stream, 0]).astype(BF16))
-        )
+        both_bias = qv_bias[stream].astype(F32)
+        bias = jnp.concatenate([both_bias[0], jnp.zeros((width,), F32), both_bias[1]], axis=0)
+        projected.append(tall(stream, (dot(normed, qkv_full[stream]) + bias).astype(BF16)))
 
     key_parts = []
     for slot in range(slot_count):
         parts = []
         for stream in range(2):
             if ctx_count == 2:
-                other = swap(key_values[stream][slot], "ctx")
+                other = swap(projected[stream][slot, :, width:], "ctx")
                 bias = key_bias[stream][slot]
                 parts.append(
                     (
-                        key_values[stream],
+                        projected[stream],
                         lax.dynamic_index_in_dim(bias, ctx_index, 0, keepdims=False),
                         True,
                         stream,
@@ -446,32 +616,72 @@
                     )
                 )
             else:
-                everyone = lax.all_gather(key_values[stream][slot], "ctx", axis=0, tiled=False)
+                everyone = lax.all_gather(
+                    projected[stream][slot, :, width:], "ctx", axis=0, tiled=False
+                )
                 parts.append((flat(everyone), flat(key_bias[stream][slot]), False, stream))
         key_parts.append(parts)
-    outs, logs = [], []
-    for slot in range(slot_count):
-        out_image, out_text, log_total = attend(slot, queries, key_parts[slot])
+    slots = range(slot_count)
+    text_unit = slot_count
+
+    def unit_stream(unit):
+        return 1 if unit == text_unit else 0
+
+    def unit_of(unit, values):
+        if unit == text_unit:
+            return values[1]
+        return values[0][unit : unit + 1]
+
+    def unit_mod(unit, which):
+        return unit_of(unit, [mod_of(0, which), mod_of(1, which)])
+
+    def unit_rows(unit, values):
+        return values.reshape(-1, caps[unit_stream(unit)], values.shape[-1])
+
+    mods = [modulation[:, 0], modulation[:, 1]]
+    units = range(slot_count + 1)
+    outs, logs, attended = [], [], []
+    att_values, middles, hidden_units = {}, {}, {}
+
+    def middle_of(unit, *ready):
+        stream = unit_stream(unit)
+        mine = dot_nt(attended[unit], out_full[stream]).astype(BF16)
+        other = swap(mine, "tp")
+        att_values[unit], middles[unit], hidden = by_rows(
+            middle_kernel,
+            "middle",
+            [unit_rows(unit, after(mine, *ready)), unit_rows(unit, other), unit_of(unit, tokens)],
+            [unit_of(unit, mods)],
+            [attn_out_bias[stream].astype(F32)[None]],
+            [F32, F32, BF16],
+            False,
+        )
+        hidden_units[unit] = flat(hidden)
+
+    ready = ()
+    for slot in slots:
+        out_image, out_text, log_total = attend(
+            slot,
+            width,
+            [after(part, *ready) for part in projected],
+            key_parts[slot],
+        )
         outs.append((out_image, out_text))
         logs.append(log_total)
-    attended = [jnp.concatenate([out[stream] for out in outs], axis=0) for stream in range(2)]
-
-    att_values, middles, hidden_mid, pre_acts, activs = [], [], [], [], []
-    for stream in range(2):
-        att_value = (
-            tall(stream, pair_sum(dot_nt(attended[stream], out_full[stream]), "tp"))
-            + attn_out_bias[stream]
-        )
-        middle = inputs[stream] + mod_of(stream, 2) * att_value
-        normed = flat(modulate(middle, mod_of(stream, 3), mod_of(stream, 4)).astype(BF16))
-        pre_act = dot(normed, up_full[stream]) + mlp_up_bias[stream]
-        att_values.append(att_value)
-        middles.append(middle)
-        hidden_mid.append(normed)
-        pre_acts.append(pre_act)
-        activs.append(gelu_tanh(pre_act).astype(BF16))
-
-    grad_finals, grad_mlp_low, down_bias_grads, pre_lows, up_bias_grads = [], [], [], [], []
+        attended.append(out_image)
+        if slot == slot_count - 1:
+            attended.append(jnp.concatenate([out[1] for out in outs], axis=0))
+            middle_of(text_unit)
+        middle_of(slot)
+        ready = (hidden_units[slot],)
+    hidden_mid = [
+        jnp.concatenate([hidden_units[slot] for slot in slots], axis=0),
+        hidden_units[text_unit],
+    ]
+    pre_acts = [dot(hidden_mid[stream], up_full[stream]) + mlp_up_bias[stream] for stream in range(2)]
+    activs = [gelu_tanh(pre_act).astype(BF16) for pre_act in pre_acts]
+
+    grad_finals, grad_mlp_low, down_bias_grads = [], [], []
     for stream in range(2):
         grad_final = (
             cotangents[stream].astype(F32) * live_rows[stream] * own_weights[:, None, None]
@@ -480,125 +690,239 @@
         grad_finals.append(grad_final)
         down_bias_grads.append(jnp.sum(flat(grad_mlp), axis=0))
         grad_mlp_low.append(flat(grad_mlp.astype(BF16)))
-        grad_act = dot(grad_mlp_low[stream], down_full[stream])
+    def mlp_weight_term(stream, *ready):
+        return dot_tn(after(grad_mlp_low[stream], *ready), activs[stream]).astype(BF16)
+
+    def up_weight_term(stream, *ready):
+        return dot_tn(after(hidden_mid[stream], *ready), pre_lows[stream]).astype(BF16)
+
+    down_terms = [mlp_weight_term(0, activs[1])]
+    down_terms.append(mlp_weight_term(1, down_terms[0]))
+    pre_lows, up_bias_grads, hid2_parts = [None, None], [None, None], {}
+    up_terms = [None, None]
+    ready = tuple(down_terms)
+    for stream in (1, 0):
+        grad_act = dot(after(grad_mlp_low[stream], *ready), down_full[stream])
         pre_grad = jax.vjp(gelu_tanh, pre_acts[stream])[1](grad_act)[0]
-        up_bias_grads.append(jnp.sum(pre_grad, axis=0))
-        pre_lows.append(pre_grad.astype(BF16))
-    hid2_sums = [
-        tall(stream, pair_sum(dot_nt(pre_lows[stream], up_full[stream]), "tp"))
-        for stream in range(2)
-    ]
-    down_grads = [
-        reduce_rows(dot_tn(grad_mlp_low[stream], activs[stream])) for stream in range(2)
-    ]
-    up_grads = [reduce_rows(dot_tn(hidden_mid[stream], pre_lows[stream])) for stream in range(2)]
-
+        up_bias_grads[stream] = jnp.sum(pre_grad, axis=0)
+        pre_lows[stream] = pre_grad.astype(BF16)
+        for unit in units:
+            if unit_stream(unit) != stream:
+                continue
+            rows = pre_lows[stream]
+            if stream == 0:
+                rows = rows[unit * cap_image : (unit + 1) * cap_image]
+            hid2_parts[unit] = dot_nt(after(rows, *ready), up_full[stream]).astype(BF16)
+            ready = (hid2_parts[unit],)
+        if stream == 0:
+            up_chip = core_step([up_terms[1]], *ready)
+            ready = (up_chip,)
+        up_terms[stream] = up_weight_term(stream, *ready)
+        ready = (up_terms[stream],)
+    down_shards = [scatter_rows(term) for term in down_terms]
+    up_shard = scatter_rows(after(up_terms[0], down_terms[1]))
+
+    grad_middles, mid_sums, grad_att_low, grad_attended = {}, {}, {}, {}
+
+    def middle_back(unit, *ready):
+        stream = unit_stream(unit)
+        other = swap(hid2_parts[unit], "tp")
+        grad_middles[unit], low, mid_sums[unit] = by_rows(
+            middle_back_kernel,
+            "middle_back",
+            [
+                unit_rows(unit, after(hid2_parts[unit], *ready)),
+                unit_rows(unit, other),
+                middles[unit],
+                att_values[unit],
+                unit_of(unit, grad_finals),
+            ],
+            [unit_of(unit, mods)],
+            [],
+            [F32, BF16],
+            True,
+        )
+        grad_att_low[unit] = flat(low)
+        grad_attended[unit] = dot(grad_att_low[unit], out_full[stream]).astype(BF16)
+
+    query_grads, given_pairs = {}, {}
+    bias_sums = 0.0
+    mlp_parts = []
+    for slot in slots:
+        middle_back(slot, *ready)
+        if slot == 0:
+            middle_back(text_unit, grad_attended[slot])
+            ready = (grad_attended[text_unit],)
+        results = attend_back(
+            slot,
+            width,
+            projected,
+            outs[slot],
+            (
+                after(grad_attended[slot], *ready),
+                tall(1, grad_attended[text_unit]),
+            ),
+            logs[slot],
+            key_parts[slot],
+        )
+        ready = (results[0],)
+        bias_sums = bias_sums + jnp.stack(
+            [jnp.swapaxes(part, 0, 1).reshape(2, width) for part in results[2:4]], axis=1
+        )
+        for stream in range(2):
+            query_grads[slot, stream] = results[stream]
+            if ctx_count == 2:
+                given_pairs[slot, stream] = (
+                    results[4 + 2 * stream],
+                    swap(results[5 + 2 * stream], "ctx"),
+                )
+            else:
+                total = lax.psum_scatter(
+                    results[4 + stream], "ctx", scatter_dimension=1, tiled=True
+                )
+                given_pairs[slot, stream] = (total, jnp.zeros_like(total))
+        if slot == 0:
+            up_both = ctx_step(up_chip, *ready)
+            for stream in range(2):
+                rows = after(activs[stream], up_both, *ready)
+                mlp_parts.append(dot_nt(rows, down_full[stream]).astype(BF16))
+                ready = (mlp_parts[stream],)
+
+    pair_grads, hid_parts = {}, {}
+
+    def hid_part(slot, *ready):
+        for stream in range(2):
+            mine, given = given_pairs[slot, stream]
+            total = add_low(after(mine, *ready), given)
+            pair_grads[slot, stream] = jnp.concatenate([total[0], total[1]], axis=1)
+        rows = jnp.concatenate([query_grads[slot, 0], pair_grads[slot, 0]], axis=1)
+        hid_parts[slot] = dot_nt(rows, qkv_full[0]).astype(BF16)
+
+    hid_part(0, *ready)
+    ready = (hid_parts[0],)
     finals, gate2_grads = [], []
     for stream in range(2):
         mlp_value = (
-            tall(stream, pair_sum(dot_nt(activs[stream], down_full[stream]), "tp"))
-            + mlp_down_bias[stream]
+            tall(stream, pair_sum(mlp_parts[stream], "tp", *ready)) + mlp_down_bias[stream]
         )
         gate2_grads.append(jnp.sum(grad_finals[stream] * mlp_value, axis=1))
+        middle = middles[text_unit]
+        if stream == 0:
+            middle = jnp.concatenate([middles[slot] for slot in slots], axis=0)
         final = (
-            (middles[stream] + mod_of(stream, 5) * mlp_value)
+            (middle + mod_of(stream, 5) * mlp_value)
             * live_rows[stream]
             * own_live[:, None, None]
         )
         finals.append(final.astype(BF16))
-
-    grad_middles, mid_mod_grads, gate1_grads, out_bias_grads = [], [], [], []
-    out_grads, grad_attended = [], []
+    ready = tuple(finals)
+    groups = []
     for stream in range(2):
-        back, shift_grad, scale_grad = modulate_back(
-            middles[stream], mod_of(stream, 4), hid2_sums[stream]
-        )
-        grad_middle = grad_finals[stream] + back
-        grad_middles.append(grad_middle)
-        mid_mod_grads.append((shift_grad, scale_grad))
-        gate1_grads.append(jnp.sum(grad_middle * att_values[stream], axis=1))
-        grad_att = grad_middle * mod_of(stream, 2)
-        out_bias_grads.append(jnp.sum(flat(grad_att), axis=0))
-        grad_att_low = flat(grad_att.astype(BF16))
-        grad_attended.append(tall(stream, dot(grad_att_low, out_full[stream]).astype(BF16)))
-        out_grads.append(reduce_rows(dot_tn(grad_att_low, attended[stream])))
-
-    query_grads, pair_grads = ([], []), ([], [])
-    bias_sums = 0.0
-    for slot in range(slot_count):
-        results = attend_back(
-            slot, queries, outs[slot], grad_attended, logs[slot], key_parts[slot]
-        )
-        bias_sums = bias_sums + jnp.stack(
-            [jnp.swapaxes(part, 0, 1).reshape(2, width) for part in results[2:4]], axis=1
-        )
-        for stream in range(2):
-            query_grads[stream].append(results[stream])
-            if ctx_count == 2:
-                mine, given = results[4 + 2 * stream], results[5 + 2 * stream]
-                total = mine.astype(F32) + swap(given, "ctx").astype(F32)
-            else:
-                total = lax.psum_scatter(
-                    results[4 + stream], "ctx", scatter_dimension=1, tiled=True
-                ).astype(F32)
-            pair_grads[stream].append(
-                jnp.concatenate([total[0].astype(BF16), total[1].astype(BF16)], axis=1)
-            )
-
-    input_grads, mod_rows, q_weight_grads, kv_weight_grads = [], [], [], []
+        members = list(slots) if stream == 0 else [text_unit]
+        groups.append([(after(grad_att_low[unit], *ready), attended[unit]) for unit in members])
     for stream in range(2):
-        query_grad = jnp.concatenate(query_grads[stream], axis=0)
-        pair_grad = jnp.concatenate(pair_grads[stream], axis=0)
-        hid_sum = tall(
-            stream,
-            pair_sum(
-                dot_nt(query_grad, q_full[stream]) + dot_nt(pair_grad, kv_full[stream]), "tp"
-            ),
-        )
-        q_weight_grads.append(reduce_rows(dot_tn(hidden_in[stream], query_grad)))
-        kv_weight_grads.append(reduce_rows(dot_tn(hidden_in[stream], pair_grad)))
-        back, shift_grad, scale_grad = modulate_back(inputs[stream], mod_of(stream, 1), hid_sum)
-        input_grads.append((grad_middles[stream] + back).astype(BF16))
-        mod_rows.append(
-            jnp.stack(
-                [
-                    shift_grad,
-                    scale_grad,
-                    gate1_grads[stream],
-                    mid_mod_grads[stream][0],
-                    mid_mod_grads[stream][1],
-                    gate2_grads[stream],
-                ],
-                axis=1,
-            )
-        )
-
-    mod_grads = jnp.stack(mod_rows, axis=1)
+        normed = tall(stream, hidden_in[stream])
+        groups.append([(normed[slot], query_grads[slot, stream]) for slot in slots])
+    first_term = weight_terms(groups)
+    first_shard = scatter_rows(first_term)
+    ready = (first_term,)
+    for slot in slots[1:]:
+        hid_part(slot, *ready)
+        ready = (hid_parts[slot],)
+    text_rows_grad = jnp.concatenate(
+        [
+            jnp.concatenate([query_grads[slot, 1], pair_grads[slot, 1]], axis=1)
+            for slot in slots
+        ],
+        axis=0,
+    )
+    hid_parts[text_unit] = dot_nt(after(text_rows_grad, *ready), qkv_full[1]).astype(BF16)
+    ready = (hid_parts[text_unit],)
+    groups = []
+    for stream in range(2):
+        normed = tall(stream, hidden_in[stream])
+        groups.append(
+            [(after(normed[slot], *ready), pair_grads[slot, stream]) for slot in slots]
+        )
+    second_term = weight_terms(groups)
+    second_shard = scatter_rows(second_term)
+    ready = (second_term,)
+    input_grads, edge_sums = {}, {}
+    for unit in list(slots) + [text_unit]:
+        other = swap(hid_parts[unit], "tp")
+        input_grads[unit], edge_sums[unit] = by_rows(
+            edge_back_kernel,
+            "edge_back",
+            [
+                unit_rows(unit, after(hid_parts[unit], *ready)),
+                unit_rows(unit, other),
+                unit_of(unit, tokens),
+                grad_middles[unit],
+            ],
+            [unit_of(unit, mods)],
+            [],
+            [BF16],
+            True,
+        )
+        ready = (input_grads[unit],)
+    up_mine = z_step(up_both, *ready)
+    down_grads = [end_step(shard, *ready) for shard in down_shards]
+    up_grads = [end_step(up_shard, *ready), end_step(up_mine)]
+    first_grads = end_step(first_shard)
+    second_grads = end_step(second_shard)
+    out_grads = [first_grads[:, :width], first_grads[:, width : 2 * width]]
+    q_weight_grads = [first_grads[:, 2 * width : 3 * width], first_grads[:, 3 * width :]]
+    kv_weight_grads = [second_grads[:, : 2 * width], second_grads[:, 2 * width :]]
+
+    def by_slot(values):
+        image = jnp.concatenate([values[slot] for slot in slots], axis=0)
+        return jnp.stack([image, values[text_unit]], axis=1)
+
+    mod_grads = jnp.stack(
+        [
+            by_slot({unit: edge_sums[unit][:, 0] for unit in units}),
+            by_slot({unit: edge_sums[unit][:, 1] for unit in units}),
+            by_slot({unit: mid_sums[unit][:, 2] for unit in units}),
+            by_slot({unit: mid_sums[unit][:, 0] for unit in units}),
+            by_slot({unit: mid_sums[unit][:, 1] for unit in units}),
+            jnp.stack(gate2_grads, axis=1),
+        ],
+        axis=2,
+    )
+    out_bias_sums = [
+        sum(mid_sums[slot][0, 3] for slot in slots),
+        jnp.sum(mid_sums[text_unit][:, 3], axis=0),
+    ]
+    input_grads = [
+        jnp.concatenate([input_grads[slot] for slot in slots], axis=0),
+        input_grads[text_unit],
+    ]
+
     mod_half_grads = lax.dynamic_slice_in_dim(mod_grads, tp_index * spans, spans, 2)
     pieces = (
         mod_half_grads,
         bias_sums,
         jnp.stack(up_bias_grads, axis=0),
-        jnp.stack(out_bias_grads, axis=0),
+        jnp.stack(out_bias_sums, axis=0),
         jnp.stack(down_bias_grads, axis=0),
     )
     row = ctx_sum(jnp.concatenate([piece.reshape(-1) for piece in pieces], axis=0))
-    everyone = lax.all_gather(row[None].astype(BF16), FSDP, axis=0, tiled=True).astype(F32)
+    everyone = gather_groups(row.astype(BF16)).astype(F32)
     ends = []
     base = 0
     for piece in pieces:
         ends.append(everyone[:, base : base + piece.size].reshape((-1,) + piece.shape))
         base += piece.size
-    mod_all = ends[0].reshape(seq_count, 2, spans, D)
+    mod_all = ends[0].reshape(seq_count, 2, spans * D)
     qv_bias_grad, up_bias_grad, out_bias_grad, down_bias_grad = [
         jnp.sum(part, axis=0) for part in ends[1:]
     ]
-    ada_bias_grad = jnp.sum(mod_all, axis=0).reshape(2, spans * D)
+    ada_bias_grad = jnp.sum(mod_all, axis=0)
     mod_low = mod_all.astype(BF16)
     ada_weight_grad = jnp.einsum(
-        "sd,stke->tdke", activated, mod_low, preferred_element_type=F32
-    ).reshape(2, rows_local, spans * D)
-    silu_part = jnp.einsum("stke,tdke->sd", mod_low, ada_local, preferred_element_type=F32)
+        "sd,stk->tdk", activated, mod_low, preferred_element_type=F32
+    )
+    silu_part = jnp.einsum("stk,tdk->sd", mod_low, ada_weight, preferred_element_type=F32)
     cond_grad = jax.vjp(jax.nn.silu, cond_float)[1](pair_sum(silu_part, "tp"))[0]
     qkv_grad = jnp.stack(
         [

time: 1420 us -> 1140 us (0.80)
  waiting for transfers between devices: 791 us -> 389 us
  local copies, waits for them, and re-layouts: 76.5 us -> 151 us
  Pallas kernels: 109 us -> 183 us
  matrix products: 253 us -> 234 us
  blocking collectives: 18.1 us -> 0 us
  starting transfers between devices: 39 us -> 54.5 us
    reduce_scatter x10 -> x5, waiting for transfers between devices: 190 us -> 0.01 us  [scatter_rows(): lax.psum_scatter(part.astype(BF16), over, scatter_dimension=0, tiled=True)]
    ppermute x30 -> x32, waiting for transfers between devices: 444 us -> 286 us  [swap(): return lax.ppermute(values, axis, PAIR)]
    all_gather x5 -> x4, waiting for transfers between devices: 151 us -> 36.6 us  [gather_rows(): whole = lax.all_gather(piece, ('ctx',) + FSDP, axis=0, tiled=True)]
    pallas_call x0 -> x11, Pallas kernels: none -> 73.8 us  [the longest x9 37.7 us: by_rows(): pl.pallas_call(kernel, grid=(slots, rows // step), in_specs=[row_spec] *...]
    ppermute x3 -> x9, waiting for transfers between devices: 5.4 us -> 66.3 us  [rotate(): lax.ppermute(values, 'z', [(index, (index + step) % count) for index in r...]
    dot_general x10 -> x4, matrix products: 86.5 us -> 47.4 us  [dot_tn(): lax.dot_general(left, right, (((0,), (0,)), ((), ())), preferred_element_...]
    reduce_sum x10 -> x2, other arithmetic: 37.2 us -> 2.81 us  [the longest x1 1.86 us: on_device(): ada_bias_grad = jnp.sum(mod_all, axis=0)]
    squeeze x1 -> x17, local copies, waits for them, and re-layouts: 0.02 us -> 25.5 us  [the longest x2 10.5 us: halves(): keep = lax.dynamic_index_in_dim(values, index, dim, keepdims=False)]
  transfers between devices with their start and end apart: 48 -> 50, of which waited for: 25 -> 22; matrix products, arithmetic and copies ran while one was open for 28% -> 39% of each run, Pallas kernels for 8% -> 16%
where the time goes in v2:
time: 1140 us; the launch traced here: 1130 us
  waiting for transfers between devices  389 us (34%)
  matrix products  234 us (21%)
  Pallas kernels  183 us (16%)
  local copies, waits for them, and re-layouts  151 us (13%)
  other arithmetic  106 us (9%)
  starting transfers between devices  54.5 us (5%)
  between operations  16.7 us (1%)
    ppermute x32, waiting for transfers between devices, swap(): return lax.ppermute(values, axis, PAIR)  286 us
    dot_general x9, matrix products, dot(): lax.dot_general(left, right, (((1,), (0,)), ((), ())), preferred_element_...  91.7 us
    dot_general x11, matrix products, dot_nt(): lax.dot_general(left, right, (((1,), (1,)), ((), ())), preferred_element_...  87 us
    pallas_call x2, Pallas kernels, attend_back(): pl.pallas_call(functools.partial(attend_back_kernel, tuple((part[3] for p...  72.3 us
    ppermute x9, waiting for transfers between devices, rotate(): lax.ppermute(values, 'z', [(index, (index + step) % count) for index in r...  66.3 us
    unnamed x413, local copies, waits for them, and re-layouts  54.8 us
    dot_general x4, matrix products, dot_tn(): lax.dot_general(left, right, (((0,), (0,)), ((), ())), preferred_element_...  47.4 us
    pallas_call x9, Pallas kernels, by_rows(): pl.pallas_call(kernel, grid=(slots, rows // step), in_specs=[row_spec] *...  37.7 us
  transfers between devices with their start and end apart: 50, of which 22 were waited for; matrix products, arithmetic and copies ran while one was open for 39% of the time, Pallas kernels for 16%

profile of v2, /device:TPU:0, one launch (start us, length us, event | category | flops | bytes accessed | tf_op | source)
XLA Modules:
  0.0 1133.5 jit_solution(2268700310728872274)
XLA Ops:
  66.6 9.2 collective-permute-done.2
  90.8 36.6 %all-gather.8.cloned.1.call-done = bf16[3072,2304]{1,0:T(8,128)(2,1)} async-done(((bf16[192,2304]{1,0:T(8,128)(2,1)}), bf16[3072,2304]{1,0:T(8,128)(2,1)}) %all-gather.8.cloned.1.call-update) | async-done | bytes 14155792 | tf_op jit(solution)/shard_map/all_gather | solution.py:60
  127.3 12.1 %fusion.6 = bf16[1152,2304]{1,0:T(8,128)(2,1)S(1)} fusion(bf16[1152,1536]{1,0:T(8,128)(2,1)} %bitcast.412, bf16[3072,2304]{1,0:T(8,128)(2,1)} %all-gather.8.cloned.1.call-done, f32[2304]{0:T(1024)} %get-tuple-element.309), kind=kOutput, calls=%fused_computation.11 | convolution fusion | flops 8159035392 | bytes 15937536 | tf_op jit(solution)/shard_map/dot_general | solution.py:44
  153.5 49.3 %collective-permute-done.6.refs_5_.refs_9_.refs_10_.refs_14_ = bf16[96,1536]{1,0:T(8,128)(2,1)S(1)} collective-permute-done((bf16[96,1536]{1,0:T(8,128)(2,1)S(1)}, bf16[96,1536]{1,0:T(8,128)(2,1)S(1)}, u32[]{:S(2)}, u32[]{:S(2)}) %collective-permute-start.6) | collective-permute-done | bytes 294944 | tf_op jit(solution)/shard_map/ppermute | solution.py:24
  202.8 18.3 %attend.2 = (bf16[576,768]{1,0:T(8,128)(2,1)S(1)}, bf16[96,768]{1,0:T(8,128)(2,1)S(1)}, f32[6,1,1344]{2,1,0:T(1,128)S(1)}) custom-call(bf16[2,576,2304]{2,1,0:T(8,128)(2,1)} %bitcast.397, bf16[2,96,2304]{2,1,0:T(8,128)(2,1)S(1)} %bitcast.359, bf16[2,576,2304]{2,1,0:T(8,128)(2,1)} %bitcast.398, ...), custom_call_target="tpu_custom_call" | custom-call | flops 1 | bytes 1 | tf_op jit(solution)/shard_map/attend/pallas_call | solution.py:430
  233.1 35.3 %collective-permute-done.7 = bf16[576,1536]{1,0:T(8,128)(2,1)S(1)} collective-permute-done((bf16[576,1536]{1,0:T(8,128)(2,1)S(1)}, bf16[576,1536]{1,0:T(8,128)(2,1)S(1)}, u32[]{:S(2)}, u32[]{:S(2)}) %collective-permute-start.7) | collective-permute-done | bytes 1769504 | tf_op jit(solution)/shard_map/ppermute | solution.py:24
  274.2 14.0 %collective-permute-done.9.refs_5_.refs_9_.refs_10_.refs_14_ = bf16[96,1536]{1,0:T(8,128)(2,1)S(1)} collective-permute-done((bf16[96,1536]{1,0:T(8,128)(2,1)S(1)}, bf16[96,1536]{1,0:T(8,128)(2,1)S(1)}, u32[]{:S(2)}, u32[]{:S(2)}) %collective-permute-start.9) | collective-permute-done | bytes 294944 | tf_op jit(solution)/shard_map/ppermute | solution.py:24
  288.3 18.7 %attend.3 = (bf16[576,768]{1,0:T(8,128)(2,1)S(1)}, bf16[96,768]{1,0:T(8,128)(2,1)S(1)}, f32[6,1,1344]{2,1,0:T(1,128)S(1)}) custom-call(bf16[2,576,2304]{2,1,0:T(8,128)(2,1)} %bitcast.400, bf16[2,96,2304]{2,1,0:T(8,128)(2,1)S(1)} %bitcast.362, bf16[2,576,2304]{2,1,0:T(8,128)(2,1)} %bitcast.401, ...), custom_call_target="tpu_custom_call" | custom-call | flops 1 | bytes 1 | tf_op jit(solution)/shard_map/attend/pallas_call | solution.py:430
  323.4 38.7 %collective-permute-done.11 = bf16[192,1536]{1,0:T(8,128)(2,1)S(1)} collective-permute-done((bf16[192,1536]{1,0:T(8,128)(2,1)S(1)}, bf16[192,1536]{1,0:T(8,128)(2,1)S(1)}, u32[]{:S(2)}, u32[]{:S(2)}) %collective-permute-start.11) | collective-permute-done | bytes 589856 | tf_op jit(solution)/shard_map/ppermute | solution.py:24
  372.7 8.5 multiply_convert_fusion.2
  381.2 21.1 %multiply_convert_fusion = (bf16[1152,3072]{1,0:T(8,128)(2,1)}, f32[1152,3072]{1,0:T(8,128)}) fusion(f32[3072]{0:T(1024)S(1)} %bitcast.426, bf16[1,3072,3072]{2,1,0:T(8,128)(2,1)} %all-gather.12.cloned.1.call-done, bf16[576,1536]{1,0:T(8,128)(2,1)S(1)} %bitcast.373, bf16[576,1536]{1,0:T(8,128)(2,1)S(1)} %bitcast.371), kind=kOutput, calls=%fused_computation.8 | convolution fusion | flops 10914103296 | bytes 34222080 | tf_op jit(solution)/shard_map/dot_general | solution.py:44
  402.3 17.8 %convolution_convert_fusion.3 = bf16[1536,3072]{1,0:T(8,128)(2,1)} fusion(bf16[1152,1536]{1,0:T(8,128)(2,1)S(1)} %bitcast.420, bf16[1152,3072]{1,0:T(8,128)(2,1)} %get-tuple-element.135), kind=kOutput, calls=%fused_computation.15 | convolution fusion | flops 10876354560 | bytes 20054016 | tf_op jit(solution)/shard_map/dot_general | solution.py:52
  420.1 7.7 convolution_convert_fusion.2
  435.8 6.6 fusion.118
  445.0 9.4 fusion.122
  454.5 8.9 fusion.63
  470.1 7.7 dynamic-slice_bitcast_fusion.1
  477.9 24.6 %fusion.117 = (bf16[3072]{0:T(1024)(128)(2,1)}, bf16[1152,3072]{1,0:T(8,128)(2,1)S(1)}) fusion(f32[1152,3072]{1,0:T(8,128)} %get-tuple-element.317, bf16[1152,1536]{1,0:T(8,128)(2,1)} %bitcast.419, bf16[1,3072,3072]{2,1,0:T(8,128)(2,1)} %all-gather.14.cloned.1.call-done), kind=kOutput, calls=%fused_computation.336 | convolution fusion | flops 10945950720 | bytes 34215936 | tf_op jit(solution)/shard_map/dot_general | solution.py:44
  506.4 10.4 fusion.41
  516.8 9.3 fusion.42
  537.8 16.9 %convolution_convert_fusion = bf16[1536,3072]{1,0:T(8,128)(2,1)} fusion(bf16[1152,1536]{1,0:T(8,128)(2,1)} %pad_maximum_fusion, bf16[1152,3072]{1,0:T(8,128)(2,1)S(1)} %copy-done.128), kind=kOutput, calls=%fused_computation.12 | convolution fusion | flops 10876354560 | bytes 20054016 | tf_op jit(solution)/shard_map/dot_general | solution.py:52
  561.3 8.0 middle_back.3
  582.2 36.2 %attend_back.2 = (bf16[576,768]{1,0:T(8,128)(2,1)S(1)}, bf16[96,768]{1,0:T(8,128)(2,1)S(1)}, f32[6,2,128]{2,1,0:T(2,128)S(1)}, f32[6,2,128]{2,1,0:T(2,128)S(1)},...) custom-call(bf16[2,576,2304]{2,1,0:T(8,128)(2,1)} %bitcast.403, ...), custom_call_target="tpu_custom_call" | custom-call | flops 1 | bytes 1 | tf_op jit(solution)/shard_map/attend_back/pallas_call | solution.py:465
  627.7 17.2 %fusion.15 = bf16[1152,1536]{1,0:T(8,128)(2,1)} fusion(bf16[1152,3072]{1,0:T(8,128)(2,1)} %get-tuple-element.135, bf16[1,3072,3072]{2,1,0:T(8,128)(2,1)} %all-gather.14.cloned.1.call-done), kind=kOutput, calls=%fused_computation.31 | convolution fusion | flops 10873405440 | bytes 20054016 | tf_op jit(solution)/shard_map/dot_general | solution.py:48
  644.9 7.1 fusion.62
  654.1 7.6 middle_back.5
  667.1 36.2 %attend_back.3 = (bf16[576,768]{1,0:T(8,128)(2,1)S(1)}, bf16[96,768]{1,0:T(8,128)(2,1)S(1)}, f32[6,2,128]{2,1,0:T(2,128)S(1)}, f32[6,2,128]{2,1,0:T(2,128)S(1)},...) custom-call(bf16[2,576,2304]{2,1,0:T(8,128)(2,1)} %bitcast.406, ...), custom_call_target="tpu_custom_call" | custom-call | flops 1 | bytes 1 | tf_op jit(solution)/shard_map/attend_back/pallas_call | solution.py:465
  708.1 9.3 fusion.43
  724.5 17.8 %collective-permute-done.18 = bf16[1152,1536]{1,0:T(8,128)(2,1)} collective-permute-done((bf16[1152,1536]{1,0:T(8,128)(2,1)}, bf16[1152,1536]{1,0:T(8,128)(2,1)}, u32[]{:S(2)}, u32[]{:S(2)}) %collective-permute-start.18) | collective-permute-done | bytes 3538976 | tf_op jit(solution)/shard_map/ppermute | solution.py:24
  746.5 5.6 multiply_reduce_fusion.1
  752.1 18.5 %weight_terms.2 = bf16[1536,3072]{1,0:T(8,128)(2,1)} custom-call(bf16[576,1536]{1,0:T(8,128)(2,1)} %bitcast.380, bf16[576,768]{1,0:T(8,128)(2,1)} %copy-done.31, bf16[576,1536]{1,0:T(8,128)(2,1)} %bitcast.382, bf16[576,768]{1,0:T(8,128)(2,1)} %copy-done.33, bf16[192,1536]{1,0:T(8,128)(2,1)S(1)} %bitcast.388, bf16[192,768]{1,0:T(8,128)(2,1)S(1)} %copy-done.84, ...), custom_call_target="tpu_custom_call" | custom-call | flops 1 | bytes 1 | tf_op jit(solution)/shard_map/weight_terms/pallas_call | solution.py:303
  771.7 16.7 %collective-permute-done.22 = bf16[2,576,768]{2,1,0:T(8,128)(2,1)} collective-permute-done((bf16[2,576,768]{2,1,0:T(8,128)(2,1)}, bf16[2,576,768]{2,1,0:T(8,128)(2,1)}, u32[]{:S(2)}, u32[]{:S(2)}) %collective-permute-start.22) | collective-permute-done | bytes 1769504 | tf_op jit(solution)/shard_map/ppermute | solution.py:24
  792.4 8.5 fusion.46
  801.0 6.3 fusion.59
  808.6 17.7 %weight_terms.3 = bf16[1536,3072]{1,0:T(8,128)(2,1)} custom-call(bf16[576,1536]{1,0:T(8,128)(2,1)} %get-tuple-element.163.refs_6_.refs_0_, bf16[576,1536]{1,0:T(8,128)(2,1)} %pad_maximum_fusion.3.refs_1_, bf16[576,1536]{1,0:T(8,128)(2,1)} %get-tuple-element.164.refs_8_.refs_2_, bf16[576,1536]{1,0:T(8,128)(2,1)} %pad_maximum_fusion.4.refs_3_, ...), custom_call_target="tpu_custom_call" | custom-call | flops 1 | bytes 1 | tf_op jit(solution)/shard_map/weight_terms/pallas_call | solution.py:303
  846.1 28.4 %collective-permute-done.23 = bf16[576,1536]{1,0:T(8,128)(2,1)} collective-permute-done((bf16[576,1536]{1,0:T(8,128)(2,1)}, bf16[576,1536]{1,0:T(8,128)(2,1)}, u32[]{:S(2)}, u32[]{:S(2)}) %collective-permute-start.23) | collective-permute-done | bytes 1769504 | tf_op jit(solution)/shard_map/ppermute | solution.py:24
  880.3 5.5 edge_back.3
  889.2 23.2 %collective-permute-done.24 = bf16[576,1536]{1,0:T(8,128)(2,1)} collective-permute-done((bf16[576,1536]{1,0:T(8,128)(2,1)}, bf16[576,1536]{1,0:T(8,128)(2,1)}, u32[]{:S(2)}, u32[]{:S(2)}) %collective-permute-start.24) | collective-permute-done | bytes 1769504 | tf_op jit(solution)/shard_map/ppermute | solution.py:24
  918.4 5.4 edge_back.4
  944.8 10.2 collective-permute-done.37
  955.0 24.3 %collective-permute-done.36 = bf16[96,3072]{1,0:T(8,128)(2,1)} collective-permute-done((bf16[96,3072]{1,0:T(8,128)(2,1)}, bf16[96,3072]{1,0:T(8,128)(2,1)}, u32[]{:S(2)}, u32[]{:S(2)}) %collective-permute-start.36) | collective-permute-done | bytes 589856 | tf_op jit(solution)/shard_map/ppermute | solution.py:72
  987.3 6.3 collective-permute-start.30
  999.0 17.3 %collective-permute-done.29 = bf16[2,33792]{1,0:T(2,128)(2,1)S(1)} collective-permute-done((bf16[2,33792]{1,0:T(2,128)(2,1)S(1)}, bf16[2,33792]{1,0:T(2,128)(2,1)S(1)}, u32[]{:S(2)}, u32[]{:S(2)}) %collective-permute-start.29) | collective-permute-done | bytes 135200 | tf_op jit(solution)/shard_map/ppermute | solution.py:72
  1048.2 16.0 %collective-permute-done.40 = bf16[96,3072]{1,0:T(8,128)(2,1)} collective-permute-done((bf16[96,3072]{1,0:T(8,128)(2,1)}, bf16[96,3072]{1,0:T(8,128)(2,1)}, u32[]{:S(2)}, u32[]{:S(2)}) %collective-permute-start.40) | collective-permute-done | bytes 589856 | tf_op jit(solution)/shard_map/ppermute | solution.py:24
  1066.9 14.9 %collective-permute-done.39 = bf16[96,3072]{1,0:T(8,128)(2,1)S(1)} collective-permute-done((bf16[96,3072]{1,0:T(8,128)(2,1)}, bf16[96,3072]{1,0:T(8,128)(2,1)S(1)}, u32[]{:S(2)}, u32[]{:S(2)}) %collective-permute-start.39) | collective-permute-done | bytes 589856 | tf_op jit(solution)/shard_map/ppermute | solution.py:24
  1088.8 10.7 collective-permute-done.34
  1104.8 7.4 collective-permute-done.33
  1114.1 8.4 collective-permute-done.32
  (697 shorter events, 345.1 us)
Async XLA Ops:
  7.2 120.1 %all-gather.8.cloned.1.call-start = ((), (), s32[]{:S(2)}) async-start(), calls=%async_computation.5 | async-start | bytes 15040512 | tf_op jit(solution)/shard_map/all_gather | solution.py:60
  10.5 214.8 %all-gather.10.cloned.1.call-start = ((), (), s32[]{:S(2)}) async-start(), calls=%async_computation.11 | async-start | bytes 5013504 | tf_op jit(solution)/shard_map/all_gather | solution.py:60
  12.2 360.5 %all-gather.12.cloned.1.call-start = ((), (), s32[]{:S(2)}) async-start(), calls=%async_computation.12 | async-start | bytes 20054016 | tf_op jit(solution)/shard_map/all_gather | solution.py:60
  14.7 430.3 %all-gather.14.cloned.1.call-start = ((), (), s32[]{:S(2)}) async-start(), calls=%async_computation.13 | async-start | bytes 20054016 | tf_op jit(solution)/shard_map/all_gather | solution.py:60
  17.1 1026.7 %reduce-scatter.14.cloned.1.call-start = ((), (), s32[]{:S(2)}) async-start(), calls=%async_computation.10 | async-start | bytes 10027008 | tf_op jit(solution)/shard_map/reduce_scatter | solution.py:67
  23.7 30.3 %collective-permute-start = (f32[4,2,2,4608]{3,2,1,0:T(2,128)}, f32[4,2,2,4608]{3,2,1,0:T(2,128)}, u32[]{:S(2)}, u32[]{:S(2)}) collective-permute-start(f32[4,2,2,4608]{3,2,1,0:T(2,128)} %bitcast.357), channel_id=1, source_target_pairs={{0,4},{4,0},{1,5},{5,1},{2,6},{6,2},{3,7},{7,3},{8,12},{12,8},{9,1... | collective-permute-start | bytes 884744 | tf_op jit(solution)/shard_map/ppermute | solution.py:24
  55.4 7.8 collective-permute-start.1
  58.1 8.5 collective-permute-start.3
  60.3 15.4 %collective-permute-start.2 = (f32[2,2,4608]{2,1,0:T(2,128)S(1)}, f32[2,2,4608]{2,1,0:T(2,128)S(1)}, u32[]{:S(2)}, u32[]{:S(2)}) collective-permute-start(f32[2,2,4608]{2,1,0:T(2,128)S(1)} %get-tuple-element.268), channel_id=1, source_target_pairs={{0,16},{8,24},{16,0},{24,8},{1,17},{9,25},{17,1},{25,9},{2,18},{10... | collective-permute-start | bytes 221192 | tf_op jit(solution)/shard_map/ppermute | solution.py:72
  142.4 60.4 %collective-permute-start.5 = (bf16[576,1536]{1,0:T(8,128)(2,1)S(1)}, bf16[576,1536]{1,0:T(8,128)(2,1)S(1)}, u32[]{:S(2)}, u32[]{:S(2)}) collective-permute-start(bf16[576,1536]{1,0:T(8,128)(2,1)S(1)} %get-tuple-element.216), channel_id=1, source_target_pairs={{0,2},{2,0},{1,3},{3,1},{4,6},{6,4},{5,7},{7,5},{8,10},{10,8},{9,1... | collective-permute-start | bytes 5308424 | tf_op jit(solution)/shard_map/ppermute | solution.py:24
  150.1 52.7 %collective-permute-start.6 = (bf16[96,1536]{1,0:T(8,128)(2,1)S(1)}, bf16[96,1536]{1,0:T(8,128)(2,1)S(1)}, u32[]{:S(2)}, u32[]{:S(2)}) collective-permute-start(bf16[96,1536]{1,0:T(8,128)(2,1)S(1)} %get-tuple-element.255), channel_id=1, source_target_pairs={{0,2},{2,0},{1,3},{3,1},{4,6},{6,4},{5,7},{7,5},{8,10},{10,8},{9,1... | collective-permute-start | bytes 884744 | tf_op jit(solution)/shard_map/ppermute | solution.py:24
  152.0 136.3 %collective-permute-start.8 = (bf16[576,1536]{1,0:T(8,128)(2,1)}, bf16[576,1536]{1,0:T(8,128)(2,1)}, u32[]{:S(2)}, u32[]{:S(2)}) collective-permute-start(bf16[576,1536]{1,0:T(8,128)(2,1)} %get-tuple-element.215), channel_id=1, source_target_pairs={{0,2},{2,0},{1,3},{3,1},{4,6},{6,4},{5,7},{7,5},{8,10},{10,8},{9,1... | collective-permute-start | bytes 5308424 | tf_op jit(solution)/shard_map/ppermute | solution.py:24
  229.1 39.4 %collective-permute-start.7 = (bf16[576,1536]{1,0:T(8,128)(2,1)S(1)}, bf16[576,1536]{1,0:T(8,128)(2,1)S(1)}, u32[]{:S(2)}, u32[]{:S(2)}) collective-permute-start(bf16[576,1536]{1,0:T(8,128)(2,1)S(1)} %convolution_convert_fusion.5), channel_id=1, source_target_pairs={{0,1},{1,0},{2,3},{3,2},{4,5},{5,4},{6,7},{7,6},{8,9},{9,8},{10,11... | collective-permute-start | bytes 5308424 | tf_op jit(solution)/shard_map/ppermute | solution.py:24
  231.5 56.7 %collective-permute-start.9 = (bf16[96,1536]{1,0:T(8,128)(2,1)S(1)}, bf16[96,1536]{1,0:T(8,128)(2,1)S(1)}, u32[]{:S(2)}, u32[]{:S(2)}) collective-permute-start(bf16[96,1536]{1,0:T(8,128)(2,1)S(1)} %copy-done.147), channel_id=1, source_target_pairs={{0,2},{2,0},{1,3},{3,1},{4,6},{6,4},{5,7},{7,5},{8,10},{10,8},{9,1... | collective-permute-start | bytes 884744 | tf_op jit(solution)/shard_map/ppermute | solution.py:24
  310.8 54.9 %collective-permute-start.10 = (bf16[576,1536]{1,0:T(8,128)(2,1)S(1)}, bf16[576,1536]{1,0:T(8,128)(2,1)S(1)}, u32[]{:S(2)}, u32[]{:S(2)}) collective-permute-start(bf16[576,1536]{1,0:T(8,128)(2,1)S(1)} %convolution_convert_fusion.4), channel_id=1, source_target_pairs={{0,1},{1,0},{2,3},{3,2},{4,5},{5,4},{6,7},{7,6},{8,9},{9,8},{10,11... | collective-permute-start | bytes 5308424 | tf_op jit(solution)/shard_map/ppermute | solution.py:24
  320.9 41.1 %collective-permute-start.11 = (bf16[192,1536]{1,0:T(8,128)(2,1)S(1)}, bf16[192,1536]{1,0:T(8,128)(2,1)S(1)}, u32[]{:S(2)}, u32[]{:S(2)}) collective-permute-start(bf16[192,1536]{1,0:T(8,128)(2,1)S(1)} %convolution_convert_fusion.6), channel_id=1, source_target_pairs={{0,1},{1,0},{2,3},{3,2},{4,5},{5,4},{6,7},{7,6},{8,9},{9,8},{10,11... | collective-permute-start | bytes 1769480 | tf_op jit(solution)/shard_map/ppermute | solution.py:24
  427.8 619.1 %reduce-scatter.12.cloned.1.call-start = ((), (), s32[]{:S(2)}) async-start(), calls=%async_computation.9 | async-start | bytes 10027008 | tf_op jit(solution)/shard_map/reduce_scatter | solution.py:67
  444.5 638.4 %reduce-scatter.10.cloned.1.call-start = ((), (), s32[]{:S(2)}) async-start(), calls=%async_computation.8 | async-start | bytes 10027008 | tf_op jit(solution)/shard_map/reduce_scatter | solution.py:67
  463.3 112.2 %collective-permute-start.14 = (bf16[192,1536]{1,0:T(8,128)(2,1)}, bf16[192,1536]{1,0:T(8,128)(2,1)}, u32[]{:S(2)}, u32[]{:S(2)}) collective-permute-start(bf16[192,1536]{1,0:T(8,128)(2,1)} %fusion.63), channel_id=1, source_target_pairs={{0,1},{1,0},{2,3},{3,2},{4,5},{5,4},{6,7},{7,6},{8,9},{9,8},{10,11... | collective-permute-start | bytes 1769480 | tf_op jit(solution)/shard_map/ppermute | solution.py:24
  477.9 50.3 %collective-permute-start.12 = (bf16[4,192,3072]{2,1,0:T(8,128)(2,1)}, bf16[4,192,3072]{2,1,0:T(8,128)(2,1)}, u32[]{:S(2)}, u32[]{:S(2)}) collective-permute-start(bf16[4,192,3072]{2,1,0:T(8,128)(2,1)} %get-tuple-element.209), channel_id=1, source_target_pairs={{0,4},{4,0},{1,5},{5,1},{2,6},{6,2},{3,7},{7,3},{8,12},{12,8},{9,1... | collective-permute-start | bytes 14155784 | tf_op jit(solution)/shard_map/ppermute | solution.py:24
  516.8 41.7 %collective-permute-start.13 = (bf16[576,1536]{1,0:T(8,128)(2,1)}, bf16[576,1536]{1,0:T(8,128)(2,1)}, u32[]{:S(2)}, u32[]{:S(2)}) collective-permute-start(bf16[576,1536]{1,0:T(8,128)(2,1)} %fusion.41), channel_id=1, source_target_pairs={{0,1},{1,0},{2,3},{3,2},{4,5},{5,4},{6,7},{7,6},{8,9},{9,8},{10,11... | collective-permute-start | bytes 5308424 | tf_op jit(solution)/shard_map/ppermute | solution.py:24
  526.1 127.9 %collective-permute-start.16 = (bf16[576,1536]{1,0:T(8,128)(2,1)}, bf16[576,1536]{1,0:T(8,128)(2,1)}, u32[]{:S(2)}, u32[]{:S(2)}) collective-permute-start(bf16[576,1536]{1,0:T(8,128)(2,1)} %fusion.42), channel_id=1, source_target_pairs={{0,1},{1,0},{2,3},{3,2},{4,5},{5,4},{6,7},{7,6},{8,9},{9,8},{10,11... | collective-permute-start | bytes 5308424 | tf_op jit(solution)/shard_map/ppermute | solution.py:24
  535.6 87.4 %collective-permute-start.15 = (bf16[4,96,3072]{2,1,0:T(8,128)(2,1)}, bf16[4,96,3072]{2,1,0:T(8,128)(2,1)}, u32[]{:S(2)}, u32[]{:S(2)}) collective-permute-start(bf16[4,96,3072]{2,1,0:T(8,128)(2,1)} %get-tuple-element.218), channel_id=1, source_target_pairs={{0,2},{2,0},{1,3},{3,1},{4,6},{6,4},{5,7},{7,5},{8,10},{10,8},{9,1... | collective-permute-start | bytes 7077896 | tf_op jit(solution)/shard_map/ppermute | solution.py:24
  620.7 82.6 %collective-permute-start.20 = (bf16[2,96,768]{2,1,0:T(8,128)(2,1)}, bf16[2,96,768]{2,1,0:T(8,128)(2,1)}, u32[]{:S(2)}, u32[]{:S(2)}) collective-permute-start(bf16[2,96,768]{2,1,0:T(8,128)(2,1)} %get-tuple-element.151), channel_id=1, source_target_pairs={{0,2},{2,0},{1,3},{3,1},{4,6},{6,4},{5,7},{7,5},{8,10},{10,8},{9,1... | collective-permute-start | bytes 884744 | tf_op jit(solution)/shard_map/ppermute | solution.py:24
  622.9 81.8 %collective-permute-start.17 = (bf16[2,576,768]{2,1,0:T(8,128)(2,1)}, bf16[2,576,768]{2,1,0:T(8,128)(2,1)}, u32[]{:S(2)}, u32[]{:S(2)}) collective-permute-start(bf16[2,576,768]{2,1,0:T(8,128)(2,1)} %get-tuple-element.145), channel_id=1, source_target_pairs={{0,2},{2,0},{1,3},{3,1},{4,6},{6,4},{5,7},{7,5},{8,10},{10,8},{9,1... | collective-permute-start | bytes 5308424 | tf_op jit(solution)/shard_map/ppermute | solution.py:24
  622.9 465.0 %reduce-scatter.8.cloned.1.call-start = ((), (), s32[]{:S(2)}) async-start(), calls=%async_computation.7 | async-start | bytes 10027008 | tf_op jit(solution)/shard_map/reduce_scatter | solution.py:67
  652.0 69.9 %collective-permute-start.19 = (bf16[192,1536]{1,0:T(8,128)(2,1)S(1)}, bf16[192,1536]{1,0:T(8,128)(2,1)S(1)}, u32[]{:S(2)}, u32[]{:S(2)}) collective-permute-start(bf16[192,1536]{1,0:T(8,128)(2,1)S(1)} %fusion.62), channel_id=1, source_target_pairs={{0,1},{1,0},{2,3},{3,2},{4,5},{5,4},{6,7},{7,6},{8,9},{9,8},{10,11... | collective-permute-start | bytes 1769480 | tf_op jit(solution)/shard_map/ppermute | solution.py:24
  653.0 89.3 %collective-permute-start.18 = (bf16[1152,1536]{1,0:T(8,128)(2,1)}, bf16[1152,1536]{1,0:T(8,128)(2,1)}, u32[]{:S(2)}, u32[]{:S(2)}) collective-permute-start(bf16[1152,1536]{1,0:T(8,128)(2,1)} %fusion.15), channel_id=1, source_target_pairs={{0,1},{1,0},{2,3},{3,2},{4,5},{5,4},{6,7},{7,6},{8,9},{9,8},{10,11... | collective-permute-start | bytes 10616840 | tf_op jit(solution)/shard_map/ppermute | solution.py:24
  717.5 53.1 %collective-permute-start.21 = (bf16[2,96,768]{2,1,0:T(8,128)(2,1)}, bf16[2,96,768]{2,1,0:T(8,128)(2,1)}, u32[]{:S(2)}, u32[]{:S(2)}) collective-permute-start(bf16[2,96,768]{2,1,0:T(8,128)(2,1)} %get-tuple-element.158), channel_id=1, source_target_pairs={{0,2},{2,0},{1,3},{3,1},{4,6},{6,4},{5,7},{7,5},{8,10},{10,8},{9,1... | collective-permute-start | bytes 884744 | tf_op jit(solution)/shard_map/ppermute | solution.py:24
  719.6 68.8 %collective-permute-start.22 = (bf16[2,576,768]{2,1,0:T(8,128)(2,1)}, bf16[2,576,768]{2,1,0:T(8,128)(2,1)}, u32[]{:S(2)}, u32[]{:S(2)}) collective-permute-start(bf16[2,576,768]{2,1,0:T(8,128)(2,1)} %get-tuple-element.161), channel_id=1, source_target_pairs={{0,2},{2,0},{1,3},{3,1},{4,6},{6,4},{5,7},{7,5},{8,10},{10,8},{9,1... | collective-permute-start | bytes 5308424 | tf_op jit(solution)/shard_map/ppermute | solution.py:24
  826.3 277.3 %reduce-scatter.6.cloned.1.call-start = ((), (), s32[]{:S(2)}) async-start(), calls=%async_computation.6 | async-start | bytes 10027008 | tf_op jit(solution)/shard_map/reduce_scatter | solution.py:67
  832.6 41.9 %collective-permute-start.23 = (bf16[576,1536]{1,0:T(8,128)(2,1)}, bf16[576,1536]{1,0:T(8,128)(2,1)}, u32[]{:S(2)}, u32[]{:S(2)}) collective-permute-start(bf16[576,1536]{1,0:T(8,128)(2,1)} %fusion.43), channel_id=1, source_target_pairs={{0,1},{1,0},{2,3},{3,2},{4,5},{5,4},{6,7},{7,6},{8,9},{9,8},{10,11... | collective-permute-start | bytes 5308424 | tf_op jit(solution)/shard_map/ppermute | solution.py:24
  837.2 75.2 %collective-permute-start.24 = (bf16[576,1536]{1,0:T(8,128)(2,1)}, bf16[576,1536]{1,0:T(8,128)(2,1)}, u32[]{:S(2)}, u32[]{:S(2)}) collective-permute-start(bf16[576,1536]{1,0:T(8,128)(2,1)} %fusion.46), channel_id=1, source_target_pairs={{0,1},{1,0},{2,3},{3,2},{4,5},{5,4},{6,7},{7,6},{8,9},{9,8},{10,11... | collective-permute-start | bytes 5308424 | tf_op jit(solution)/shard_map/ppermute | solution.py:24
  845.7 78.3 %collective-permute-start.25 = (bf16[192,1536]{1,0:T(8,128)(2,1)}, bf16[192,1536]{1,0:T(8,128)(2,1)}, u32[]{:S(2)}, u32[]{:S(2)}) collective-permute-start(bf16[192,1536]{1,0:T(8,128)(2,1)} %fusion.59), channel_id=1, source_target_pairs={{0,1},{1,0},{2,3},{3,2},{4,5},{5,4},{6,7},{7,6},{8,9},{9,8},{10,11... | collective-permute-start | bytes 1769480 | tf_op jit(solution)/shard_map/ppermute | solution.py:24
  940.7 14.3 %collective-permute-start.37 = (bf16[96,3072]{1,0:T(8,128)(2,1)}, bf16[96,3072]{1,0:T(8,128)(2,1)}, u32[]{:S(2)}, u32[]{:S(2)}) collective-permute-start(bf16[96,3072]{1,0:T(8,128)(2,1)} %get-tuple-element.226), channel_id=1, source_target_pairs={{0,24},{8,0},{16,8},{24,16},{1,25},{9,1},{17,9},{25,17},{2,26},{10... | collective-permute-start | bytes 1769480 | tf_op jit(solution)/shard_map/ppermute | solution.py:72
  940.7 38.6 %collective-permute-start.36 = (bf16[96,3072]{1,0:T(8,128)(2,1)}, bf16[96,3072]{1,0:T(8,128)(2,1)}, u32[]{:S(2)}, u32[]{:S(2)}) collective-permute-start(bf16[96,3072]{1,0:T(8,128)(2,1)} %get-tuple-element.227), channel_id=1, source_target_pairs={{0,16},{8,24},{16,0},{24,8},{1,17},{9,25},{17,1},{25,9},{2,18},{10... | collective-permute-start | bytes 1769480 | tf_op jit(solution)/shard_map/ppermute | solution.py:72
  940.7 38.6 %collective-permute-start.35 = (bf16[96,3072]{1,0:T(8,128)(2,1)}, bf16[96,3072]{1,0:T(8,128)(2,1)}, u32[]{:S(2)}, u32[]{:S(2)}) collective-permute-start(bf16[96,3072]{1,0:T(8,128)(2,1)} %get-tuple-element.228), channel_id=1, source_target_pairs={{0,8},{8,16},{16,24},{24,0},{1,9},{9,17},{17,25},{25,1},{2,10},{10... | collective-permute-start | bytes 1769480 | tf_op jit(solution)/shard_map/ppermute | solution.py:72
  944.7 37.6 %collective-permute-start.27 = (bf16[33792]{0:T(1024)(128)(2,1)S(1)}, bf16[33792]{0:T(1024)(128)(2,1)S(1)}, u32[]{:S(2)}, u32[]{:S(2)}) collective-permute-start(bf16[33792]{0:T(1024)(128)(2,1)S(1)} %add_convert_fusion.7), channel_id=1, source_target_pairs={{0,4},{4,0},{1,5},{5,1},{2,6},{6,2},{3,7},{7,3},{8,12},{12,8},{9,1... | collective-permute-start | bytes 202760 | tf_op jit(solution)/shard_map/ppermute | solution.py:24
  982.9 16.0 %collective-permute-start.28 = (bf16[2,33792]{1,0:T(2,128)(2,1)S(1)}, bf16[2,33792]{1,0:T(2,128)(2,1)S(1)}, u32[]{:S(2)}, u32[]{:S(2)}) collective-permute-start(bf16[2,33792]{1,0:T(2,128)(2,1)S(1)} %get-tuple-element.205), channel_id=1, source_target_pairs={{0,24},{8,0},{16,8},{24,16},{1,25},{9,1},{17,9},{25,17},{2,26},{10... | collective-permute-start | bytes 405512 | tf_op jit(solution)/shard_map/ppermute | solution.py:72
  985.9 58.7 %collective-permute-start.38 = (bf16[96,3072]{1,0:T(8,128)(2,1)}, bf16[96,3072]{1,0:T(8,128)(2,1)}, u32[]{:S(2)}, u32[]{:S(2)}) collective-permute-start(bf16[96,3072]{1,0:T(8,128)(2,1)} %add_convert_fusion.4), channel_id=1, source_target_pairs={{0,2},{2,0},{1,3},{3,1},{4,6},{6,4},{5,7},{7,5},{8,10},{10,8},{9,1... | collective-permute-start | bytes 1769480 | tf_op jit(solution)/shard_map/ppermute | solution.py:24
  987.3 29.2 %collective-permute-start.30 = (bf16[2,33792]{1,0:T(2,128)(2,1)S(1)}, bf16[2,33792]{1,0:T(2,128)(2,1)S(1)}, u32[]{:S(2)}, u32[]{:S(2)}) collective-permute-start(bf16[2,33792]{1,0:T(2,128)(2,1)S(1)} %get-tuple-element.205), channel_id=1, source_target_pairs={{0,8},{8,16},{16,24},{24,0},{1,9},{9,17},{17,25},{25,1},{2,10},{10... | collective-permute-start | bytes 405512 | tf_op jit(solution)/shard_map/ppermute | solution.py:72
  993.6 22.8 %collective-permute-start.29 = (bf16[2,33792]{1,0:T(2,128)(2,1)S(1)}, bf16[2,33792]{1,0:T(2,128)(2,1)S(1)}, u32[]{:S(2)}, u32[]{:S(2)}) collective-permute-start(bf16[2,33792]{1,0:T(2,128)(2,1)S(1)} %get-tuple-element.205), channel_id=1, source_target_pairs={{0,16},{8,24},{16,0},{24,8},{1,17},{9,25},{17,1},{25,9},{2,18},{10... | collective-permute-start | bytes 405512 | tf_op jit(solution)/shard_map/ppermute | solution.py:72
  1031.9 10.6 collective-permute-start.31
  1043.8 20.4 %collective-permute-start.40 = (bf16[96,3072]{1,0:T(8,128)(2,1)}, bf16[96,3072]{1,0:T(8,128)(2,1)}, u32[]{:S(2)}, u32[]{:S(2)}) collective-permute-start(bf16[96,3072]{1,0:T(8,128)(2,1)} %reduce-scatter.14.cloned.1.call-done), channel_id=1, source_target_pairs={{0,2},{2,0},{1,3},{3,1},{4,6},{6,4},{5,7},{7,5},{8,10},{10,8},{9,1... | collective-permute-start | bytes 1769480 | tf_op jit(solution)/shard_map/ppermute | solution.py:24
  1046.9 34.9 %collective-permute-start.39 = (bf16[96,3072]{1,0:T(8,128)(2,1)}, bf16[96,3072]{1,0:T(8,128)(2,1)S(1)}, u32[]{:S(2)}, u32[]{:S(2)}) collective-permute-start(bf16[96,3072]{1,0:T(8,128)(2,1)} %reduce-scatter.12.cloned.1.call-done), channel_id=1, source_target_pairs={{0,2},{2,0},{1,3},{3,1},{4,6},{6,4},{5,7},{7,5},{8,10},{10,8},{9,1... | collective-permute-start | bytes 1769480 | tf_op jit(solution)/shard_map/ppermute | solution.py:24
  1082.9 16.6 %collective-permute-start.34 = (bf16[96,3072]{1,0:T(8,128)(2,1)}, bf16[96,3072]{1,0:T(8,128)(2,1)}, u32[]{:S(2)}, u32[]{:S(2)}) collective-permute-start(bf16[96,3072]{1,0:T(8,128)(2,1)} %reduce-scatter.10.cloned.1.call-done), channel_id=1, source_target_pairs={{0,2},{2,0},{1,3},{3,1},{4,6},{6,4},{5,7},{7,5},{8,10},{10,8},{9,1... | collective-permute-start | bytes 1769480 | tf_op jit(solution)/shard_map/ppermute | solution.py:24
  1087.9 24.2 %collective-permute-start.33 = (bf16[96,3072]{1,0:T(8,128)(2,1)}, bf16[96,3072]{1,0:T(8,128)(2,1)}, u32[]{:S(2)}, u32[]{:S(2)}) collective-permute-start(bf16[96,3072]{1,0:T(8,128)(2,1)} %reduce-scatter.8.cloned.1.call-done), channel_id=1, source_target_pairs={{0,2},{2,0},{1,3},{3,1},{4,6},{6,4},{5,7},{7,5},{8,10},{10,8},{9,1... | collective-permute-start | bytes 1769480 | tf_op jit(solution)/shard_map/ppermute | solution.py:24
  1103.6 18.9 %collective-permute-start.32 = (bf16[96,3072]{1,0:T(8,128)(2,1)}, bf16[96,3072]{1,0:T(8,128)(2,1)S(1)}, u32[]{:S(2)}, u32[]{:S(2)}) collective-permute-start(bf16[96,3072]{1,0:T(8,128)(2,1)} %reduce-scatter.6.cloned.1.call-done), channel_id=1, source_target_pairs={{0,2},{2,0},{1,3},{3,1},{4,6},{6,4},{5,7},{7,5},{8,10},{10,8},{9,1... | collective-permute-start | bytes 1769480 | tf_op jit(solution)/shard_map/ppermute | solution.py:24
  (200 other events, 2147.3 us)
Sparse Core Ops, SparseCore 0:
  10.9 116.3 all-gather.7
  130.2 65.5 all-gather.9
  198.0 138.5 all-gather.11
  338.0 98.2 all-gather.13
  440.2 115.9 reduce-scatter.13
  560.8 126.2 reduce-scatter.11
  691.2 126.6 reduce-scatter.9
  826.5 112.9 reduce-scatter.7
  943.7 146.8 reduce-scatter.5

commit v3 on v2

--- a/solution.py
+++ b/solution.py
@@ -62,9 +62,15 @@
     return lax.all_gather(shard.reshape(streams, rows, -1), FSDP, axis=1, tiled=True)
 
 
+def gather_over_fsdp(shard):
+    pair = jnp.concatenate([shard[0], shard[1]], axis=1)
+    whole = lax.all_gather(pair, FSDP, axis=0, tiled=True)
+    columns = shard.shape[2]
+    return whole[:, :columns], whole[:, columns:]
+
+
 def scatter_rows(part):
-    over = FSDP + ("ctx",) if lax.axis_size("ctx") == 2 else FSDP
-    return lax.psum_scatter(part.astype(BF16), over, scatter_dimension=0, tiled=True)
+    return lax.psum_scatter(part.astype(BF16), FSDP, scatter_dimension=0, tiled=True)
 
 
 def rotate(values, step):
@@ -102,17 +108,24 @@
     return add_low(after(keep, *ready), swap(give, "ctx"))
 
 
-def z_step(both, *ready):
+def z_step(both):
     if lax.axis_size("ctx") != 2:
         return both
-    count, z_index = lax.axis_size("z"), lax.axis_index("z")
-    keep = lax.dynamic_index_in_dim(both, z_index, 0, keepdims=False)
-    total = after(keep, *ready).astype(F32)
-    for step in range(1, count):
-        target = lax.rem(z_index + step, count)
-        given = lax.dynamic_index_in_dim(both, target, 0, keepdims=False)
-        total = total + rotate(given, step).astype(F32)
-    return total.astype(BF16)
+    return lax.psum_scatter(
+        both.reshape(-1, both.shape[2]), "z", scatter_dimension=0, tiled=True
+    )
+
+
+def ctx_given(mine):
+    if lax.axis_size("ctx") == 2:
+        return swap(mine, "ctx")
+    return lax.psum(mine, "ctx")
+
+
+def ctx_total(mine, given):
+    if lax.axis_size("ctx") == 2:
+        return mine.astype(F32) + given.astype(F32)
+    return given.astype(F32)
 
 
 def end_step(mine, *ready):
@@ -529,7 +542,7 @@
     width = qkv_weight.shape[3]
 
     qkv_full = gather_rows(qkv_weight)
-    out_full = gather_rows(jnp.swapaxes(attn_out_weight, 1, 2))
+    out_full = gather_over_fsdp(jnp.swapaxes(attn_out_weight, 1, 2))
     up_full = gather_rows(mlp_up_weight)
     down_full = gather_rows(jnp.swapaxes(mlp_down_weight, 1, 2))
 
@@ -717,10 +730,10 @@
         if stream == 0:
             up_chip = core_step([up_terms[1]], *ready)
             ready = (up_chip,)
-        up_terms[stream] = up_weight_term(stream, *ready)
-        ready = (up_terms[stream],)
+        else:
+            up_terms[stream] = up_weight_term(stream, *ready)
+            ready = (up_terms[stream],)
     down_shards = [scatter_rows(term) for term in down_terms]
-    up_shard = scatter_rows(after(up_terms[0], down_terms[1]))
 
     grad_middles, mid_sums, grad_att_low, grad_attended = {}, {}, {}, {}
 
@@ -749,7 +762,7 @@
     bias_sums = 0.0
     mlp_parts = []
     for slot in slots:
-        middle_back(slot, *ready)
+        middle_back(slot, *ready, *down_shards[slot : slot + 1])
         if slot == 0:
             middle_back(text_unit, grad_attended[slot])
             ready = (grad_attended[text_unit],)
@@ -782,11 +795,14 @@
                 )
                 given_pairs[slot, stream] = (total, jnp.zeros_like(total))
         if slot == 0:
-            up_both = ctx_step(up_chip, *ready)
+            up_terms[0] = up_weight_term(0, *ready)
+            up_shard = scatter_rows(up_terms[0])
+            ready = (up_terms[0],)
             for stream in range(2):
-                rows = after(activs[stream], up_both, *ready)
+                rows = after(activs[stream], *ready)
                 mlp_parts.append(dot_nt(rows, down_full[stream]).astype(BF16))
                 ready = (mlp_parts[stream],)
+            up_both = ctx_step(up_chip, *ready)
 
     pair_grads, hid_parts = {}, {}
 
@@ -816,19 +832,21 @@
         )
         finals.append(final.astype(BF16))
     ready = tuple(finals)
+    for slot in slots[1:]:
+        hid_part(slot, *ready)
+        ready = (hid_parts[slot],)
     groups = []
     for stream in range(2):
         members = list(slots) if stream == 0 else [text_unit]
-        groups.append([(after(grad_att_low[unit], *ready), attended[unit]) for unit in members])
+        groups.append(
+            [(after(grad_att_low[unit], *ready, up_shard), attended[unit]) for unit in members]
+        )
     for stream in range(2):
         normed = tall(stream, hidden_in[stream])
         groups.append([(normed[slot], query_grads[slot, stream]) for slot in slots])
     first_term = weight_terms(groups)
     first_shard = scatter_rows(first_term)
     ready = (first_term,)
-    for slot in slots[1:]:
-        hid_part(slot, *ready)
-        ready = (hid_parts[slot],)
     text_rows_grad = jnp.concatenate(
         [
             jnp.concatenate([query_grads[slot, 1], pair_grads[slot, 1]], axis=1)
@@ -846,7 +864,10 @@
         )
     second_term = weight_terms(groups)
     second_shard = scatter_rows(second_term)
-    ready = (second_term,)
+    up_mine = z_step(up_both)
+    down_given = [ctx_given(after(shard, second_term)) for shard in down_shards]
+    up_given = ctx_given(after(up_shard, second_term))
+    ready = (second_term, up_mine, up_given, down_given[0])
     input_grads, edge_sums = {}, {}
     for unit in list(slots) + [text_unit]:
         other = swap(hid_parts[unit], "tp")
@@ -864,16 +885,11 @@
             [BF16],
             True,
         )
-        ready = (input_grads[unit],)
-    up_mine = z_step(up_both, *ready)
-    down_grads = [end_step(shard, *ready) for shard in down_shards]
-    up_grads = [end_step(up_shard, *ready), end_step(up_mine)]
-    first_grads = end_step(first_shard)
-    second_grads = end_step(second_shard)
-    out_grads = [first_grads[:, :width], first_grads[:, width : 2 * width]]
-    q_weight_grads = [first_grads[:, 2 * width : 3 * width], first_grads[:, 3 * width :]]
-    kv_weight_grads = [second_grads[:, : 2 * width], second_grads[:, 2 * width :]]
-
+        ready = (input_grads[unit], down_given[1])
+    first_given = ctx_given(first_shard)
+    down_grads = [ctx_total(*pair) for pair in zip(down_shards, down_given)]
+    up_grads = [ctx_total(up_shard, up_given), end_step(up_mine)]
+    first_grads = ctx_total(first_shard, first_given)
     def by_slot(values):
         image = jnp.concatenate([values[slot] for slot in slots], axis=0)
         return jnp.stack([image, values[text_unit]], axis=1)
@@ -906,8 +922,15 @@
         jnp.stack(out_bias_sums, axis=0),
         jnp.stack(down_bias_grads, axis=0),
     )
-    row = ctx_sum(jnp.concatenate([piece.reshape(-1) for piece in pieces], axis=0))
-    everyone = gather_groups(row.astype(BF16)).astype(F32)
+    row = jnp.concatenate([piece.reshape(-1) for piece in pieces], axis=0).astype(BF16)
+    row = ctx_sum(row)
+    gathered = gather_groups(after(row.astype(BF16), first_shard))
+    second_shard = after(second_shard, gathered)
+    second_grads = ctx_total(second_shard, ctx_given(second_shard))
+    out_grads = [first_grads[:, :width], first_grads[:, width : 2 * width]]
+    q_weight_grads = [first_grads[:, 2 * width : 3 * width], first_grads[:, 3 * width :]]
+    kv_weight_grads = [second_grads[:, : 2 * width], second_grads[:, 2 * width :]]
+    everyone = gathered.astype(F32)
     ends = []
     base = 0
     for piece in pieces:

time: 1140 us -> 1080 us (0.947)
  waiting for transfers between devices: 389 us -> 340 us
  starting transfers between devices: 54.5 us -> 37.1 us
    ppermute x9 -> x6, waiting for transfers between devices: 66.3 us -> 25.8 us  [rotate(): lax.ppermute(values, 'z', [(index, (index + step) % count) for index in r...]
    ppermute x32, waiting for transfers between devices: 286 us -> 256 us  [swap(): return lax.ppermute(values, axis, PAIR)]
    all_gather x4 -> x3, waiting for transfers between devices: 36.6 us -> 50.7 us  [gather_rows(): whole = lax.all_gather(piece, ('ctx',) + FSDP, axis=0, tiled=True)]
    unnamed x413 -> x435, local copies, waits for them, and re-layouts: 54.8 us -> 59.1 us
  transfers between devices with their start and end apart: 50 -> 48, of which waited for: 22 -> 20; matrix products, arithmetic and copies ran while one was open for 39% -> 41% of each run, Pallas kernels for 16% -> 17%
where the time goes in v3:
time: 1080 us; the launch traced here: 1070 us
  waiting for transfers between devices  340 us (31%)
  matrix products  225 us (21%)
  Pallas kernels  182 us (17%)
  local copies, waits for them, and re-layouts  158 us (15%)
  other arithmetic  110 us (10%)
  starting transfers between devices  37.1 us (3%)
  between operations  16.8 us (2%)
    ppermute x32, waiting for transfers between devices, swap(): return lax.ppermute(values, axis, PAIR)  256 us
    dot_general x9, matrix products, dot(): lax.dot_general(left, right, (((1,), (0,)), ((), ())), preferred_element_...  88.5 us
    dot_general x11, matrix products, dot_nt(): lax.dot_general(left, right, (((1,), (1,)), ((), ())), preferred_element_...  83.6 us
    pallas_call x2, Pallas kernels, attend_back(): pl.pallas_call(functools.partial(attend_back_kernel, tuple((part[3] for p...  73.4 us
    unnamed x435, local copies, waits for them, and re-layouts  59.1 us
    all_gather x3, waiting for transfers between devices, gather_rows(): whole = lax.all_gather(piece, ('ctx',) + FSDP, axis=0, tiled=True)  50.7 us
    dot_general x4, matrix products, dot_tn(): lax.dot_general(left, right, (((0,), (0,)), ((), ())), preferred_element_...  45.2 us
    pallas_call x2, Pallas kernels, attend(): pl.pallas_call(functools.partial(attend_kernel, len(key_parts), image_row...  37 us
  transfers between devices with their start and end apart: 48, of which 20 were waited for; matrix products, arithmetic and copies ran while one was open for 41% of the time, Pallas kernels for 17%

profile of v3, /device:TPU:0, one launch (start us, length us, event | category | flops | bytes accessed | tf_op | source)
XLA Modules:
  0.0 1069.0 jit_solution(5131837031880339101)
XLA Ops:
  76.1 50.6 %all-gather.7.cloned.1.call-done = bf16[3072,2304]{1,0:T(8,128)(2,1)} async-done(((bf16[192,2304]{1,0:T(8,128)(2,1)}), bf16[3072,2304]{1,0:T(8,128)(2,1)}) %all-gather.7.cloned.1.call-update) | async-done | bytes 14155792 | tf_op jit(solution)/shard_map/all_gather | solution.py:60
  126.8 12.4 %fusion.6 = bf16[1152,2304]{1,0:T(8,128)(2,1)S(1)} fusion(bf16[1152,1536]{1,0:T(8,128)(2,1)} %bitcast.389, bf16[3072,2304]{1,0:T(8,128)(2,1)} %all-gather.7.cloned.1.call-done, f32[2304]{0:T(1024)} %get-tuple-element.297), kind=kOutput, calls=%fused_computation.11 | convolution fusion | flops 8159035392 | bytes 15937536 | tf_op jit(solution)/shard_map/dot_general | solution.py:44
  159.2 33.3 %collective-permute-done.6.refs_5_.refs_9_.refs_10_.refs_14_ = bf16[96,1536]{1,0:T(8,128)(2,1)} collective-permute-done((bf16[96,1536]{1,0:T(8,128)(2,1)}, bf16[96,1536]{1,0:T(8,128)(2,1)}, u32[]{:S(2)}, u32[]{:S(2)}) %collective-permute-start.6) | collective-permute-done | bytes 294944 | tf_op jit(solution)/shard_map/ppermute | solution.py:24
  197.2 18.2 %attend.2 = (bf16[576,768]{1,0:T(8,128)(2,1)S(1)}, bf16[96,768]{1,0:T(8,128)(2,1)S(1)}, f32[6,1,1344]{2,1,0:T(1,128)S(1)}) custom-call(bf16[2,576,2304]{2,1,0:T(8,128)(2,1)} %bitcast.374, bf16[2,96,2304]{2,1,0:T(8,128)(2,1)S(1)} %bitcast.337, bf16[2,576,2304]{2,1,0:T(8,128)(2,1)} %bitcast.375, ...), custom_call_target="tpu_custom_call" | custom-call | flops 1 | bytes 1 | tf_op jit(solution)/shard_map/attend/pallas_call | solution.py:443
  225.1 34.4 %collective-permute-done.7 = bf16[576,1536]{1,0:T(8,128)(2,1)S(1)} collective-permute-done((bf16[576,1536]{1,0:T(8,128)(2,1)S(1)}, bf16[576,1536]{1,0:T(8,128)(2,1)S(1)}, u32[]{:S(2)}, u32[]{:S(2)}) %collective-permute-start.7) | collective-permute-done | bytes 1769504 | tf_op jit(solution)/shard_map/ppermute | solution.py:24
  265.3 14.9 %collective-permute-done.9.refs_5_.refs_9_.refs_10_.refs_14_ = bf16[96,1536]{1,0:T(8,128)(2,1)S(1)} collective-permute-done((bf16[96,1536]{1,0:T(8,128)(2,1)S(1)}, bf16[96,1536]{1,0:T(8,128)(2,1)S(1)}, u32[]{:S(2)}, u32[]{:S(2)}) %collective-permute-start.9) | collective-permute-done | bytes 294944 | tf_op jit(solution)/shard_map/ppermute | solution.py:24
  280.3 18.8 %attend.3 = (bf16[576,768]{1,0:T(8,128)(2,1)S(1)}, bf16[96,768]{1,0:T(8,128)(2,1)S(1)}, f32[6,1,1344]{2,1,0:T(1,128)S(1)}) custom-call(bf16[2,576,2304]{2,1,0:T(8,128)(2,1)} %bitcast.377, bf16[2,96,2304]{2,1,0:T(8,128)(2,1)S(1)} %bitcast.340, bf16[2,576,2304]{2,1,0:T(8,128)(2,1)} %bitcast.378, ...), custom_call_target="tpu_custom_call" | custom-call | flops 1 | bytes 1 | tf_op jit(solution)/shard_map/attend/pallas_call | solution.py:443
  308.2 5.2 multiply_multiply_fusion.2
  313.4 40.9 %collective-permute-done.11 = bf16[192,1536]{1,0:T(8,128)(2,1)S(1)} collective-permute-done((bf16[192,1536]{1,0:T(8,128)(2,1)S(1)}, bf16[192,1536]{1,0:T(8,128)(2,1)S(1)}, u32[]{:S(2)}, u32[]{:S(2)}) %collective-permute-start.11) | collective-permute-done | bytes 589856 | tf_op jit(solution)/shard_map/ppermute | solution.py:24
  364.9 8.4 multiply_convert_fusion.2
  373.4 21.1 %multiply_convert_fusion = (bf16[1152,3072]{1,0:T(8,128)(2,1)}, f32[1152,3072]{1,0:T(8,128)}) fusion(f32[3072]{0:T(1024)S(1)} %bitcast.407, bf16[1,3072,3072]{2,1,0:T(8,128)(2,1)} %all-gather.11.cloned.1.call-done, bf16[576,1536]{1,0:T(8,128)(2,1)S(1)} %bitcast.351, bf16[576,1536]{1,0:T(8,128)(2,1)S(1)} %bitcast.349), kind=kOutput, calls=%fused_computation.8 | convolution fusion | flops 10914103296 | bytes 34222080 | tf_op jit(solution)/shard_map/dot_general | solution.py:44
  394.5 17.7 %convolution_convert_fusion.3 = bf16[1536,3072]{1,0:T(8,128)(2,1)} fusion(bf16[1152,1536]{1,0:T(8,128)(2,1)S(1)} %bitcast.400, bf16[1152,3072]{1,0:T(8,128)(2,1)} %get-tuple-element.134), kind=kOutput, calls=%fused_computation.15 | convolution fusion | flops 10876354560 | bytes 20054016 | tf_op jit(solution)/shard_map/dot_general | solution.py:52
  422.0 6.7 fusion.130
  430.7 8.9 fusion.134
  439.6 7.9 fusion.63
  449.3 5.5 convolution_convert_fusion.1
  454.8 7.0 dynamic-slice_bitcast_fusion.1
  461.8 24.6 %fusion.129 = (bf16[3072]{0:T(1024)(128)(2,1)}, bf16[1152,3072]{1,0:T(8,128)(2,1)S(1)}) fusion(f32[1152,3072]{1,0:T(8,128)} %get-tuple-element.305, bf16[1152,1536]{1,0:T(8,128)(2,1)} %bitcast.399, bf16[1,3072,3072]{2,1,0:T(8,128)(2,1)} %all-gather.13.cloned.1.call-done), kind=kOutput, calls=%fused_computation.329 | convolution fusion | flops 10945950720 | bytes 34215936 | tf_op jit(solution)/shard_map/dot_general | solution.py:44
  490.3 10.4 fusion.41
  501.1 9.8 fusion.42
  510.9 6.5 add_convert_fusion
  517.4 7.3 reduce-scatter.7.cloned.1.call-done
  524.7 17.4 %collective-permute-done.13 = bf16[576,1536]{1,0:T(8,128)(2,1)} collective-permute-done((bf16[576,1536]{1,0:T(8,128)(2,1)}, bf16[576,1536]{1,0:T(8,128)(2,1)}, u32[]{:S(2)}, u32[]{:S(2)}) %collective-permute-start.13) | collective-permute-done | bytes 1769504 | tf_op jit(solution)/shard_map/ppermute | solution.py:24
  544.9 7.6 middle_back.3
  564.8 36.8 %attend_back.2 = (bf16[576,768]{1,0:T(8,128)(2,1)S(1)}, bf16[96,768]{1,0:T(8,128)(2,1)S(1)}, f32[6,2,128]{2,1,0:T(2,128)S(1)}, f32[6,2,128]{2,1,0:T(2,128)S(1)},...) custom-call(bf16[2,576,2304]{2,1,0:T(8,128)(2,1)} %bitcast.380, ...), custom_call_target="tpu_custom_call" | custom-call | flops 1 | bytes 1 | tf_op jit(solution)/shard_map/attend_back/pallas_call | solution.py:478
  604.6 16.8 %convolution_convert_fusion = bf16[1536,3072]{1,0:T(8,128)(2,1)} fusion(bf16[1152,1536]{1,0:T(8,128)(2,1)} %pad_maximum_fusion.2, bf16[1152,3072]{1,0:T(8,128)(2,1)S(1)} %bitcast.392), kind=kOutput, calls=%fused_computation.12 | convolution fusion | flops 10876354560 | bytes 20054016 | tf_op jit(solution)/shard_map/dot_general | solution.py:52
  630.2 5.8 dynamic-slice_bitcast_fusion.3
  637.3 17.6 %fusion.15 = bf16[1152,1536]{1,0:T(8,128)(2,1)} fusion(bf16[1152,3072]{1,0:T(8,128)(2,1)} %get-tuple-element.134, bf16[1,3072,3072]{2,1,0:T(8,128)(2,1)} %all-gather.13.cloned.1.call-done), kind=kOutput, calls=%fused_computation.31 | convolution fusion | flops 10873405440 | bytes 20054016 | tf_op jit(solution)/shard_map/dot_general | solution.py:48
  661.9 10.1 collective-permute-done.15
  674.8 7.6 middle_back.5
  688.9 36.6 %attend_back.3 = (bf16[576,768]{1,0:T(8,128)(2,1)S(1)}, bf16[96,768]{1,0:T(8,128)(2,1)S(1)}, f32[6,2,128]{2,1,0:T(2,128)S(1)}, f32[6,2,128]{2,1,0:T(2,128)S(1)},...) custom-call(bf16[2,576,2304]{2,1,0:T(8,128)(2,1)} %bitcast.383, ...), custom_call_target="tpu_custom_call" | custom-call | flops 1 | bytes 1 | tf_op jit(solution)/shard_map/attend_back/pallas_call | solution.py:478
  734.5 8.6 fusion.43
  743.1 15.9 %collective-permute-done.18 = bf16[192,1536]{1,0:T(8,128)(2,1)} collective-permute-done((bf16[192,1536]{1,0:T(8,128)(2,1)}, bf16[192,1536]{1,0:T(8,128)(2,1)}, u32[]{:S(2)}, u32[]{:S(2)}) %collective-permute-start.18) | collective-permute-done | bytes 589856 | tf_op jit(solution)/shard_map/ppermute | solution.py:24
  768.8 5.5 multiply_reduce_fusion.1
  777.7 8.5 fusion.46
  792.0 18.1 %weight_terms.2 = bf16[1536,3072]{1,0:T(8,128)(2,1)} custom-call(bf16[576,1536]{1,0:T(8,128)(2,1)} %bitcast.357, bf16[576,768]{1,0:T(8,128)(2,1)} %copy-done.30, bf16[576,1536]{1,0:T(8,128)(2,1)} %bitcast.358, bf16[576,768]{1,0:T(8,128)(2,1)} %copy-done.32, bf16[192,1536]{1,0:T(8,128)(2,1)S(1)} %bitcast.364, bf16[192,768]{1,0:T(8,128)(2,1)S(1)} %copy-done.82, ...), custom_call_target="tpu_custom_call" | custom-call | flops 1 | bytes 1 | tf_op jit(solution)/shard_map/weight_terms/pallas_call | solution.py:316
  825.0 10.4 collective-permute-done.19
  848.9 6.7 fusion.59
  855.6 17.8 %weight_terms.3 = bf16[1536,3072]{1,0:T(8,128)(2,1)} custom-call(bf16[576,1536]{1,0:T(8,128)(2,1)} %get-tuple-element.162.refs_6_.refs_0_, bf16[576,1536]{1,0:T(8,128)(2,1)} %pad_maximum_fusion.5.refs_1_, bf16[576,1536]{1,0:T(8,128)(2,1)} %get-tuple-element.163.refs_8_.refs_2_, bf16[576,1536]{1,0:T(8,128)(2,1)} %pad_maximum_fusion.6.refs_3_, ...), custom_call_target="tpu_custom_call" | custom-call | flops 1 | bytes 1 | tf_op jit(solution)/shard_map/weight_terms/pallas_call | solution.py:316
  882.6 20.1 %collective-permute-done.23 = bf16[192,3072]{1,0:T(8,128)(2,1)} collective-permute-done((bf16[192,3072]{1,0:T(8,128)(2,1)}, bf16[192,3072]{1,0:T(8,128)(2,1)}, u32[]{:S(2)}, u32[]{:S(2)}) %collective-permute-start.23) | collective-permute-done | bytes 1179680 | tf_op jit(solution)/shard_map/ppermute | solution.py:24
  903.1 24.8 %collective-permute-done.24 = bf16[192,3072]{1,0:T(8,128)(2,1)} collective-permute-done((bf16[192,3072]{1,0:T(8,128)(2,1)}, bf16[192,3072]{1,0:T(8,128)(2,1)}, u32[]{:S(2)}, u32[]{:S(2)}) %collective-permute-start.24) | collective-permute-done | bytes 1179680 | tf_op jit(solution)/shard_map/ppermute | solution.py:24
  932.3 6.0 edge_back.3
  938.3 11.3 %collective-permute-done.26 = bf16[192,3072]{1,0:T(8,128)(2,1)} collective-permute-done((bf16[192,3072]{1,0:T(8,128)(2,1)}, bf16[192,3072]{1,0:T(8,128)(2,1)}, u32[]{:S(2)}, u32[]{:S(2)}) %collective-permute-start.26) | collective-permute-done | bytes 1179680 | tf_op jit(solution)/shard_map/ppermute | solution.py:24
  949.7 5.8 edge_back.4
  973.7 5.4 pad_maximum_fusion
  986.5 5.6 collective-permute-done.31
  992.2 12.1 %collective-permute-done.32 = bf16[2,33792]{1,0:T(2,128)(2,1)S(1)} collective-permute-done((bf16[2,33792]{1,0:T(2,128)(2,1)S(1)}, bf16[2,33792]{1,0:T(2,128)(2,1)S(1)}, u32[]{:S(2)}, u32[]{:S(2)}) %collective-permute-start.32) | collective-permute-done | bytes 135200 | tf_op jit(solution)/shard_map/ppermute | solution.py:78
  1037.0 21.9 %collective-permute-done.36 = bf16[192,3072]{1,0:T(8,128)(2,1)S(1)} collective-permute-done((bf16[192,3072]{1,0:T(8,128)(2,1)}, bf16[192,3072]{1,0:T(8,128)(2,1)S(1)}, u32[]{:S(2)}, u32[]{:S(2)}) %collective-permute-start.36) | collective-permute-done | bytes 1179680 | tf_op jit(solution)/shard_map/ppermute | solution.py:24
  (714 shorter events, 320.8 us)
Async XLA Ops:
  7.2 119.6 %all-gather.7.cloned.1.call-start = ((), (), s32[]{:S(2)}) async-start(), calls=%async_computation.6 | async-start | bytes 15040512 | tf_op jit(solution)/shard_map/all_gather | solution.py:60
  10.5 207.2 %all-gather.9.cloned.1.call-start = ((), (), s32[]{:S(2)}) async-start(), calls=%async_computation.7 | async-start | bytes 5308416 | tf_op jit(solution)/shard_map/all_gather | solution.py:67
  12.5 352.5 %all-gather.11.cloned.1.call-start = ((), (), s32[]{:S(2)}) async-start(), calls=%async_computation.14 | async-start | bytes 20054016 | tf_op jit(solution)/shard_map/all_gather | solution.py:60
  14.9 415.8 %all-gather.13.cloned.1.call-start = ((), (), s32[]{:S(2)}) async-start(), calls=%async_computation.15 | async-start | bytes 20054016 | tf_op jit(solution)/shard_map/all_gather | solution.py:60
  17.4 507.3 %reduce-scatter.7.cloned.1.call-start = ((), (), s32[]{:S(2)}) async-start(), calls=%async_computation.8 | async-start | bytes 10616832 | tf_op jit(solution)/shard_map/reduce_scatter | solution.py:73
  23.9 21.6 %collective-permute-start = (f32[4,2,2,4608]{3,2,1,0:T(2,128)}, f32[4,2,2,4608]{3,2,1,0:T(2,128)}, u32[]{:S(2)}, u32[]{:S(2)}) collective-permute-start(f32[4,2,2,4608]{3,2,1,0:T(2,128)} %bitcast.335), channel_id=1, source_target_pairs={{0,4},{4,0},{1,5},{5,1},{2,6},{6,2},{3,7},{7,3},{8,12},{12,8},{9,1... | collective-permute-start | bytes 884744 | tf_op jit(solution)/shard_map/ppermute | solution.py:24
  47.0 9.4 collective-permute-start.1
  49.6 7.0 collective-permute-start.3
  52.0 9.0 collective-permute-start.2
  62.5 4.7 collective-permute-start.4
  142.5 50.0 %collective-permute-start.5 = (bf16[576,1536]{1,0:T(8,128)(2,1)}, bf16[576,1536]{1,0:T(8,128)(2,1)}, u32[]{:S(2)}, u32[]{:S(2)}) collective-permute-start(bf16[576,1536]{1,0:T(8,128)(2,1)} %get-tuple-element.216), channel_id=1, source_target_pairs={{0,2},{2,0},{1,3},{3,1},{4,6},{6,4},{5,7},{7,5},{8,10},{10,8},{9,1... | collective-permute-start | bytes 5308424 | tf_op jit(solution)/shard_map/ppermute | solution.py:24
  147.0 45.5 %collective-permute-start.6 = (bf16[96,1536]{1,0:T(8,128)(2,1)}, bf16[96,1536]{1,0:T(8,128)(2,1)}, u32[]{:S(2)}, u32[]{:S(2)}) collective-permute-start(bf16[96,1536]{1,0:T(8,128)(2,1)} %get-tuple-element.241), channel_id=1, source_target_pairs={{0,2},{2,0},{1,3},{3,1},{4,6},{6,4},{5,7},{7,5},{8,10},{10,8},{9,1... | collective-permute-start | bytes 884744 | tf_op jit(solution)/shard_map/ppermute | solution.py:24
  158.6 121.6 %collective-permute-start.8 = (bf16[576,1536]{1,0:T(8,128)(2,1)}, bf16[576,1536]{1,0:T(8,128)(2,1)}, u32[]{:S(2)}, u32[]{:S(2)}) collective-permute-start(bf16[576,1536]{1,0:T(8,128)(2,1)} %get-tuple-element.215), channel_id=1, source_target_pairs={{0,2},{2,0},{1,3},{3,1},{4,6},{6,4},{5,7},{7,5},{8,10},{10,8},{9,1... | collective-permute-start | bytes 5308424 | tf_op jit(solution)/shard_map/ppermute | solution.py:24
  221.4 38.0 %collective-permute-start.7 = (bf16[576,1536]{1,0:T(8,128)(2,1)S(1)}, bf16[576,1536]{1,0:T(8,128)(2,1)S(1)}, u32[]{:S(2)}, u32[]{:S(2)}) collective-permute-start(bf16[576,1536]{1,0:T(8,128)(2,1)S(1)} %convolution_convert_fusion.5), channel_id=1, source_target_pairs={{0,1},{1,0},{2,3},{3,2},{4,5},{5,4},{6,7},{7,6},{8,9},{9,8},{10,11... | collective-permute-start | bytes 5308424 | tf_op jit(solution)/shard_map/ppermute | solution.py:24
  223.8 56.4 %collective-permute-start.9 = (bf16[96,1536]{1,0:T(8,128)(2,1)S(1)}, bf16[96,1536]{1,0:T(8,128)(2,1)S(1)}, u32[]{:S(2)}, u32[]{:S(2)}) collective-permute-start(bf16[96,1536]{1,0:T(8,128)(2,1)S(1)} %copy-done.149), channel_id=1, source_target_pairs={{0,2},{2,0},{1,3},{3,1},{4,6},{6,4},{5,7},{7,5},{8,10},{10,8},{9,1... | collective-permute-start | bytes 884744 | tf_op jit(solution)/shard_map/ppermute | solution.py:24
  302.8 55.1 %collective-permute-start.10 = (bf16[576,1536]{1,0:T(8,128)(2,1)S(1)}, bf16[576,1536]{1,0:T(8,128)(2,1)S(1)}, u32[]{:S(2)}, u32[]{:S(2)}) collective-permute-start(bf16[576,1536]{1,0:T(8,128)(2,1)S(1)} %convolution_convert_fusion.4), channel_id=1, source_target_pairs={{0,1},{1,0},{2,3},{3,2},{4,5},{5,4},{6,7},{7,6},{8,9},{9,8},{10,11... | collective-permute-start | bytes 5308424 | tf_op jit(solution)/shard_map/ppermute | solution.py:24
  307.1 47.2 %collective-permute-start.11 = (bf16[192,1536]{1,0:T(8,128)(2,1)S(1)}, bf16[192,1536]{1,0:T(8,128)(2,1)S(1)}, u32[]{:S(2)}, u32[]{:S(2)}) collective-permute-start(bf16[192,1536]{1,0:T(8,128)(2,1)S(1)} %convolution_convert_fusion.6), channel_id=1, source_target_pairs={{0,1},{1,0},{2,3},{3,2},{4,5},{5,4},{6,7},{7,6},{8,9},{9,8},{10,11... | collective-permute-start | bytes 1769480 | tf_op jit(solution)/shard_map/ppermute | solution.py:24
  412.2 249.6 %reduce-scatter.9.cloned.1.call-start = ((), (), s32[]{:S(2)}) async-start(), calls=%async_computation.9 | async-start | bytes 10616832 | tf_op jit(solution)/shard_map/reduce_scatter | solution.py:73
  421.8 364.5 %reduce-scatter.11.cloned.1.call-start = ((), (), s32[]{:S(2)}) async-start(), calls=%async_computation.10 | async-start | bytes 10616832 | tf_op jit(solution)/shard_map/reduce_scatter | solution.py:73
  447.5 110.8 %collective-permute-start.14 = (bf16[192,1536]{1,0:T(8,128)(2,1)}, bf16[192,1536]{1,0:T(8,128)(2,1)}, u32[]{:S(2)}, u32[]{:S(2)}) collective-permute-start(bf16[192,1536]{1,0:T(8,128)(2,1)} %fusion.63), channel_id=1, source_target_pairs={{0,1},{1,0},{2,3},{3,2},{4,5},{5,4},{6,7},{7,6},{8,9},{9,8},{10,11... | collective-permute-start | bytes 1769480 | tf_op jit(solution)/shard_map/ppermute | solution.py:24
  461.8 49.1 %collective-permute-start.12 = (bf16[4,192,3072]{2,1,0:T(8,128)(2,1)}, bf16[4,192,3072]{2,1,0:T(8,128)(2,1)}, u32[]{:S(2)}, u32[]{:S(2)}) collective-permute-start(bf16[4,192,3072]{2,1,0:T(8,128)(2,1)} %get-tuple-element.209), channel_id=1, source_target_pairs={{0,4},{4,0},{1,5},{5,1},{2,6},{6,2},{3,7},{7,3},{8,12},{12,8},{9,1... | collective-permute-start | bytes 14155784 | tf_op jit(solution)/shard_map/ppermute | solution.py:24
  500.7 41.4 %collective-permute-start.13 = (bf16[576,1536]{1,0:T(8,128)(2,1)}, bf16[576,1536]{1,0:T(8,128)(2,1)}, u32[]{:S(2)}, u32[]{:S(2)}) collective-permute-start(bf16[576,1536]{1,0:T(8,128)(2,1)} %fusion.41), channel_id=1, source_target_pairs={{0,1},{1,0},{2,3},{3,2},{4,5},{5,4},{6,7},{7,6},{8,9},{9,8},{10,11... | collective-permute-start | bytes 5308424 | tf_op jit(solution)/shard_map/ppermute | solution.py:24
  621.5 226.1 %reduce-scatter.13.cloned.1.call-start = ((), (), s32[]{:S(2)}) async-start(), calls=%async_computation.11 | async-start | bytes 2949120 | tf_op jit(solution)/shard_map/reduce_scatter | solution.py:114
  630.1 41.8 %collective-permute-start.15 = (bf16[576,1536]{1,0:T(8,128)(2,1)}, bf16[576,1536]{1,0:T(8,128)(2,1)}, u32[]{:S(2)}, u32[]{:S(2)}) collective-permute-start(bf16[576,1536]{1,0:T(8,128)(2,1)} %fusion.42), channel_id=1, source_target_pairs={{0,1},{1,0},{2,3},{3,2},{4,5},{5,4},{6,7},{7,6},{8,9},{9,8},{10,11... | collective-permute-start | bytes 5308424 | tf_op jit(solution)/shard_map/ppermute | solution.py:24
  636.0 90.2 %collective-permute-start.22 = (bf16[4,96,3072]{2,1,0:T(8,128)(2,1)}, bf16[4,96,3072]{2,1,0:T(8,128)(2,1)}, u32[]{:S(2)}, u32[]{:S(2)}) collective-permute-start(bf16[4,96,3072]{2,1,0:T(8,128)(2,1)} %get-tuple-element.218), channel_id=1, source_target_pairs={{0,2},{2,0},{1,3},{3,1},{4,6},{6,4},{5,7},{7,5},{8,10},{10,8},{9,1... | collective-permute-start | bytes 7077896 | tf_op jit(solution)/shard_map/ppermute | solution.py:24
  654.9 107.6 %collective-permute-start.17 = (bf16[1152,1536]{1,0:T(8,128)(2,1)}, bf16[1152,1536]{1,0:T(8,128)(2,1)}, u32[]{:S(2)}, u32[]{:S(2)}) collective-permute-start(bf16[1152,1536]{1,0:T(8,128)(2,1)} %fusion.15), channel_id=1, source_target_pairs={{0,1},{1,0},{2,3},{3,2},{4,5},{5,4},{6,7},{7,6},{8,9},{9,8},{10,11... | collective-permute-start | bytes 10616840 | tf_op jit(solution)/shard_map/ppermute | solution.py:24
  655.8 74.5 %collective-permute-start.16 = (bf16[2,576,768]{2,1,0:T(8,128)(2,1)}, bf16[2,576,768]{2,1,0:T(8,128)(2,1)}, u32[]{:S(2)}, u32[]{:S(2)}) collective-permute-start(bf16[2,576,768]{2,1,0:T(8,128)(2,1)} %get-tuple-element.144), channel_id=1, source_target_pairs={{0,2},{2,0},{1,3},{3,1},{4,6},{6,4},{5,7},{7,5},{8,10},{10,8},{9,1... | collective-permute-start | bytes 5308424 | tf_op jit(solution)/shard_map/ppermute | solution.py:24
  661.9 97.2 %collective-permute-start.18 = (bf16[192,1536]{1,0:T(8,128)(2,1)}, bf16[192,1536]{1,0:T(8,128)(2,1)}, u32[]{:S(2)}, u32[]{:S(2)}) collective-permute-start(bf16[192,1536]{1,0:T(8,128)(2,1)} %fusion.62), channel_id=1, source_target_pairs={{0,1},{1,0},{2,3},{3,2},{4,5},{5,4},{6,7},{7,6},{8,9},{9,8},{10,11... | collective-permute-start | bytes 1769480 | tf_op jit(solution)/shard_map/ppermute | solution.py:24
  725.5 48.7 %collective-permute-start.21 = (bf16[2,576,768]{2,1,0:T(8,128)(2,1)}, bf16[2,576,768]{2,1,0:T(8,128)(2,1)}, u32[]{:S(2)}, u32[]{:S(2)}) collective-permute-start(bf16[2,576,768]{2,1,0:T(8,128)(2,1)} %get-tuple-element.157), channel_id=1, source_target_pairs={{0,2},{2,0},{1,3},{3,1},{4,6},{6,4},{5,7},{7,5},{8,10},{10,8},{9,1... | collective-permute-start | bytes 5308424 | tf_op jit(solution)/shard_map/ppermute | solution.py:24
  730.3 243.4 %reduce-scatter.15.cloned.1.call-start = ((), (), s32[]{:S(2)}) async-start(), calls=%async_computation.12 | async-start | bytes 10616832 | tf_op jit(solution)/shard_map/reduce_scatter | solution.py:73
  810.2 216.0 %reduce-scatter.17.cloned.1.call-start = ((), (), s32[]{:S(2)}) async-start(), calls=%async_computation.13 | async-start | bytes 10616832 | tf_op jit(solution)/shard_map/reduce_scatter | solution.py:73
  821.3 23.1 %collective-permute-start.20 = (bf16[2,96,768]{2,1,0:T(8,128)(2,1)}, bf16[2,96,768]{2,1,0:T(8,128)(2,1)S(1)}, u32[]{:S(2)}, u32[]{:S(2)}) collective-permute-start(bf16[2,96,768]{2,1,0:T(8,128)(2,1)} %copy-done.120), channel_id=1, source_target_pairs={{0,2},{2,0},{1,3},{3,1},{4,6},{6,4},{5,7},{7,5},{8,10},{10,8},{9,1... | collective-permute-start | bytes 884744 | tf_op jit(solution)/shard_map/ppermute | solution.py:24
  822.2 13.2 %collective-permute-start.19 = (bf16[2,96,768]{2,1,0:T(8,128)(2,1)}, bf16[2,96,768]{2,1,0:T(8,128)(2,1)S(1)}, u32[]{:S(2)}, u32[]{:S(2)}) collective-permute-start(bf16[2,96,768]{2,1,0:T(8,128)(2,1)} %copy-done.119), channel_id=1, source_target_pairs={{0,2},{2,0},{1,3},{3,1},{4,6},{6,4},{5,7},{7,5},{8,10},{10,8},{9,1... | collective-permute-start | bytes 884744 | tf_op jit(solution)/shard_map/ppermute | solution.py:24
  839.1 88.8 %collective-permute-start.25 = (bf16[576,1536]{1,0:T(8,128)(2,1)}, bf16[576,1536]{1,0:T(8,128)(2,1)}, u32[]{:S(2)}, u32[]{:S(2)}) collective-permute-start(bf16[576,1536]{1,0:T(8,128)(2,1)} %fusion.43), channel_id=1, source_target_pairs={{0,1},{1,0},{2,3},{3,2},{4,5},{5,4},{6,7},{7,6},{8,9},{9,8},{10,11... | collective-permute-start | bytes 5308424 | tf_op jit(solution)/shard_map/ppermute | solution.py:24
  842.2 107.4 %collective-permute-start.27 = (bf16[576,1536]{1,0:T(8,128)(2,1)}, bf16[576,1536]{1,0:T(8,128)(2,1)}, u32[]{:S(2)}, u32[]{:S(2)}) collective-permute-start(bf16[576,1536]{1,0:T(8,128)(2,1)} %fusion.46), channel_id=1, source_target_pairs={{0,1},{1,0},{2,3},{3,2},{4,5},{5,4},{6,7},{7,6},{8,9},{9,8},{10,11... | collective-permute-start | bytes 5308424 | tf_op jit(solution)/shard_map/ppermute | solution.py:24
  847.6 27.8 %collective-permute-start.37 = (bf16[96,3072]{1,0:T(8,128)(2,1)}, bf16[96,3072]{1,0:T(8,128)(2,1)}, u32[]{:S(2)}, u32[]{:S(2)}) collective-permute-start(bf16[96,3072]{1,0:T(8,128)(2,1)} %reduce-scatter.13.cloned.1.call-done), channel_id=1, source_target_pairs={{0,2},{2,0},{1,3},{3,1},{4,6},{6,4},{5,7},{7,5},{8,10},{10,8},{9,1... | collective-permute-start | bytes 1769480 | tf_op jit(solution)/shard_map/ppermute | solution.py:24
  873.4 29.2 %collective-permute-start.23 = (bf16[192,3072]{1,0:T(8,128)(2,1)}, bf16[192,3072]{1,0:T(8,128)(2,1)}, u32[]{:S(2)}, u32[]{:S(2)}) collective-permute-start(bf16[192,3072]{1,0:T(8,128)(2,1)} %reduce-scatter.11.cloned.1.call-done), channel_id=1, source_target_pairs={{0,2},{2,0},{1,3},{3,1},{4,6},{6,4},{5,7},{7,5},{8,10},{10,8},{9,1... | collective-permute-start | bytes 3538952 | tf_op jit(solution)/shard_map/ppermute | solution.py:24
  874.3 53.6 %collective-permute-start.24 = (bf16[192,3072]{1,0:T(8,128)(2,1)}, bf16[192,3072]{1,0:T(8,128)(2,1)}, u32[]{:S(2)}, u32[]{:S(2)}) collective-permute-start(bf16[192,3072]{1,0:T(8,128)(2,1)} %reduce-scatter.7.cloned.1.call-done), channel_id=1, source_target_pairs={{0,2},{2,0},{1,3},{3,1},{4,6},{6,4},{5,7},{7,5},{8,10},{10,8},{9,1... | collective-permute-start | bytes 3538952 | tf_op jit(solution)/shard_map/ppermute | solution.py:24
  875.5 74.1 %collective-permute-start.26 = (bf16[192,3072]{1,0:T(8,128)(2,1)}, bf16[192,3072]{1,0:T(8,128)(2,1)}, u32[]{:S(2)}, u32[]{:S(2)}) collective-permute-start(bf16[192,3072]{1,0:T(8,128)(2,1)} %reduce-scatter.9.cloned.1.call-done), channel_id=1, source_target_pairs={{0,2},{2,0},{1,3},{3,1},{4,6},{6,4},{5,7},{7,5},{8,10},{10,8},{9,1... | collective-permute-start | bytes 3538952 | tf_op jit(solution)/shard_map/ppermute | solution.py:24
  902.6 53.0 %collective-permute-start.28 = (bf16[192,1536]{1,0:T(8,128)(2,1)}, bf16[192,1536]{1,0:T(8,128)(2,1)S(1)}, u32[]{:S(2)}, u32[]{:S(2)}) collective-permute-start(bf16[192,1536]{1,0:T(8,128)(2,1)} %fusion.59), channel_id=1, source_target_pairs={{0,1},{1,0},{2,3},{3,2},{4,5},{5,4},{6,7},{7,6},{8,9},{9,8},{10,11... | collective-permute-start | bytes 1769480 | tf_op jit(solution)/shard_map/ppermute | solution.py:24
  963.2 9.8 collective-permute-start.29
  973.7 5.4 collective-permute-start.30
  979.6 12.5 %collective-permute-start.31 = (bf16[2,33792]{1,0:T(2,128)(2,1)S(1)}, bf16[2,33792]{1,0:T(2,128)(2,1)S(1)}, u32[]{:S(2)}, u32[]{:S(2)}) collective-permute-start(bf16[2,33792]{1,0:T(2,128)(2,1)S(1)} %get-tuple-element.205), channel_id=1, source_target_pairs={{0,24},{8,0},{16,8},{24,16},{1,25},{9,1},{17,9},{25,17},{2,26},{10... | collective-permute-start | bytes 405512 | tf_op jit(solution)/shard_map/ppermute | solution.py:78
  982.7 51.1 %collective-permute-start.35 = (bf16[192,3072]{1,0:T(8,128)(2,1)}, bf16[192,3072]{1,0:T(8,128)(2,1)}, u32[]{:S(2)}, u32[]{:S(2)}) collective-permute-start(bf16[192,3072]{1,0:T(8,128)(2,1)} %reduce-scatter.15.cloned.1.call-done), channel_id=1, source_target_pairs={{0,2},{2,0},{1,3},{3,1},{4,6},{6,4},{5,7},{7,5},{8,10},{10,8},{9,1... | collective-permute-start | bytes 3538952 | tf_op jit(solution)/shard_map/ppermute | solution.py:24
  984.3 20.1 %collective-permute-start.33 = (bf16[2,33792]{1,0:T(2,128)(2,1)S(1)}, bf16[2,33792]{1,0:T(2,128)(2,1)S(1)}, u32[]{:S(2)}, u32[]{:S(2)}) collective-permute-start(bf16[2,33792]{1,0:T(2,128)(2,1)S(1)} %get-tuple-element.205), channel_id=1, source_target_pairs={{0,8},{8,16},{16,24},{24,0},{1,9},{9,17},{17,25},{25,1},{2,10},{10... | collective-permute-start | bytes 405512 | tf_op jit(solution)/shard_map/ppermute | solution.py:78
  986.5 17.8 %collective-permute-start.32 = (bf16[2,33792]{1,0:T(2,128)(2,1)S(1)}, bf16[2,33792]{1,0:T(2,128)(2,1)S(1)}, u32[]{:S(2)}, u32[]{:S(2)}) collective-permute-start(bf16[2,33792]{1,0:T(2,128)(2,1)S(1)} %get-tuple-element.205), channel_id=1, source_target_pairs={{0,16},{8,24},{16,0},{24,8},{1,17},{9,25},{17,1},{25,9},{2,18},{10... | collective-permute-start | bytes 405512 | tf_op jit(solution)/shard_map/ppermute | solution.py:78
  1016.7 15.7 %collective-permute-start.34 = (bf16[16,192]{1,0:T(8,128)(2,1)S(1)}, bf16[16,192]{1,0:T(8,128)(2,1)}, u32[]{:S(2)}, u32[]{:S(2)}) collective-permute-start(bf16[16,192]{1,0:T(8,128)(2,1)S(1)} %fusion.94), channel_id=1, source_target_pairs={{0,1},{1,0},{2,3},{3,2},{4,5},{5,4},{6,7},{7,6},{8,9},{9,8},{10,11... | collective-permute-start | bytes 18440 | tf_op jit(solution)/shard_map/ppermute | solution.py:24
  1031.4 27.4 %collective-permute-start.36 = (bf16[192,3072]{1,0:T(8,128)(2,1)}, bf16[192,3072]{1,0:T(8,128)(2,1)S(1)}, u32[]{:S(2)}, u32[]{:S(2)}) collective-permute-start(bf16[192,3072]{1,0:T(8,128)(2,1)} %reduce-scatter.17.cloned.1.call-done), channel_id=1, source_target_pairs={{0,2},{2,0},{1,3},{3,1},{4,6},{6,4},{5,7},{7,5},{8,10},{10,8},{9,1... | collective-permute-start | bytes 3538952 | tf_op jit(solution)/shard_map/ppermute | solution.py:24
  (209 other events, 1994.5 us)
Sparse Core Ops, SparseCore 0:
  10.9 115.7 all-gather.6
  129.0 49.8 all-gather.8
  181.1 143.1 all-gather.10
  325.7 97.2 all-gather.12
  425.1 99.4 reduce-scatter.6
  526.8 97.8 reduce-scatter.8
  627.0 97.8 reduce-scatter.10
  730.4 45.1 reduce-scatter.12
  810.3 96.2 reduce-scatter.14
  908.7 106.5 reduce-scatter.16

commit v4 on v3

--- a/solution.py
+++ b/solution.py
@@ -865,8 +865,8 @@
     second_term = weight_terms(groups)
     second_shard = scatter_rows(second_term)
     up_mine = z_step(up_both)
-    down_given = [ctx_given(after(shard, second_term)) for shard in down_shards]
-    up_given = ctx_given(after(up_shard, second_term))
+    down_given = [ctx_given(after(shard, first_term)) for shard in down_shards]
+    up_given = ctx_given(after(up_shard, first_term))
     ready = (second_term, up_mine, up_given, down_given[0])
     input_grads, edge_sums = {}, {}
     for unit in list(slots) + [text_unit]:

time: 1080 us -> 1070 us (level)
  waiting for transfers between devices: 340 us -> 325 us
    ppermute x32, waiting for transfers between devices: 256 us -> 239 us  [swap(): return lax.ppermute(values, axis, PAIR)]
    unnamed x435 -> x441, local copies, waits for them, and re-layouts: 59.1 us -> 60.3 us
  transfers between devices with their start and end apart: 48 -> 48, of which waited for: 20 -> 21; matrix products, arithmetic and copies ran while one was open for 41% -> 41% of each run, Pallas kernels for 17% -> 17%
where the time goes in v4:
time: 1070 us; the launch traced here: 1060 us
  waiting for transfers between devices  325 us (30%)
  matrix products  224 us (21%)
  Pallas kernels  182 us (17%)
  local copies, waits for them, and re-layouts  159 us (15%)
  other arithmetic  111 us (10%)
  starting transfers between devices  38.6 us (4%)
  between operations  16.9 us (2%)
    ppermute x32, waiting for transfers between devices, swap(): return lax.ppermute(values, axis, PAIR)  239 us
    dot_general x9, matrix products, dot(): lax.dot_general(left, right, (((1,), (0,)), ((), ())), preferred_element_...  88.5 us
    dot_general x11, matrix products, dot_nt(): lax.dot_general(left, right, (((1,), (1,)), ((), ())), preferred_element_...  83.2 us
    pallas_call x2, Pallas kernels, attend_back(): pl.pallas_call(functools.partial(attend_back_kernel, tuple((part[3] for p...  73.3 us
    unnamed x441, local copies, waits for them, and re-layouts  60.3 us
    all_gather x3, waiting for transfers between devices, gather_rows(): whole = lax.all_gather(piece, ('ctx',) + FSDP, axis=0, tiled=True)  50.7 us
    dot_general x4, matrix products, dot_tn(): lax.dot_general(left, right, (((0,), (0,)), ((), ())), preferred_element_...  45.1 us
    pallas_call x2, Pallas kernels, attend(): pl.pallas_call(functools.partial(attend_kernel, len(key_parts), image_row...  37 us
  transfers between devices with their start and end apart: 48, of which 21 were waited for; matrix products, arithmetic and copies ran while one was open for 41% of the time, Pallas kernels for 17%

profile of v4, /device:TPU:0, one launch (start us, length us, event | category | flops | bytes accessed | tf_op | source)
XLA Modules:
  0.0 1056.6 jit_solution(18410465056003652794)
XLA Ops:
  76.1 50.7 %all-gather.7.cloned.1.call-done = bf16[3072,2304]{1,0:T(8,128)(2,1)} async-done(((bf16[192,2304]{1,0:T(8,128)(2,1)}), bf16[3072,2304]{1,0:T(8,128)(2,1)}) %all-gather.7.cloned.1.call-update) | async-done | bytes 14155792 | tf_op jit(solution)/shard_map/all_gather | solution.py:60
  126.8 12.3 %fusion.6 = bf16[1152,2304]{1,0:T(8,128)(2,1)S(1)} fusion(bf16[1152,1536]{1,0:T(8,128)(2,1)} %bitcast.389, bf16[3072,2304]{1,0:T(8,128)(2,1)} %all-gather.7.cloned.1.call-done, f32[2304]{0:T(1024)} %get-tuple-element.297), kind=kOutput, calls=%fused_computation.11 | convolution fusion | flops 8159035392 | bytes 15937536 | tf_op jit(solution)/shard_map/dot_general | solution.py:44
  159.2 33.4 %collective-permute-done.6.refs_5_.refs_9_.refs_10_.refs_14_ = bf16[96,1536]{1,0:T(8,128)(2,1)} collective-permute-done((bf16[96,1536]{1,0:T(8,128)(2,1)}, bf16[96,1536]{1,0:T(8,128)(2,1)}, u32[]{:S(2)}, u32[]{:S(2)}) %collective-permute-start.6) | collective-permute-done | bytes 294944 | tf_op jit(solution)/shard_map/ppermute | solution.py:24
  197.3 18.2 %attend.2 = (bf16[576,768]{1,0:T(8,128)(2,1)S(1)}, bf16[96,768]{1,0:T(8,128)(2,1)S(1)}, f32[6,1,1344]{2,1,0:T(1,128)S(1)}) custom-call(bf16[2,576,2304]{2,1,0:T(8,128)(2,1)} %bitcast.374, bf16[2,96,2304]{2,1,0:T(8,128)(2,1)S(1)} %bitcast.337, bf16[2,576,2304]{2,1,0:T(8,128)(2,1)} %bitcast.375, ...), custom_call_target="tpu_custom_call" | custom-call | flops 1 | bytes 1 | tf_op jit(solution)/shard_map/attend/pallas_call | solution.py:443
  225.1 34.4 %collective-permute-done.7 = bf16[576,1536]{1,0:T(8,128)(2,1)S(1)} collective-permute-done((bf16[576,1536]{1,0:T(8,128)(2,1)S(1)}, bf16[576,1536]{1,0:T(8,128)(2,1)S(1)}, u32[]{:S(2)}, u32[]{:S(2)}) %collective-permute-start.7) | collective-permute-done | bytes 1769504 | tf_op jit(solution)/shard_map/ppermute | solution.py:24
  265.3 15.0 %collective-permute-done.9.refs_5_.refs_9_.refs_10_.refs_14_ = bf16[96,1536]{1,0:T(8,128)(2,1)S(1)} collective-permute-done((bf16[96,1536]{1,0:T(8,128)(2,1)S(1)}, bf16[96,1536]{1,0:T(8,128)(2,1)S(1)}, u32[]{:S(2)}, u32[]{:S(2)}) %collective-permute-start.9) | collective-permute-done | bytes 294944 | tf_op jit(solution)/shard_map/ppermute | solution.py:24
  280.3 18.8 %attend.3 = (bf16[576,768]{1,0:T(8,128)(2,1)S(1)}, bf16[96,768]{1,0:T(8,128)(2,1)S(1)}, f32[6,1,1344]{2,1,0:T(1,128)S(1)}) custom-call(bf16[2,576,2304]{2,1,0:T(8,128)(2,1)} %bitcast.377, bf16[2,96,2304]{2,1,0:T(8,128)(2,1)S(1)} %bitcast.340, bf16[2,576,2304]{2,1,0:T(8,128)(2,1)} %bitcast.378, ...), custom_call_target="tpu_custom_call" | custom-call | flops 1 | bytes 1 | tf_op jit(solution)/shard_map/attend/pallas_call | solution.py:443
  308.2 5.2 multiply_multiply_fusion.2
  313.5 40.9 %collective-permute-done.11 = bf16[192,1536]{1,0:T(8,128)(2,1)S(1)} collective-permute-done((bf16[192,1536]{1,0:T(8,128)(2,1)S(1)}, bf16[192,1536]{1,0:T(8,128)(2,1)S(1)}, u32[]{:S(2)}, u32[]{:S(2)}) %collective-permute-start.11) | collective-permute-done | bytes 589856 | tf_op jit(solution)/shard_map/ppermute | solution.py:24
  365.0 8.4 multiply_convert_fusion.2
  373.4 21.1 %multiply_convert_fusion = (bf16[1152,3072]{1,0:T(8,128)(2,1)}, f32[1152,3072]{1,0:T(8,128)}) fusion(f32[3072]{0:T(1024)S(1)} %bitcast.407, bf16[1,3072,3072]{2,1,0:T(8,128)(2,1)} %all-gather.11.cloned.1.call-done, bf16[576,1536]{1,0:T(8,128)(2,1)S(1)} %bitcast.351, bf16[576,1536]{1,0:T(8,128)(2,1)S(1)} %bitcast.349), kind=kOutput, calls=%fused_computation.8 | convolution fusion | flops 10914103296 | bytes 34222080 | tf_op jit(solution)/shard_map/dot_general | solution.py:44
  394.5 17.7 %convolution_convert_fusion.3 = bf16[1536,3072]{1,0:T(8,128)(2,1)} fusion(bf16[1152,1536]{1,0:T(8,128)(2,1)S(1)} %bitcast.400, bf16[1152,3072]{1,0:T(8,128)(2,1)} %get-tuple-element.134), kind=kOutput, calls=%fused_computation.15 | convolution fusion | flops 10876354560 | bytes 20054016 | tf_op jit(solution)/shard_map/dot_general | solution.py:52
  422.1 6.7 fusion.130
  430.7 8.9 fusion.134
  439.6 7.9 fusion.63
  449.3 5.5 convolution_convert_fusion.1
  454.8 7.0 dynamic-slice_bitcast_fusion.1
  461.8 24.6 %fusion.129 = (bf16[3072]{0:T(1024)(128)(2,1)}, bf16[1152,3072]{1,0:T(8,128)(2,1)S(1)}) fusion(f32[1152,3072]{1,0:T(8,128)} %get-tuple-element.305, bf16[1152,1536]{1,0:T(8,128)(2,1)} %bitcast.399, bf16[1,3072,3072]{2,1,0:T(8,128)(2,1)} %all-gather.13.cloned.1.call-done), kind=kOutput, calls=%fused_computation.329 | convolution fusion | flops 10945950720 | bytes 34215936 | tf_op jit(solution)/shard_map/dot_general | solution.py:44
  490.3 10.4 fusion.41
  501.1 9.8 fusion.42
  510.9 6.5 add_convert_fusion
  517.4 7.4 reduce-scatter.7.cloned.1.call-done
  524.7 17.4 %collective-permute-done.13 = bf16[576,1536]{1,0:T(8,128)(2,1)} collective-permute-done((bf16[576,1536]{1,0:T(8,128)(2,1)}, bf16[576,1536]{1,0:T(8,128)(2,1)}, u32[]{:S(2)}, u32[]{:S(2)}) %collective-permute-start.13) | collective-permute-done | bytes 1769504 | tf_op jit(solution)/shard_map/ppermute | solution.py:24
  545.0 7.6 middle_back.3
  564.8 36.8 %attend_back.2 = (bf16[576,768]{1,0:T(8,128)(2,1)S(1)}, bf16[96,768]{1,0:T(8,128)(2,1)S(1)}, f32[6,2,128]{2,1,0:T(2,128)S(1)}, f32[6,2,128]{2,1,0:T(2,128)S(1)},...) custom-call(bf16[2,576,2304]{2,1,0:T(8,128)(2,1)} %bitcast.380, ...), custom_call_target="tpu_custom_call" | custom-call | flops 1 | bytes 1 | tf_op jit(solution)/shard_map/attend_back/pallas_call | solution.py:478
  604.6 16.8 %convolution_convert_fusion = bf16[1536,3072]{1,0:T(8,128)(2,1)} fusion(bf16[1152,1536]{1,0:T(8,128)(2,1)} %pad_maximum_fusion.2, bf16[1152,3072]{1,0:T(8,128)(2,1)S(1)} %bitcast.392), kind=kOutput, calls=%fused_computation.12 | convolution fusion | flops 10876354560 | bytes 20054016 | tf_op jit(solution)/shard_map/dot_general | solution.py:52
  630.1 5.8 dynamic-slice_bitcast_fusion.3
  637.2 17.6 %fusion.15 = bf16[1152,1536]{1,0:T(8,128)(2,1)} fusion(bf16[1152,3072]{1,0:T(8,128)(2,1)} %get-tuple-element.134, bf16[1,3072,3072]{2,1,0:T(8,128)(2,1)} %all-gather.13.cloned.1.call-done), kind=kOutput, calls=%fused_computation.31 | convolution fusion | flops 10873405440 | bytes 20054016 | tf_op jit(solution)/shard_map/dot_general | solution.py:48
  661.8 10.1 collective-permute-done.15
  674.7 7.6 middle_back.5
  688.8 36.6 %attend_back.3 = (bf16[576,768]{1,0:T(8,128)(2,1)S(1)}, bf16[96,768]{1,0:T(8,128)(2,1)S(1)}, f32[6,2,128]{2,1,0:T(2,128)S(1)}, f32[6,2,128]{2,1,0:T(2,128)S(1)},...) custom-call(bf16[2,576,2304]{2,1,0:T(8,128)(2,1)} %bitcast.383, ...), custom_call_target="tpu_custom_call" | custom-call | flops 1 | bytes 1 | tf_op jit(solution)/shard_map/attend_back/pallas_call | solution.py:478
  734.4 8.6 fusion.43
  742.9 16.1 %collective-permute-done.18 = bf16[192,1536]{1,0:T(8,128)(2,1)} collective-permute-done((bf16[192,1536]{1,0:T(8,128)(2,1)}, bf16[192,1536]{1,0:T(8,128)(2,1)}, u32[]{:S(2)}, u32[]{:S(2)}) %collective-permute-start.18) | collective-permute-done | bytes 589856 | tf_op jit(solution)/shard_map/ppermute | solution.py:24
  768.7 5.5 multiply_reduce_fusion.1
  777.6 8.5 fusion.46
  791.9 18.2 %weight_terms.2 = bf16[1536,3072]{1,0:T(8,128)(2,1)} custom-call(bf16[576,1536]{1,0:T(8,128)(2,1)} %bitcast.357, bf16[576,768]{1,0:T(8,128)(2,1)} %copy-done.30, bf16[576,1536]{1,0:T(8,128)(2,1)} %bitcast.358, bf16[576,768]{1,0:T(8,128)(2,1)} %copy-done.32, bf16[192,1536]{1,0:T(8,128)(2,1)S(1)} %bitcast.364, bf16[192,768]{1,0:T(8,128)(2,1)S(1)} %copy-done.82, ...), custom_call_target="tpu_custom_call" | custom-call | flops 1 | bytes 1 | tf_op jit(solution)/shard_map/weight_terms/pallas_call | solution.py:316
  824.8 10.4 collective-permute-done.19
  856.5 7.9 collective-permute-done.37
  868.6 6.4 fusion.59
  875.0 17.8 %weight_terms.3 = bf16[1536,3072]{1,0:T(8,128)(2,1)} custom-call(bf16[576,1536]{1,0:T(8,128)(2,1)} %get-tuple-element.162.refs_6_.refs_0_, bf16[576,1536]{1,0:T(8,128)(2,1)} %pad_maximum_fusion.5.refs_1_, bf16[576,1536]{1,0:T(8,128)(2,1)} %get-tuple-element.163.refs_8_.refs_2_, bf16[576,1536]{1,0:T(8,128)(2,1)} %pad_maximum_fusion.6.refs_3_, ...), custom_call_target="tpu_custom_call" | custom-call | flops 1 | bytes 1 | tf_op jit(solution)/shard_map/weight_terms/pallas_call | solution.py:316
  893.5 21.5 %collective-permute-done.24 = bf16[192,3072]{1,0:T(8,128)(2,1)} collective-permute-done((bf16[192,3072]{1,0:T(8,128)(2,1)}, bf16[192,3072]{1,0:T(8,128)(2,1)}, u32[]{:S(2)}, u32[]{:S(2)}) %collective-permute-start.24) | collective-permute-done | bytes 1179680 | tf_op jit(solution)/shard_map/ppermute | solution.py:24
  919.3 6.0 edge_back.3
  925.3 11.3 %collective-permute-done.26 = bf16[192,3072]{1,0:T(8,128)(2,1)} collective-permute-done((bf16[192,3072]{1,0:T(8,128)(2,1)}, bf16[192,3072]{1,0:T(8,128)(2,1)}, u32[]{:S(2)}, u32[]{:S(2)}) %collective-permute-start.26) | collective-permute-done | bytes 1179680 | tf_op jit(solution)/shard_map/ppermute | solution.py:24
  936.7 5.8 edge_back.4
  962.0 5.3 pad_maximum_fusion
  973.6 9.7 collective-permute-done.31
  983.5 7.9 collective-permute-done.32
  1026.6 19.9 %collective-permute-done.36 = bf16[192,3072]{1,0:T(8,128)(2,1)S(1)} collective-permute-done((bf16[192,3072]{1,0:T(8,128)(2,1)}, bf16[192,3072]{1,0:T(8,128)(2,1)S(1)}, u32[]{:S(2)}, u32[]{:S(2)}) %collective-permute-start.36) | collective-permute-done | bytes 1179680 | tf_op jit(solution)/shard_map/ppermute | solution.py:24
  (720 shorter events, 326.0 us)
Async XLA Ops:
  7.2 119.6 %all-gather.7.cloned.1.call-start = ((), (), s32[]{:S(2)}) async-start(), calls=%async_computation.6 | async-start | bytes 15040512 | tf_op jit(solution)/shard_map/all_gather | solution.py:60
  10.5 207.3 %all-gather.9.cloned.1.call-start = ((), (), s32[]{:S(2)}) async-start(), calls=%async_computation.7 | async-start | bytes 5308416 | tf_op jit(solution)/shard_map/all_gather | solution.py:67
  12.5 352.5 %all-gather.11.cloned.1.call-start = ((), (), s32[]{:S(2)}) async-start(), calls=%async_computation.14 | async-start | bytes 20054016 | tf_op jit(solution)/shard_map/all_gather | solution.py:60
  14.9 415.8 %all-gather.13.cloned.1.call-start = ((), (), s32[]{:S(2)}) async-start(), calls=%async_computation.15 | async-start | bytes 20054016 | tf_op jit(solution)/shard_map/all_gather | solution.py:60
  17.4 507.3 %reduce-scatter.7.cloned.1.call-start = ((), (), s32[]{:S(2)}) async-start(), calls=%async_computation.8 | async-start | bytes 10616832 | tf_op jit(solution)/shard_map/reduce_scatter | solution.py:73
  23.9 21.6 %collective-permute-start = (f32[4,2,2,4608]{3,2,1,0:T(2,128)}, f32[4,2,2,4608]{3,2,1,0:T(2,128)}, u32[]{:S(2)}, u32[]{:S(2)}) collective-permute-start(f32[4,2,2,4608]{3,2,1,0:T(2,128)} %bitcast.335), channel_id=1, source_target_pairs={{0,4},{4,0},{1,5},{5,1},{2,6},{6,2},{3,7},{7,3},{8,12},{12,8},{9,1... | collective-permute-start | bytes 884744 | tf_op jit(solution)/shard_map/ppermute | solution.py:24
  46.9 9.3 collective-permute-start.1
  49.5 7.0 collective-permute-start.3
  52.0 9.1 collective-permute-start.2
  62.5 4.7 collective-permute-start.4
  142.6 50.0 %collective-permute-start.5 = (bf16[576,1536]{1,0:T(8,128)(2,1)}, bf16[576,1536]{1,0:T(8,128)(2,1)}, u32[]{:S(2)}, u32[]{:S(2)}) collective-permute-start(bf16[576,1536]{1,0:T(8,128)(2,1)} %get-tuple-element.216), channel_id=1, source_target_pairs={{0,2},{2,0},{1,3},{3,1},{4,6},{6,4},{5,7},{7,5},{8,10},{10,8},{9,1... | collective-permute-start | bytes 5308424 | tf_op jit(solution)/shard_map/ppermute | solution.py:24
  147.1 45.5 %collective-permute-start.6 = (bf16[96,1536]{1,0:T(8,128)(2,1)}, bf16[96,1536]{1,0:T(8,128)(2,1)}, u32[]{:S(2)}, u32[]{:S(2)}) collective-permute-start(bf16[96,1536]{1,0:T(8,128)(2,1)} %get-tuple-element.241), channel_id=1, source_target_pairs={{0,2},{2,0},{1,3},{3,1},{4,6},{6,4},{5,7},{7,5},{8,10},{10,8},{9,1... | collective-permute-start | bytes 884744 | tf_op jit(solution)/shard_map/ppermute | solution.py:24
  158.6 121.6 %collective-permute-start.8 = (bf16[576,1536]{1,0:T(8,128)(2,1)}, bf16[576,1536]{1,0:T(8,128)(2,1)}, u32[]{:S(2)}, u32[]{:S(2)}) collective-permute-start(bf16[576,1536]{1,0:T(8,128)(2,1)} %get-tuple-element.215), channel_id=1, source_target_pairs={{0,2},{2,0},{1,3},{3,1},{4,6},{6,4},{5,7},{7,5},{8,10},{10,8},{9,1... | collective-permute-start | bytes 5308424 | tf_op jit(solution)/shard_map/ppermute | solution.py:24
  221.5 38.0 %collective-permute-start.7 = (bf16[576,1536]{1,0:T(8,128)(2,1)S(1)}, bf16[576,1536]{1,0:T(8,128)(2,1)S(1)}, u32[]{:S(2)}, u32[]{:S(2)}) collective-permute-start(bf16[576,1536]{1,0:T(8,128)(2,1)S(1)} %convolution_convert_fusion.5), channel_id=1, source_target_pairs={{0,1},{1,0},{2,3},{3,2},{4,5},{5,4},{6,7},{7,6},{8,9},{9,8},{10,11... | collective-permute-start | bytes 5308424 | tf_op jit(solution)/shard_map/ppermute | solution.py:24
  223.9 56.4 %collective-permute-start.9 = (bf16[96,1536]{1,0:T(8,128)(2,1)S(1)}, bf16[96,1536]{1,0:T(8,128)(2,1)S(1)}, u32[]{:S(2)}, u32[]{:S(2)}) collective-permute-start(bf16[96,1536]{1,0:T(8,128)(2,1)S(1)} %copy-done.152), channel_id=1, source_target_pairs={{0,2},{2,0},{1,3},{3,1},{4,6},{6,4},{5,7},{7,5},{8,10},{10,8},{9,1... | collective-permute-start | bytes 884744 | tf_op jit(solution)/shard_map/ppermute | solution.py:24
  302.9 55.1 %collective-permute-start.10 = (bf16[576,1536]{1,0:T(8,128)(2,1)S(1)}, bf16[576,1536]{1,0:T(8,128)(2,1)S(1)}, u32[]{:S(2)}, u32[]{:S(2)}) collective-permute-start(bf16[576,1536]{1,0:T(8,128)(2,1)S(1)} %convolution_convert_fusion.4), channel_id=1, source_target_pairs={{0,1},{1,0},{2,3},{3,2},{4,5},{5,4},{6,7},{7,6},{8,9},{9,8},{10,11... | collective-permute-start | bytes 5308424 | tf_op jit(solution)/shard_map/ppermute | solution.py:24
  307.2 47.2 %collective-permute-start.11 = (bf16[192,1536]{1,0:T(8,128)(2,1)S(1)}, bf16[192,1536]{1,0:T(8,128)(2,1)S(1)}, u32[]{:S(2)}, u32[]{:S(2)}) collective-permute-start(bf16[192,1536]{1,0:T(8,128)(2,1)S(1)} %convolution_convert_fusion.6), channel_id=1, source_target_pairs={{0,1},{1,0},{2,3},{3,2},{4,5},{5,4},{6,7},{7,6},{8,9},{9,8},{10,11... | collective-permute-start | bytes 1769480 | tf_op jit(solution)/shard_map/ppermute | solution.py:24
  412.2 249.5 %reduce-scatter.9.cloned.1.call-start = ((), (), s32[]{:S(2)}) async-start(), calls=%async_computation.9 | async-start | bytes 10616832 | tf_op jit(solution)/shard_map/reduce_scatter | solution.py:73
  421.8 364.3 %reduce-scatter.11.cloned.1.call-start = ((), (), s32[]{:S(2)}) async-start(), calls=%async_computation.10 | async-start | bytes 10616832 | tf_op jit(solution)/shard_map/reduce_scatter | solution.py:73
  447.5 110.9 %collective-permute-start.14 = (bf16[192,1536]{1,0:T(8,128)(2,1)}, bf16[192,1536]{1,0:T(8,128)(2,1)}, u32[]{:S(2)}, u32[]{:S(2)}) collective-permute-start(bf16[192,1536]{1,0:T(8,128)(2,1)} %fusion.63), channel_id=1, source_target_pairs={{0,1},{1,0},{2,3},{3,2},{4,5},{5,4},{6,7},{7,6},{8,9},{9,8},{10,11... | collective-permute-start | bytes 1769480 | tf_op jit(solution)/shard_map/ppermute | solution.py:24
  461.8 49.1 %collective-permute-start.12 = (bf16[4,192,3072]{2,1,0:T(8,128)(2,1)}, bf16[4,192,3072]{2,1,0:T(8,128)(2,1)}, u32[]{:S(2)}, u32[]{:S(2)}) collective-permute-start(bf16[4,192,3072]{2,1,0:T(8,128)(2,1)} %get-tuple-element.209), channel_id=1, source_target_pairs={{0,4},{4,0},{1,5},{5,1},{2,6},{6,2},{3,7},{7,3},{8,12},{12,8},{9,1... | collective-permute-start | bytes 14155784 | tf_op jit(solution)/shard_map/ppermute | solution.py:24
  500.7 41.4 %collective-permute-start.13 = (bf16[576,1536]{1,0:T(8,128)(2,1)}, bf16[576,1536]{1,0:T(8,128)(2,1)}, u32[]{:S(2)}, u32[]{:S(2)}) collective-permute-start(bf16[576,1536]{1,0:T(8,128)(2,1)} %fusion.41), channel_id=1, source_target_pairs={{0,1},{1,0},{2,3},{3,2},{4,5},{5,4},{6,7},{7,6},{8,9},{9,8},{10,11... | collective-permute-start | bytes 5308424 | tf_op jit(solution)/shard_map/ppermute | solution.py:24
  621.5 226.4 %reduce-scatter.13.cloned.1.call-start = ((), (), s32[]{:S(2)}) async-start(), calls=%async_computation.11 | async-start | bytes 2949120 | tf_op jit(solution)/shard_map/reduce_scatter | solution.py:114
  630.1 41.8 %collective-permute-start.15 = (bf16[576,1536]{1,0:T(8,128)(2,1)}, bf16[576,1536]{1,0:T(8,128)(2,1)}, u32[]{:S(2)}, u32[]{:S(2)}) collective-permute-start(bf16[576,1536]{1,0:T(8,128)(2,1)} %fusion.42), channel_id=1, source_target_pairs={{0,1},{1,0},{2,3},{3,2},{4,5},{5,4},{6,7},{7,6},{8,9},{9,8},{10,11... | collective-permute-start | bytes 5308424 | tf_op jit(solution)/shard_map/ppermute | solution.py:24
  635.9 90.2 %collective-permute-start.22 = (bf16[4,96,3072]{2,1,0:T(8,128)(2,1)}, bf16[4,96,3072]{2,1,0:T(8,128)(2,1)}, u32[]{:S(2)}, u32[]{:S(2)}) collective-permute-start(bf16[4,96,3072]{2,1,0:T(8,128)(2,1)} %get-tuple-element.218), channel_id=1, source_target_pairs={{0,2},{2,0},{1,3},{3,1},{4,6},{6,4},{5,7},{7,5},{8,10},{10,8},{9,1... | collective-permute-start | bytes 7077896 | tf_op jit(solution)/shard_map/ppermute | solution.py:24
  654.8 107.7 %collective-permute-start.17 = (bf16[1152,1536]{1,0:T(8,128)(2,1)}, bf16[1152,1536]{1,0:T(8,128)(2,1)}, u32[]{:S(2)}, u32[]{:S(2)}) collective-permute-start(bf16[1152,1536]{1,0:T(8,128)(2,1)} %fusion.15), channel_id=1, source_target_pairs={{0,1},{1,0},{2,3},{3,2},{4,5},{5,4},{6,7},{7,6},{8,9},{9,8},{10,11... | collective-permute-start | bytes 10616840 | tf_op jit(solution)/shard_map/ppermute | solution.py:24
  655.3 74.9 %collective-permute-start.16 = (bf16[2,576,768]{2,1,0:T(8,128)(2,1)}, bf16[2,576,768]{2,1,0:T(8,128)(2,1)}, u32[]{:S(2)}, u32[]{:S(2)}) collective-permute-start(bf16[2,576,768]{2,1,0:T(8,128)(2,1)} %get-tuple-element.144), channel_id=1, source_target_pairs={{0,2},{2,0},{1,3},{3,1},{4,6},{6,4},{5,7},{7,5},{8,10},{10,8},{9,1... | collective-permute-start | bytes 5308424 | tf_op jit(solution)/shard_map/ppermute | solution.py:24
  661.8 97.2 %collective-permute-start.18 = (bf16[192,1536]{1,0:T(8,128)(2,1)}, bf16[192,1536]{1,0:T(8,128)(2,1)}, u32[]{:S(2)}, u32[]{:S(2)}) collective-permute-start(bf16[192,1536]{1,0:T(8,128)(2,1)} %fusion.62), channel_id=1, source_target_pairs={{0,1},{1,0},{2,3},{3,2},{4,5},{5,4},{6,7},{7,6},{8,9},{9,8},{10,11... | collective-permute-start | bytes 1769480 | tf_op jit(solution)/shard_map/ppermute | solution.py:24
  725.4 48.7 %collective-permute-start.21 = (bf16[2,576,768]{2,1,0:T(8,128)(2,1)}, bf16[2,576,768]{2,1,0:T(8,128)(2,1)}, u32[]{:S(2)}, u32[]{:S(2)}) collective-permute-start(bf16[2,576,768]{2,1,0:T(8,128)(2,1)} %get-tuple-element.157), channel_id=1, source_target_pairs={{0,2},{2,0},{1,3},{3,1},{4,6},{6,4},{5,7},{7,5},{8,10},{10,8},{9,1... | collective-permute-start | bytes 5308424 | tf_op jit(solution)/shard_map/ppermute | solution.py:24
  730.1 231.8 %reduce-scatter.15.cloned.1.call-start = ((), (), s32[]{:S(2)}) async-start(), calls=%async_computation.12 | async-start | bytes 10616832 | tf_op jit(solution)/shard_map/reduce_scatter | solution.py:73
  810.1 205.2 %reduce-scatter.17.cloned.1.call-start = ((), (), s32[]{:S(2)}) async-start(), calls=%async_computation.13 | async-start | bytes 10616832 | tf_op jit(solution)/shard_map/reduce_scatter | solution.py:73
  821.1 23.9 %collective-permute-start.20 = (bf16[2,96,768]{2,1,0:T(8,128)(2,1)}, bf16[2,96,768]{2,1,0:T(8,128)(2,1)S(1)}, u32[]{:S(2)}, u32[]{:S(2)}) collective-permute-start(bf16[2,96,768]{2,1,0:T(8,128)(2,1)} %copy-done.118), channel_id=1, source_target_pairs={{0,2},{2,0},{1,3},{3,1},{4,6},{6,4},{5,7},{7,5},{8,10},{10,8},{9,1... | collective-permute-start | bytes 884744 | tf_op jit(solution)/shard_map/ppermute | solution.py:24
  821.9 13.3 %collective-permute-start.19 = (bf16[2,96,768]{2,1,0:T(8,128)(2,1)}, bf16[2,96,768]{2,1,0:T(8,128)(2,1)S(1)}, u32[]{:S(2)}, u32[]{:S(2)}) collective-permute-start(bf16[2,96,768]{2,1,0:T(8,128)(2,1)} %copy-done.117), channel_id=1, source_target_pairs={{0,2},{2,0},{1,3},{3,1},{4,6},{6,4},{5,7},{7,5},{8,10},{10,8},{9,1... | collective-permute-start | bytes 884744 | tf_op jit(solution)/shard_map/ppermute | solution.py:24
  839.7 75.4 %collective-permute-start.25 = (bf16[576,1536]{1,0:T(8,128)(2,1)}, bf16[576,1536]{1,0:T(8,128)(2,1)}, u32[]{:S(2)}, u32[]{:S(2)}) collective-permute-start(bf16[576,1536]{1,0:T(8,128)(2,1)} %fusion.43), channel_id=1, source_target_pairs={{0,1},{1,0},{2,3},{3,2},{4,5},{5,4},{6,7},{7,6},{8,9},{9,8},{10,11... | collective-permute-start | bytes 5308424 | tf_op jit(solution)/shard_map/ppermute | solution.py:24
  842.8 93.8 %collective-permute-start.27 = (bf16[576,1536]{1,0:T(8,128)(2,1)}, bf16[576,1536]{1,0:T(8,128)(2,1)}, u32[]{:S(2)}, u32[]{:S(2)}) collective-permute-start(bf16[576,1536]{1,0:T(8,128)(2,1)} %fusion.46), channel_id=1, source_target_pairs={{0,1},{1,0},{2,3},{3,2},{4,5},{5,4},{6,7},{7,6},{8,9},{9,8},{10,11... | collective-permute-start | bytes 5308424 | tf_op jit(solution)/shard_map/ppermute | solution.py:24
  847.9 16.6 %collective-permute-start.37 = (bf16[96,3072]{1,0:T(8,128)(2,1)}, bf16[96,3072]{1,0:T(8,128)(2,1)}, u32[]{:S(2)}, u32[]{:S(2)}) collective-permute-start(bf16[96,3072]{1,0:T(8,128)(2,1)} %reduce-scatter.13.cloned.1.call-done), channel_id=1, source_target_pairs={{0,2},{2,0},{1,3},{3,1},{4,6},{6,4},{5,7},{7,5},{8,10},{10,8},{9,1... | collective-permute-start | bytes 1769480 | tf_op jit(solution)/shard_map/ppermute | solution.py:24
  854.5 38.3 %collective-permute-start.23 = (bf16[192,3072]{1,0:T(8,128)(2,1)}, bf16[192,3072]{1,0:T(8,128)(2,1)}, u32[]{:S(2)}, u32[]{:S(2)}) collective-permute-start(bf16[192,3072]{1,0:T(8,128)(2,1)} %reduce-scatter.11.cloned.1.call-done), channel_id=1, source_target_pairs={{0,2},{2,0},{1,3},{3,1},{4,6},{6,4},{5,7},{7,5},{8,10},{10,8},{9,1... | collective-permute-start | bytes 3538952 | tf_op jit(solution)/shard_map/ppermute | solution.py:24
  855.4 59.7 %collective-permute-start.24 = (bf16[192,3072]{1,0:T(8,128)(2,1)}, bf16[192,3072]{1,0:T(8,128)(2,1)}, u32[]{:S(2)}, u32[]{:S(2)}) collective-permute-start(bf16[192,3072]{1,0:T(8,128)(2,1)} %reduce-scatter.7.cloned.1.call-done), channel_id=1, source_target_pairs={{0,2},{2,0},{1,3},{3,1},{4,6},{6,4},{5,7},{7,5},{8,10},{10,8},{9,1... | collective-permute-start | bytes 3538952 | tf_op jit(solution)/shard_map/ppermute | solution.py:24
  864.5 72.1 %collective-permute-start.26 = (bf16[192,3072]{1,0:T(8,128)(2,1)}, bf16[192,3072]{1,0:T(8,128)(2,1)}, u32[]{:S(2)}, u32[]{:S(2)}) collective-permute-start(bf16[192,3072]{1,0:T(8,128)(2,1)} %reduce-scatter.9.cloned.1.call-done), channel_id=1, source_target_pairs={{0,2},{2,0},{1,3},{3,1},{4,6},{6,4},{5,7},{7,5},{8,10},{10,8},{9,1... | collective-permute-start | bytes 3538952 | tf_op jit(solution)/shard_map/ppermute | solution.py:24
  892.8 49.9 %collective-permute-start.28 = (bf16[192,1536]{1,0:T(8,128)(2,1)}, bf16[192,1536]{1,0:T(8,128)(2,1)S(1)}, u32[]{:S(2)}, u32[]{:S(2)}) collective-permute-start(bf16[192,1536]{1,0:T(8,128)(2,1)} %fusion.59), channel_id=1, source_target_pairs={{0,1},{1,0},{2,3},{3,2},{4,5},{5,4},{6,7},{7,6},{8,9},{9,8},{10,11... | collective-permute-start | bytes 1769480 | tf_op jit(solution)/shard_map/ppermute | solution.py:24
  950.3 11.0 %collective-permute-start.29 = (bf16[33792]{0:T(1024)(128)(2,1)S(1)}, bf16[33792]{0:T(1024)(128)(2,1)S(1)}, u32[]{:S(2)}, u32[]{:S(2)}) collective-permute-start(bf16[33792]{0:T(1024)(128)(2,1)S(1)} %constant_dynamic-update-slice_fusion.9), channel_id=1, source_target_pairs={{0,2},{2,0},{1,3},{3,1},{4,6},{6,4},{5,7},{7,5},{8,10},{10,8},{9,1... | collective-permute-start | bytes 202760 | tf_op jit(solution)/shard_map/ppermute | solution.py:24
  961.9 5.3 collective-permute-start.30
  967.8 15.5 %collective-permute-start.31 = (bf16[2,33792]{1,0:T(2,128)(2,1)S(1)}, bf16[2,33792]{1,0:T(2,128)(2,1)S(1)}, u32[]{:S(2)}, u32[]{:S(2)}) collective-permute-start(bf16[2,33792]{1,0:T(2,128)(2,1)S(1)} %get-tuple-element.205), channel_id=1, source_target_pairs={{0,24},{8,0},{16,8},{24,16},{1,25},{9,1},{17,9},{25,17},{2,26},{10... | collective-permute-start | bytes 405512 | tf_op jit(solution)/shard_map/ppermute | solution.py:78
  970.8 52.5 %collective-permute-start.35 = (bf16[192,3072]{1,0:T(8,128)(2,1)}, bf16[192,3072]{1,0:T(8,128)(2,1)}, u32[]{:S(2)}, u32[]{:S(2)}) collective-permute-start(bf16[192,3072]{1,0:T(8,128)(2,1)} %reduce-scatter.15.cloned.1.call-done), channel_id=1, source_target_pairs={{0,2},{2,0},{1,3},{3,1},{4,6},{6,4},{5,7},{7,5},{8,10},{10,8},{9,1... | collective-permute-start | bytes 3538952 | tf_op jit(solution)/shard_map/ppermute | solution.py:24
  971.4 20.1 %collective-permute-start.33 = (bf16[2,33792]{1,0:T(2,128)(2,1)S(1)}, bf16[2,33792]{1,0:T(2,128)(2,1)S(1)}, u32[]{:S(2)}, u32[]{:S(2)}) collective-permute-start(bf16[2,33792]{1,0:T(2,128)(2,1)S(1)} %get-tuple-element.205), channel_id=1, source_target_pairs={{0,8},{8,16},{16,24},{24,0},{1,9},{9,17},{17,25},{25,1},{2,10},{10... | collective-permute-start | bytes 405512 | tf_op jit(solution)/shard_map/ppermute | solution.py:78
  973.6 17.8 %collective-permute-start.32 = (bf16[2,33792]{1,0:T(2,128)(2,1)S(1)}, bf16[2,33792]{1,0:T(2,128)(2,1)S(1)}, u32[]{:S(2)}, u32[]{:S(2)}) collective-permute-start(bf16[2,33792]{1,0:T(2,128)(2,1)S(1)} %get-tuple-element.205), channel_id=1, source_target_pairs={{0,16},{8,24},{16,0},{24,8},{1,17},{9,25},{17,1},{25,9},{2,18},{10... | collective-permute-start | bytes 405512 | tf_op jit(solution)/shard_map/ppermute | solution.py:78
  1003.8 18.2 %collective-permute-start.34 = (bf16[16,192]{1,0:T(8,128)(2,1)S(1)}, bf16[16,192]{1,0:T(8,128)(2,1)}, u32[]{:S(2)}, u32[]{:S(2)}) collective-permute-start(bf16[16,192]{1,0:T(8,128)(2,1)S(1)} %fusion.94), channel_id=1, source_target_pairs={{0,1},{1,0},{2,3},{3,2},{4,5},{5,4},{6,7},{7,6},{8,9},{9,8},{10,11... | collective-permute-start | bytes 18440 | tf_op jit(solution)/shard_map/ppermute | solution.py:24
  1020.5 26.0 %collective-permute-start.36 = (bf16[192,3072]{1,0:T(8,128)(2,1)}, bf16[192,3072]{1,0:T(8,128)(2,1)S(1)}, u32[]{:S(2)}, u32[]{:S(2)}) collective-permute-start(bf16[192,3072]{1,0:T(8,128)(2,1)} %reduce-scatter.17.cloned.1.call-done), channel_id=1, source_target_pairs={{0,2},{2,0},{1,3},{3,1},{4,6},{6,4},{5,7},{7,5},{8,10},{10,8},{9,1... | collective-permute-start | bytes 3538952 | tf_op jit(solution)/shard_map/ppermute | solution.py:24
  (212 other events, 1990.3 us)
Sparse Core Ops, SparseCore 0:
  10.9 115.8 all-gather.6
  129.0 49.8 all-gather.8
  181.1 143.1 all-gather.10
  325.8 97.2 all-gather.12
  425.2 99.4 reduce-scatter.6
  526.9 97.8 reduce-scatter.8
  627.1 97.8 reduce-scatter.10
  730.2 45.2 reduce-scatter.12
  810.2 96.2 reduce-scatter.14
  908.6 106.5 reduce-scatter.16
